TPU v7x, 32 devices: a whole 2x2x4 slice. The times are simulated.
32 devices in a mesh: dp: 8 (over z, y), tensor: 4 (over x, core).
Axes of the slice: x: 2, y: 2, z: 4, core: 2. Of those that a mesh axis runs over, the one named last changes fastest.
Arguments:
- tokens: bfloat16 [2048, 2, 2048], P(('dp', 'tensor')), may hold values from -6 to 6
- cotangent: bfloat16 [2048, 2, 2048], P(('dp', 'tensor')), may hold values from -6 to 6
- segments: int32 [2048, 2], P('dp'), may hold values from 0 to 3, as said below
- expert_ids: int32 [2048, 2, 8], P('dp'), may hold values from 0 to 31, all different within a row; in each aligned block of 512 rows (0 to 511, 512 to 1023, ..., all dimensions but the last counted through in order) at most 176 rows name the same one
- attn_gain: bfloat16 [2048], P('dp'), may hold values from 0.5 to 1.5
- w_qkv: bfloat16 [2048, 3, 2048], P('dp', None, 'tensor'), may hold values from -0.125 to 0.125
- qk_gain: bfloat16 [128, 2, 16], P('dp', None, 'tensor'), may hold values from 0.5 to 1.5
- w_out: bfloat16 [2048, 2048], P('dp', 'tensor'), may hold values from -1 to 1
- mlp_gain: bfloat16 [2048], P('dp'), may hold values from 0.5 to 1.5
- router: bfloat16 [2048, 32], P('dp'), may hold values from -0.0625 to 0.0625
- expert_in: bfloat16 [32, 2048, 2, 1024], P(None, 'dp', None, 'tensor'), may hold values from -0.125 to 0.125
- expert_out: bfloat16 [32, 2048, 1024], P(None, 'dp', 'tensor'), may hold values from -3 to 3
Outputs:
- layer_out: bfloat16 [2048, 2, 2048], P(('dp', 'tensor'))
- grad_tokens: bfloat16 [2048, 2, 2048], P(('dp', 'tensor'))
- grad_attn_gain: float32 [2048], P('dp')
- grad_w_qkv: float32 [2048, 3, 2048], P('dp', None, 'tensor')
- grad_qk_gain: float32 [128, 2, 16], P('dp', None, 'tensor')
- grad_w_out: float32 [2048, 2048], P('dp', 'tensor')
- grad_mlp_gain: float32 [2048], P('dp')
- grad_router: float32 [2048, 32], P('dp')
- grad_expert_in: float32 [32, 2048, 2, 1024], P(None, 'dp', None, 'tensor')
- grad_expert_out: float32 [32, 2048, 1024], P(None, 'dp', 'tensor')
Inputs may be any that keep to these rules, and one draw needn't show every extreme that they name: `segments`: document numbers start at 0 and never fall along a sequence; a sequence holds one document or 4; in each group one micro-batch, drawn from the seed, holds a single document. `expert_ids`: A token's 8 experts differ; within the 512 rows of one group no expert is named more than 176 times, and in some group an expert is named exactly 176 times.
All inputs are finite; a program needn't handle non-finite values.
Results may differ from a plain program's by a relative error of at most 0.024.
Values may be sent and summed in bfloat16 or wider, within the bound.
A program may use at most 384 MiB of HBM per device.

v0:
```python
import jax
import jax.numpy as jnp
from jax import lax
from jax.sharding import PartitionSpec as P

EG = 8
WINDOW = 128
CAP = 176


EPSILON = 1e-05
MASKED = -1e30


def norm_factor(values):
    return lax.rsqrt(jnp.mean(values * values, axis=-1, keepdims=True) + EPSILON)


def norm_back(values, factor, gain_row, upstream):
    features = values.shape[-1]
    inner = jnp.sum(values * gain_row * upstream, axis=-1, keepdims=True)
    return factor * gain_row * upstream - values * factor**3 * inner / features


def softmax_rows(logits):
    highest = jnp.max(logits, axis=-1, keepdims=True)
    raised = jnp.exp(logits - highest)
    return raised / jnp.sum(raised, axis=-1, keepdims=True)


def rounded(values):
    return lax.optimization_barrier(values.astype(jnp.bfloat16)).astype(jnp.float32)


def expert_math(chosen, pushed, whole_in, whole_out):
    gate_up = jnp.einsum("ecd,edjf->ecjf", chosen, whole_in, preferred_element_type=jnp.float32)
    gate_part = gate_up[:, :, 0]
    up_part = gate_up[:, :, 1]
    sigmoid_gate = jax.nn.sigmoid(gate_part)
    activated = gate_part * sigmoid_gate
    hidden = (activated * up_part).astype(jnp.bfloat16)
    expert_rows = jnp.einsum("ecf,edf->ecd", hidden, whole_out, preferred_element_type=jnp.float32)
    d_hidden = jnp.einsum("ecd,edf->ecf", pushed, whole_out, preferred_element_type=jnp.float32)
    d_gate_part = d_hidden * up_part * sigmoid_gate * (1.0 + gate_part * (1.0 - sigmoid_gate))
    d_gate_up = jnp.stack([d_gate_part, d_hidden * activated], axis=2).astype(jnp.bfloat16)
    d_chosen = jnp.einsum("ecjf,edjf->ecd", d_gate_up, whole_in, preferred_element_type=jnp.float32)
    grad_in_part = jnp.einsum(
        "ecd,ecjf->edjf", chosen, d_gate_up, preferred_element_type=jnp.float32
    )
    grad_out_part = jnp.einsum("ecd,ecf->edf", pushed, hidden, preferred_element_type=jnp.float32)
    return (expert_rows, d_chosen, grad_in_part, grad_out_part)


def body(
    tokens,
    cotangent,
    segments,
    expert_ids,
    attn_gain,
    w_qkv,
    qk_gain,
    w_out,
    mlp_gain,
    router,
    expert_in,
    expert_out,
):
    full_qkv, full_out, full_router, gain_one, gain_two, full_qk = (
        lax.all_gather(w_qkv, "dp", axis=0, tiled=True),
        lax.all_gather(w_out, "dp", axis=0, tiled=True),
        lax.all_gather(router, "dp", axis=0, tiled=True),
        lax.all_gather(attn_gain, "dp", axis=0, tiled=True),
        lax.all_gather(mlp_gain, "dp", axis=0, tiled=True),
        lax.all_gather(qk_gain, "dp", axis=0, tiled=True),
    )
    local_rows = tokens.shape[0]
    micro_count = tokens.shape[1]
    features = tokens.shape[2]
    head_dim = full_qk.shape[0]
    local_heads = full_qk.shape[2]
    local_width = local_heads * head_dim
    experts = full_router.shape[1]
    top_count = expert_ids.shape[2]
    factor_scale = head_dim ** (-0.5)
    inputs = tokens.astype(jnp.float32)
    gain_one_f = gain_one.astype(jnp.float32)
    factor_one = norm_factor(inputs)
    normed_one = (inputs * factor_one * gain_one_f).astype(jnp.bfloat16)
    rows_one = lax.all_gather(normed_one, "tensor", axis=0, tiled=True)
    seq_len = rows_one.shape[0]
    projected = jnp.einsum("smd,djf->jmsf", rows_one, full_qkv, preferred_element_type=jnp.float32)
    query_raw = projected[0]
    key_raw = projected[1]
    value_rows = projected[2].astype(jnp.bfloat16)
    square_q, square_k = lax.psum(
        (jnp.sum(query_raw * query_raw, axis=-1), jnp.sum(key_raw * key_raw, axis=-1)), "tensor"
    )
    factor_q = lax.rsqrt(square_q[..., None] / features + EPSILON)
    factor_k = lax.rsqrt(square_k[..., None] / features + EPSILON)
    qk_rows = jnp.transpose(full_qk.astype(jnp.float32), (1, 2, 0)).reshape(2, local_width)
    queries = (query_raw * factor_q * qk_rows[0]).astype(jnp.bfloat16)
    keys_low = (key_raw * factor_k * qk_rows[1]).astype(jnp.bfloat16)
    query_heads = queries.reshape(micro_count, seq_len, local_heads, head_dim)
    key_heads = keys_low.reshape(micro_count, seq_len, local_heads, head_dim)
    value_heads = value_rows.reshape(micro_count, seq_len, local_heads, head_dim)
    query_span = min(seq_len, 512)
    block_count = seq_len // query_span
    seq_major = segments.T
    key_positions = jnp.arange(seq_len)

    def allowed_at(first_row):
        query_positions = first_row + jnp.arange(query_span)
        same_doc = seq_major[:, :, None] == seq_major[:, None, :]
        distance = query_positions[:, None] - key_positions[None, :]
        return (same_doc & (distance >= 0) & (distance < WINDOW))[:, None]

    def score_block(first_row):
        scores = (
            jnp.einsum(
                "mqhc,mkhc->mhqk", query_heads, key_heads, preferred_element_type=jnp.float32
            )
            * factor_scale
        )
        return jnp.where(allowed_at(first_row), scores, MASKED)

    def forward_block(first_row):
        scores = score_block(first_row)
        highest = jnp.max(scores, axis=-1, keepdims=True)
        raised = jnp.exp(scores - highest)
        totals = jnp.sum(raised, axis=-1, keepdims=True)
        weights_low = (raised / totals).astype(jnp.bfloat16)
        head_mix = jnp.einsum(
            "mhqk,mkhc->mqhc", weights_low, value_heads, preferred_element_type=jnp.float32
        )
        return (head_mix.astype(jnp.bfloat16), highest + jnp.log(totals))

    starts = jnp.arange(block_count, dtype=jnp.int32) * query_span
    mixed_blocks, log_totals = lax.map(forward_block, starts)
    head_out = jnp.moveaxis(mixed_blocks, 0, 1).reshape(micro_count, seq_len, local_width)
    piece = head_out
    attended = lax.psum_scatter(
        jnp.einsum("msf,df->smd", piece, full_out, preferred_element_type=jnp.float32),
        "tensor",
        scatter_dimension=0,
        tiled=True,
    )
    residual = inputs + attended
    gain_two_f = gain_two.astype(jnp.float32)
    factor_two = norm_factor(residual)
    normed_two = (residual * factor_two * gain_two_f).astype(jnp.bfloat16)
    rows_two, pulled = (
        lax.all_gather(normed_two, "tensor", axis=0, tiled=True),
        lax.all_gather(cotangent, "tensor", axis=0, tiled=True),
    )
    token_count = seq_len * micro_count
    flat_rows = rows_two.reshape(token_count, features)
    flat_pull = pulled.reshape(token_count, features)
    logits = jnp.dot(flat_rows, full_router, preferred_element_type=jnp.float32)
    router_probs = softmax_rows(logits)
    routes = expert_ids.reshape(token_count, top_count)
    choose = (routes[:, :, None] == jnp.arange(experts, dtype=jnp.int32)).astype(jnp.float32)
    gate_values = jnp.sum(choose * router_probs[:, None, :], axis=-1).reshape(-1)
    flat_routes = routes.reshape(-1)
    member = (flat_routes[:, None] == jnp.arange(experts, dtype=jnp.int32)).astype(jnp.int32)
    position = jnp.sum(jnp.cumsum(member, axis=0) * member, axis=1) - 1
    slot_index = flat_routes * CAP + position
    row_tokens = jnp.arange(flat_routes.shape[0], dtype=jnp.int32) // top_count
    source = jnp.full((experts * CAP,), token_count, jnp.int32).at[slot_index].set(row_tokens)
    slot_gate = jnp.zeros((experts * CAP,), jnp.float32).at[slot_index].set(gate_values)
    zero_row = jnp.zeros((1, features), jnp.bfloat16)
    padded_rows = jnp.concatenate([flat_rows, zero_row], axis=0)
    padded_pull = jnp.concatenate([flat_pull, zero_row], axis=0)
    group_count = experts // EG
    group_slots = EG * CAP
    stacked_in = expert_in.reshape((group_count, EG) + expert_in.shape[1:])
    stacked_out = expert_out.reshape((group_count, EG) + expert_out.shape[1:])

    def expert_step(carry, item):
        mixture_acc, return_acc, slot_dots = carry
        group_index, part_in, part_out = item
        whole_in, whole_out = (
            lax.all_gather(part_in, "dp", axis=1, tiled=True),
            lax.all_gather(part_out, "dp", axis=1, tiled=True),
        )
        where_from = lax.dynamic_slice_in_dim(source, group_index * group_slots, group_slots)
        gate_slice = lax.dynamic_slice_in_dim(slot_gate, group_index * group_slots, group_slots)
        chosen = padded_rows[where_from].reshape(EG, CAP, features)
        pull_rows = padded_pull[where_from].astype(jnp.float32)
        pushed = (pull_rows * gate_slice[:, None]).astype(jnp.bfloat16).reshape(EG, CAP, features)
        expert_rows, d_chosen, grad_in_part, grad_out_part = expert_math(
            chosen, pushed, whole_in, whole_out
        )
        expert_rows = expert_rows.reshape(group_slots, features)
        mixture_acc = mixture_acc.at[where_from].add(expert_rows * gate_slice[:, None])
        return_acc = return_acc.at[where_from].add(d_chosen.reshape(group_slots, features))
        slot_dots = lax.dynamic_update_slice_in_dim(
            slot_dots, jnp.sum(expert_rows * pull_rows, axis=-1), group_index * group_slots, 0
        )
        shares = (
            lax.psum_scatter(
                grad_in_part.astype(jnp.bfloat16), "dp", scatter_dimension=1, tiled=True
            ).astype(jnp.float32),
            lax.psum_scatter(
                grad_out_part.astype(jnp.bfloat16), "dp", scatter_dimension=1, tiled=True
            ).astype(jnp.float32),
        )
        return ((mixture_acc, return_acc, slot_dots), shares)

    initial = (
        jnp.zeros((token_count + 1, features), jnp.float32),
        jnp.zeros((token_count + 1, features), jnp.float32),
        jnp.zeros((experts * CAP,), jnp.float32),
    )
    scanned, grad_groups = lax.scan(
        expert_step, initial, (jnp.arange(group_count, dtype=jnp.int32), stacked_in, stacked_out)
    )
    mixture_acc, return_acc, slot_dots = scanned
    grad_expert_in = grad_groups[0].reshape((experts,) + grad_groups[0].shape[2:])
    grad_expert_out = grad_groups[1].reshape((experts,) + grad_groups[1].shape[2:])
    d_gate_rows = slot_dots[slot_index].reshape(seq_len, micro_count, top_count)
    mixture, returned, d_gate_own = (
        lax.psum_scatter(
            mixture_acc[:token_count].reshape(seq_len, micro_count, features).astype(jnp.bfloat16),
            "tensor",
            scatter_dimension=0,
            tiled=True,
        ).astype(jnp.float32),
        lax.psum_scatter(
            return_acc[:token_count].reshape(seq_len, micro_count, features).astype(jnp.bfloat16),
            "tensor",
            scatter_dimension=0,
            tiled=True,
        ).astype(jnp.float32),
        lax.psum_scatter(
            d_gate_rows.astype(jnp.bfloat16), "tensor", scatter_dimension=0, tiled=True
        ).astype(jnp.float32),
    )
    layer_out = (residual + mixture).astype(jnp.bfloat16)
    pull_own = cotangent.astype(jnp.float32)
    logits_own = jnp.einsum(
        "smd,de->sme", normed_two, full_router, preferred_element_type=jnp.float32
    )
    probs_own = softmax_rows(logits_own)
    routes_own = lax.dynamic_slice_in_dim(
        expert_ids, lax.axis_index("tensor") * local_rows, local_rows, 0
    )
    choose_own = (routes_own[..., None] == jnp.arange(experts, dtype=jnp.int32)).astype(jnp.float32)
    d_probs_router = jnp.sum(d_gate_own[..., None] * choose_own, axis=2)
    d_logits = (
        probs_own * (d_probs_router - jnp.sum(d_probs_router * probs_own, axis=-1, keepdims=True))
    ).astype(jnp.bfloat16)
    d_normed_two = returned + jnp.einsum(
        "sme,de->smd", d_logits, full_router, preferred_element_type=jnp.float32
    )
    grad_router = jnp.einsum(
        "smd,sme->de", normed_two, d_logits, preferred_element_type=jnp.float32
    )
    d_residual = pull_own + norm_back(residual, factor_two, gain_two_f, d_normed_two)
    grad_gain_two = jnp.sum(residual * factor_two * d_normed_two, axis=(0, 1))
    d_attended = d_residual.astype(jnp.bfloat16)
    rows_back = lax.all_gather(d_attended, "tensor", axis=0, tiled=True)
    d_head_out = jnp.einsum(
        "smd,df->msf", rows_back, full_out, preferred_element_type=jnp.float32
    ).astype(jnp.bfloat16)
    grad_w_out = jnp.einsum("smd,msf->df", rows_back, head_out, preferred_element_type=jnp.float32)
    d_head_parts = d_head_out.reshape(micro_count, seq_len, local_heads, head_dim)

    def backward_block(carry, item):
        d_keys_acc, d_values_acc = carry
        first_row, log_total = item
        scores = score_block(first_row)
        weights_full = jnp.exp(scores - log_total)
        weights_low = weights_full.astype(jnp.bfloat16)
        d_weights = jnp.einsum(
            "mqhc,mkhc->mhqk", d_head_parts, value_heads, preferred_element_type=jnp.float32
        )
        d_scores = (
            weights_full * (d_weights - jnp.sum(d_weights * weights_full, axis=-1, keepdims=True))
        ).astype(jnp.bfloat16)
        d_query_part = (
            jnp.einsum("mhqk,mkhc->mqhc", d_scores, key_heads, preferred_element_type=jnp.float32)
            * factor_scale
        )
        d_keys_acc = (
            d_keys_acc
            + jnp.einsum(
                "mhqk,mqhc->mkhc", d_scores, query_heads, preferred_element_type=jnp.float32
            )
            * factor_scale
        )
        d_values_acc = d_values_acc + jnp.einsum(
            "mhqk,mqhc->mkhc", weights_low, d_head_parts, preferred_element_type=jnp.float32
        )
        return ((d_keys_acc, d_values_acc), d_query_part)

    zero_heads = jnp.zeros((micro_count, seq_len, local_heads, head_dim), jnp.float32)
    key_value_grads, d_query_blocks = lax.scan(
        backward_block, (zero_heads, zero_heads), (starts, log_totals)
    )
    d_queries = rounded(
        jnp.moveaxis(d_query_blocks, 0, 1).reshape(micro_count, seq_len, local_width)
    )
    d_keys = rounded(key_value_grads[0].reshape(micro_count, seq_len, local_width))
    d_values = key_value_grads[1].reshape(micro_count, seq_len, local_width).astype(jnp.bfloat16)
    inner_q, inner_k = lax.psum(
        (
            jnp.sum(query_raw * qk_rows[0] * d_queries, axis=-1),
            jnp.sum(key_raw * qk_rows[1] * d_keys, axis=-1),
        ),
        "tensor",
    )
    d_query_raw = (
        factor_q * qk_rows[0] * d_queries - query_raw * factor_q**3 * inner_q[..., None] / features
    )
    d_key_raw = (
        factor_k * qk_rows[1] * d_keys - key_raw * factor_k**3 * inner_k[..., None] / features
    )
    grad_qk_rows = jnp.stack(
        [
            jnp.sum(query_raw * factor_q * d_queries, axis=(0, 1)),
            jnp.sum(key_raw * factor_k * d_keys, axis=(0, 1)),
        ]
    )
    grad_qk = jnp.transpose(grad_qk_rows.reshape(2, local_heads, head_dim), (2, 0, 1))
    d_projected = jnp.stack(
        [d_query_raw.astype(jnp.bfloat16), d_key_raw.astype(jnp.bfloat16), d_values]
    )
    grad_qkv = jnp.einsum(
        "smd,jmsf->djf", rows_one, d_projected, preferred_element_type=jnp.float32
    )
    piece = d_projected
    d_normed_one = lax.psum_scatter(
        jnp.einsum("jmsf,djf->smd", piece, full_qkv, preferred_element_type=jnp.float32).astype(
            jnp.bfloat16
        ),
        "tensor",
        scatter_dimension=0,
        tiled=True,
    ).astype(jnp.float32)
    grad_tokens = (d_residual + norm_back(inputs, factor_one, gain_one_f, d_normed_one)).astype(
        jnp.bfloat16
    )
    grad_gain_one = jnp.sum(inputs * factor_one * d_normed_one, axis=(0, 1))
    gain_one_sum, gain_two_sum, router_sum = (
        lax.psum(grad_gain_one.astype(jnp.bfloat16), "tensor").astype(jnp.float32),
        lax.psum(grad_gain_two.astype(jnp.bfloat16), "tensor").astype(jnp.float32),
        lax.psum(grad_router.astype(jnp.bfloat16), "tensor").astype(jnp.float32),
    )
    grads = (
        lax.psum_scatter(
            grad_qkv.astype(jnp.bfloat16), "dp", scatter_dimension=0, tiled=True
        ).astype(jnp.float32),
        lax.psum_scatter(
            grad_w_out.astype(jnp.bfloat16), "dp", scatter_dimension=0, tiled=True
        ).astype(jnp.float32),
        lax.psum_scatter(
            router_sum.astype(jnp.bfloat16), "dp", scatter_dimension=0, tiled=True
        ).astype(jnp.float32),
        lax.psum_scatter(
            gain_one_sum.astype(jnp.bfloat16), "dp", scatter_dimension=0, tiled=True
        ).astype(jnp.float32),
        lax.psum_scatter(
            gain_two_sum.astype(jnp.bfloat16), "dp", scatter_dimension=0, tiled=True
        ).astype(jnp.float32),
        lax.psum_scatter(
            grad_qk.astype(jnp.bfloat16), "dp", scatter_dimension=0, tiled=True
        ).astype(jnp.float32),
    )
    return (
        layer_out,
        grad_tokens,
        grads[3],
        grads[0],
        grads[5],
        grads[1],
        grads[4],
        grads[2],
        grad_expert_in,
        grad_expert_out,
    )


def solution(mesh):
    placed = (
        P(("dp", "tensor"), None, None),
        P(("dp", "tensor"), None, None),
        P("dp", None),
        P("dp", None, None),
        P("dp"),
        P("dp", None, "tensor"),
        P("dp", None, "tensor"),
        P("dp", "tensor"),
        P("dp"),
        P("dp", None),
        P(None, "dp", None, "tensor"),
        P(None, "dp", "tensor"),
    )
    return jax.shard_map(
        body,
        mesh=mesh,
        in_specs=placed,
        out_specs=(
            P(("dp", "tensor"), None, None),
            P(("dp", "tensor"), None, None),
            P("dp"),
            P("dp", None, "tensor"),
            P("dp", None, "tensor"),
            P("dp", "tensor"),
            P("dp"),
            P("dp", None),
            P(None, "dp", None, "tensor"),
            P(None, "dp", "tensor"),
        ),
        check_vma=False,
    )
```

profile of v0, /device:TPU:0, one launch (start us, length us, event | category | flops | bytes accessed | tf_op | source)
XLA Modules:
  0.0 4096.0 jit_solution(964198343564231878)
XLA Ops:
  9.8 22.3 all-gather.2
  36.4 30.5 all_gather.39
  67.7 88.3 %all-gather.19.cloned.1.call-done = bf16[2048,3,512]{2,0,1:T(8,128)(2,1)} async-done(((bf16[256,3,512]{2,0,1:T(8,128)(2,1)}), bf16[2048,3,512]{2,0,1:T(8,128)(2,1)}) %all-gather.19.cloned.1.call-update) | async-done | bytes 6291472 | tf_op jit(solution)/shard_map/all_gather | solution.py:69
  184.0 21.8 all-gather.21.cloned.1.call-done
  211.4 18.2 all-gather.3
  229.6 24.2 reduce-scatter.13.cloned.1.call-done
  278.5 15.5 scatter_custom_fusion.2
  294.1 30.6 all_gather.43
  344.3 15.5 scatter_custom_fusion.3
  365.6 3256.8 %while.2 = (s32[]{:T(128)}, f32[513,2048]{1,0:T(8,128)}, f32[513,2048]{1,0:T(8,128)}, bf16[5632]{0:T(1024)(128)(2,1)}, f32[4,8,256,2,256]{4,3,2,1,0:T(2,128)}, /...) while((s32[]{:T(128)}, f32[513,2048]{1,0:T(8,128)}, ...), condition=%wide.region_23.24_spmd, body=%wide.region_17.23_spmd.sunk | while | flops 13343166464 | bytes 489328256 | solution.py:214
  373.9 14.4 gather_fusion.1
  395.2 202.4 %all-gather.29.cloned.1.call-done = bf16[1,8,2048,2,256]{4,2,3,1,0:T(8,128)(2,1)} async-done(((bf16[1,8,256,2,256]{4,2,3,1,0:T(8,128)(2,1)}), bf16[1,8,2048,2,256]{4,2,3,1,0:T(8,128)(2,1)}) %all-gather.29.cloned.1.call-update) | async-done | bytes 16777232 | tf_op jit(solution)/shard_map/while/body/eval_jaxpr/all_gather | solution.py:182
  597.6 12.3 fusion.165
  610.0 113.0 %all-gather.31.cloned.1.call-done = bf16[1,8,2048,256]{3,2,1,0:T(8,128)(2,1)} async-done(((bf16[1,8,256,256]{3,2,1,0:T(8,128)(2,1)}), bf16[1,8,2048,256]{3,2,1,0:T(8,128)(2,1)}) %all-gather.31.cloned.1.call-update) | async-done | bytes 8388624 | tf_op jit(solution)/shard_map/while/body/eval_jaxpr/all_gather | solution.py:183
  740.2 11.6 convolution_convert_fusion.6
  751.9 12.3 fusion.167
  764.3 11.7 fusion.168
  776.0 25.4 scatter_fusion.1
  810.9 25.7 scatter_fusion
  838.0 48.2 %reduce-scatter.31.cloned.1.call-done = bf16[8,256,256]{2,1,0:T(8,128)(2,1)} async-done(((bf16[8,2048,256]{2,1,0:T(8,128)(2,1)}), bf16[8,256,256]{2,1,0:T(8,128)(2,1)}) %reduce-scatter.31.cloned.1.call-update) | async-done | bytes 1048592 | tf_op jit(solution)/shard_map/while/body/eval_jaxpr/reduce_scatter | solution.py:203
  889.0 282.4 %reduce-scatter.29.cloned.1.call-done = bf16[8,256,2,256]{3,1,2,0:T(8,128)(2,1)} async-done(((bf16[8,2048,2,256]{3,1,2,0:T(8,128)(2,1)}), bf16[8,256,2,256]{3,1,2,0:T(8,128)(2,1)}) %reduce-scatter.29.cloned.1.call-update) | async-done | bytes 2097168 | tf_op jit(solution)/shard_map/while/body/eval_jaxpr/reduce_scatter | solution.py:200
  1186.8 14.4 gather_fusion.1
  1208.1 201.5 %all-gather.29.cloned.1.call-done = bf16[1,8,2048,2,256]{4,2,3,1,0:T(8,128)(2,1)} async-done(((bf16[1,8,256,2,256]{4,2,3,1,0:T(8,128)(2,1)}), bf16[1,8,2048,2,256]{4,2,3,1,0:T(8,128)(2,1)}) %all-gather.29.cloned.1.call-update) | async-done | bytes 16777232 | tf_op jit(solution)/shard_map/while/body/eval_jaxpr/all_gather | solution.py:182
  1409.7 12.4 fusion.165
  1422.1 112.8 %all-gather.31.cloned.1.call-done = bf16[1,8,2048,256]{3,2,1,0:T(8,128)(2,1)} async-done(((bf16[1,8,256,256]{3,2,1,0:T(8,128)(2,1)}), bf16[1,8,2048,256]{3,2,1,0:T(8,128)(2,1)}) %all-gather.31.cloned.1.call-update) | async-done | bytes 8388624 | tf_op jit(solution)/shard_map/while/body/eval_jaxpr/all_gather | solution.py:183
  1552.1 11.6 convolution_convert_fusion.6
  1563.8 12.3 fusion.167
  1576.2 11.7 fusion.168
  1587.9 25.4 scatter_fusion.1
  1622.8 25.5 scatter_fusion
  1649.8 48.4 %reduce-scatter.31.cloned.1.call-done = bf16[8,256,256]{2,1,0:T(8,128)(2,1)} async-done(((bf16[8,2048,256]{2,1,0:T(8,128)(2,1)}), bf16[8,256,256]{2,1,0:T(8,128)(2,1)}) %reduce-scatter.31.cloned.1.call-update) | async-done | bytes 1048592 | tf_op jit(solution)/shard_map/while/body/eval_jaxpr/reduce_scatter | solution.py:203
  1700.9 282.2 %reduce-scatter.29.cloned.1.call-done = bf16[8,256,2,256]{3,1,2,0:T(8,128)(2,1)} async-done(((bf16[8,2048,2,256]{3,1,2,0:T(8,128)(2,1)}), bf16[8,256,2,256]{3,1,2,0:T(8,128)(2,1)}) %reduce-scatter.29.cloned.1.call-update) | async-done | bytes 2097168 | tf_op jit(solution)/shard_map/while/body/eval_jaxpr/reduce_scatter | solution.py:200
  1998.8 14.4 gather_fusion.1
  2020.1 201.6 %all-gather.29.cloned.1.call-done = bf16[1,8,2048,2,256]{4,2,3,1,0:T(8,128)(2,1)} async-done(((bf16[1,8,256,2,256]{4,2,3,1,0:T(8,128)(2,1)}), bf16[1,8,2048,2,256]{4,2,3,1,0:T(8,128)(2,1)}) %all-gather.29.cloned.1.call-update) | async-done | bytes 16777232 | tf_op jit(solution)/shard_map/while/body/eval_jaxpr/all_gather | solution.py:182
  2221.7 12.4 fusion.165
  2234.1 112.8 %all-gather.31.cloned.1.call-done = bf16[1,8,2048,256]{3,2,1,0:T(8,128)(2,1)} async-done(((bf16[1,8,256,256]{3,2,1,0:T(8,128)(2,1)}), bf16[1,8,2048,256]{3,2,1,0:T(8,128)(2,1)}) %all-gather.31.cloned.1.call-update) | async-done | bytes 8388624 | tf_op jit(solution)/shard_map/while/body/eval_jaxpr/all_gather | solution.py:183
  2364.1 11.6 convolution_convert_fusion.6
  2375.7 12.3 fusion.167
  2388.1 11.7 fusion.168
  2399.9 25.4 scatter_fusion.1
  2434.8 25.7 scatter_fusion
  2461.9 48.3 %reduce-scatter.31.cloned.1.call-done = bf16[8,256,256]{2,1,0:T(8,128)(2,1)} async-done(((bf16[8,2048,256]{2,1,0:T(8,128)(2,1)}), bf16[8,256,256]{2,1,0:T(8,128)(2,1)}) %reduce-scatter.31.cloned.1.call-update) | async-done | bytes 1048592 | tf_op jit(solution)/shard_map/while/body/eval_jaxpr/reduce_scatter | solution.py:203
  2512.9 282.4 %reduce-scatter.29.cloned.1.call-done = bf16[8,256,2,256]{3,1,2,0:T(8,128)(2,1)} async-done(((bf16[8,2048,2,256]{3,1,2,0:T(8,128)(2,1)}), bf16[8,256,2,256]{3,1,2,0:T(8,128)(2,1)}) %reduce-scatter.29.cloned.1.call-update) | async-done | bytes 2097168 | tf_op jit(solution)/shard_map/while/body/eval_jaxpr/reduce_scatter | solution.py:200
  2810.8 14.4 gather_fusion.1
  2832.1 201.5 %all-gather.29.cloned.1.call-done = bf16[1,8,2048,2,256]{4,2,3,1,0:T(8,128)(2,1)} async-done(((bf16[1,8,256,2,256]{4,2,3,1,0:T(8,128)(2,1)}), bf16[1,8,2048,2,256]{4,2,3,1,0:T(8,128)(2,1)}) %all-gather.29.cloned.1.call-update) | async-done | bytes 16777232 | tf_op jit(solution)/shard_map/while/body/eval_jaxpr/all_gather | solution.py:182
  3033.6 12.4 fusion.165
  3046.0 112.8 %all-gather.31.cloned.1.call-done = bf16[1,8,2048,256]{3,2,1,0:T(8,128)(2,1)} async-done(((bf16[1,8,256,256]{3,2,1,0:T(8,128)(2,1)}), bf16[1,8,2048,256]{3,2,1,0:T(8,128)(2,1)}) %all-gather.31.cloned.1.call-update) | async-done | bytes 8388624 | tf_op jit(solution)/shard_map/while/body/eval_jaxpr/all_gather | solution.py:183
  3176.0 11.6 convolution_convert_fusion.6
  3187.7 12.3 fusion.167
  3200.1 11.7 fusion.168
  3211.8 25.4 scatter_fusion.1
  3246.7 25.5 scatter_fusion
  3273.6 48.5 %reduce-scatter.31.cloned.1.call-done = bf16[8,256,256]{2,1,0:T(8,128)(2,1)} async-done(((bf16[8,2048,256]{2,1,0:T(8,128)(2,1)}), bf16[8,256,256]{2,1,0:T(8,128)(2,1)}) %reduce-scatter.31.cloned.1.call-update) | async-done | bytes 1048592 | tf_op jit(solution)/shard_map/while/body/eval_jaxpr/reduce_scatter | solution.py:203
  3324.8 282.4 %reduce-scatter.29.cloned.1.call-done = bf16[8,256,2,256]{3,1,2,0:T(8,128)(2,1)} async-done(((bf16[8,2048,2,256]{3,1,2,0:T(8,128)(2,1)}), bf16[8,256,2,256]{3,1,2,0:T(8,128)(2,1)}) %reduce-scatter.29.cloned.1.call-update) | async-done | bytes 2097168 | tf_op jit(solution)/shard_map/while/body/eval_jaxpr/reduce_scatter | solution.py:200
  3642.7 25.6 gather_fusion.2
  3668.5 12.8 all-reduce.2
  3681.6 14.4 reduce-scatter.17.cloned.1.call-done
  3700.6 22.5 all-gather.27.cloned.1.call-done
  3775.6 21.4 reduce-scatter.27.cloned.1.call-done
  3798.3 31.7 reduce-scatter.19.cloned.1.call-done
  3833.7 21.7 all-reduce.7
  3855.5 39.6 reduce-scatter.25.cloned.1.call-done
  3907.2 58.4 %reduce-scatter.23.cloned.1.call-done = bf16[256,512]{1,0:T(8,128)(2,1)} async-done(((bf16[2048,512]{1,0:T(8,128)(2,1)}), bf16[256,512]{1,0:T(8,128)(2,1)}) %reduce-scatter.23.cloned.1.call-update) | async-done | bytes 262160 | tf_op jit(solution)/shard_map/reduce_scatter | solution.py:353
  3967.4 119.0 %reduce-scatter.21.cloned.1.call-done = bf16[256,3,512]{2,0,1:T(8,128)(2,1)} async-done(((bf16[2048,3,512]{2,0,1:T(8,128)(2,1)}), bf16[256,3,512]{2,0,1:T(8,128)(2,1)}) %reduce-scatter.21.cloned.1.call-update) | async-done | bytes 786448 | tf_op jit(solution)/shard_map/reduce_scatter | solution.py:350
  (484 shorter events, 398.0 us)
Async XLA Ops:
  7.2 29.1 copy-start.71
  7.2 60.1 %copy-start.67 = (s32[256,2]{0,1:T(2,128)S(1)}, s32[256,2]{0,1:T(2,128)}, u32[]{:S(2)}) copy-start(s32[256,2]{0,1:T(2,128)} %param.16) | copy-start | bytes 6148
  7.2 60.3 %all-gather.17.cloned.1.call-start = ((), (), s32[]{:S(2)}) async-start(), calls=%async_computation.10 | async-start | bytes 2621440 | tf_op jit(solution)/shard_map/all_gather | solution.py:89
  9.8 22.3 copy-start.65
  34.7 121.3 %all-gather.19.cloned.1.call-start = ((), (), s32[]{:S(2)}) async-start(), calls=%async_computation.11 | async-start | bytes 7077888 | tf_op jit(solution)/shard_map/all_gather | solution.py:69
  35.5 170.3 %all-gather.21.cloned.1.call-start = ((), (), s32[]{:S(2)}) async-start(), calls=%async_computation.12 | async-start | bytes 2359296 | tf_op jit(solution)/shard_map/all_gather | solution.py:70
  36.2 217.7 %reduce-scatter.13.cloned.1.call-start = ((), (), s32[]{:S(2)}) async-start(), calls=%async_computation.13 | async-start | bytes 5242880 | tf_op jit(solution)/shard_map/reduce_scatter | solution.py:141
  67.1 112.0 %copy-start.60 = (f32[4,128]{1,0:T(4,128)}, f32[4,128]{1,0:T(4,128)S(1)}, u32[]{:S(2)}) copy-start(f32[4,128]{1,0:T(4,128)S(1)} %copy.218) | copy-start | bytes 6148
  67.2 111.9 %copy-start.58 = (f32[4,128]{1,0:T(4,128)}, f32[4,128]{1,0:T(4,128)S(1)}, u32[]{:S(2)}) copy-start(f32[4,128]{1,0:T(4,128)S(1)} %copy.220) | copy-start | bytes 6148
  162.2 9.9 copy-start.7
  184.0 21.8 copy-start.32
  210.7 43.2 %copy-start.14 = (bf16[64,2,2048]{2,1,0:T(2,128)(2,1)S(1)}, bf16[64,2,2048]{2,1,0:T(2,128)(2,1)}, u32[]{:S(2)}) copy-start(bf16[64,2,2048]{2,1,0:T(2,128)(2,1)} %param.14) | copy-start | bytes 1572868
  210.7 46.9 %copy-start.42 = (s32[256,2,8]{0,2,1:T(8,128)S(1)}, s32[256,2,8]{0,2,1:T(8,128)}, u32[]{:S(2)}) copy-start(s32[256,2,8]{0,2,1:T(8,128)} %param.17) | copy-start | bytes 49156
  210.7 114.0 %all-gather.25.cloned.1.call-start = ((), (), s32[]{:S(2)}) async-start(), calls=%async_computation.15 | async-start | bytes 2621440 | tf_op jit(solution)/shard_map/all_gather | solution.py:153
  211.3 119.3 %all-gather.23.cloned.1.call-start = ((), (), s32[]{:S(2)}) async-start(), calls=%async_computation.14 | async-start | bytes 2621440 | tf_op jit(solution)/shard_map/all_gather | solution.py:152
  229.6 29.4 copy-start.46
  269.4 24.7 copy-start.62
  278.5 65.8 %copy-start.48 = (s32[4096,1]{0,1:T(1,128)}, s32[4096,1]{0,1:T(1,128)S(1)}, u32[]{:S(2)}) copy-start(s32[4096,1]{0,1:T(1,128)S(1)} %compare_select_fusion.1) | copy-start | bytes 49156
  324.7 18.4 copy-start.22
  366.0 22.2 copy-start
  366.0 231.6 %all-gather.29.cloned.1.call-start = ((), (), s32[]{:S(2)}) async-start(), calls=%async_computation.24 | async-start | bytes 18874368 | tf_op jit(solution)/shard_map/while/body/eval_jaxpr/all_gather | solution.py:182
  369.9 353.0 %all-gather.31.cloned.1.call-start = ((), (), s32[]{:S(2)}) async-start(), calls=%async_computation.25 | async-start | bytes 9437184 | tf_op jit(solution)/shard_map/while/body/eval_jaxpr/all_gather | solution.py:183
  372.4 513.9 %reduce-scatter.31.cloned.1.call-start = ((), (), s32[]{:S(2)}) async-start(), calls=%async_computation.27 | async-start | bytes 9437184 | tf_op jit(solution)/shard_map/while/body/eval_jaxpr/reduce_scatter | solution.py:203
  597.6 134.7 %slice-start = ((s8[5767168]{0:T(1024)(128)(4,1)}), s8[1572864]{0:T(1024)(128)(4,1)S(1)}, s32[]{:S(2)}) async-start(s8[5767168]{0:T(1024)(128)(4,1)} %bitcast.290), calls=%async_computation.28 | async-start | bytes 3145728 | tf_op jit(solution)/shard_map/while
  738.9 432.5 %reduce-scatter.29.cloned.1.call-start = ((), (), s32[]{:S(2)}) async-start(), calls=%async_computation.26 | async-start | bytes 18874368 | tf_op jit(solution)/shard_map/while/body/eval_jaxpr/reduce_scatter | solution.py:200
  1179.0 22.2 copy-start
  1179.0 230.7 %all-gather.29.cloned.1.call-start = ((), (), s32[]{:S(2)}) async-start(), calls=%async_computation.24 | async-start | bytes 18874368 | tf_op jit(solution)/shard_map/while/body/eval_jaxpr/all_gather | solution.py:182
  1182.9 352.0 %all-gather.31.cloned.1.call-start = ((), (), s32[]{:S(2)}) async-start(), calls=%async_computation.25 | async-start | bytes 9437184 | tf_op jit(solution)/shard_map/while/body/eval_jaxpr/all_gather | solution.py:183
  1185.3 512.8 %reduce-scatter.31.cloned.1.call-start = ((), (), s32[]{:S(2)}) async-start(), calls=%async_computation.27 | async-start | bytes 9437184 | tf_op jit(solution)/shard_map/while/body/eval_jaxpr/reduce_scatter | solution.py:203
  1409.7 134.6 %slice-start = ((s8[5767168]{0:T(1024)(128)(4,1)}), s8[1572864]{0:T(1024)(128)(4,1)S(1)}, s32[]{:S(2)}) async-start(s8[5767168]{0:T(1024)(128)(4,1)} %bitcast.290), calls=%async_computation.28 | async-start | bytes 3145728 | tf_op jit(solution)/shard_map/while
  1550.8 432.3 %reduce-scatter.29.cloned.1.call-start = ((), (), s32[]{:S(2)}) async-start(), calls=%async_computation.26 | async-start | bytes 18874368 | tf_op jit(solution)/shard_map/while/body/eval_jaxpr/reduce_scatter | solution.py:200
  1990.9 22.2 copy-start
  1990.9 230.7 %all-gather.29.cloned.1.call-start = ((), (), s32[]{:S(2)}) async-start(), calls=%async_computation.24 | async-start | bytes 18874368 | tf_op jit(solution)/shard_map/while/body/eval_jaxpr/all_gather | solution.py:182
  1994.8 352.0 %all-gather.31.cloned.1.call-start = ((), (), s32[]{:S(2)}) async-start(), calls=%async_computation.25 | async-start | bytes 9437184 | tf_op jit(solution)/shard_map/while/body/eval_jaxpr/all_gather | solution.py:183
  1997.2 512.9 %reduce-scatter.31.cloned.1.call-start = ((), (), s32[]{:S(2)}) async-start(), calls=%async_computation.27 | async-start | bytes 9437184 | tf_op jit(solution)/shard_map/while/body/eval_jaxpr/reduce_scatter | solution.py:203
  2221.7 134.5 %slice-start = ((s8[5767168]{0:T(1024)(128)(4,1)}), s8[1572864]{0:T(1024)(128)(4,1)S(1)}, s32[]{:S(2)}) async-start(s8[5767168]{0:T(1024)(128)(4,1)} %bitcast.290), calls=%async_computation.28 | async-start | bytes 3145728 | tf_op jit(solution)/shard_map/while
  2362.8 432.6 %reduce-scatter.29.cloned.1.call-start = ((), (), s32[]{:S(2)}) async-start(), calls=%async_computation.26 | async-start | bytes 18874368 | tf_op jit(solution)/shard_map/while/body/eval_jaxpr/reduce_scatter | solution.py:200
  2802.9 22.2 copy-start
  2802.9 230.7 %all-gather.29.cloned.1.call-start = ((), (), s32[]{:S(2)}) async-start(), calls=%async_computation.24 | async-start | bytes 18874368 | tf_op jit(solution)/shard_map/while/body/eval_jaxpr/all_gather | solution.py:182
  2806.8 351.9 %all-gather.31.cloned.1.call-start = ((), (), s32[]{:S(2)}) async-start(), calls=%async_computation.25 | async-start | bytes 9437184 | tf_op jit(solution)/shard_map/while/body/eval_jaxpr/all_gather | solution.py:183
  2809.2 512.8 %reduce-scatter.31.cloned.1.call-start = ((), (), s32[]{:S(2)}) async-start(), calls=%async_computation.27 | async-start | bytes 9437184 | tf_op jit(solution)/shard_map/while/body/eval_jaxpr/reduce_scatter | solution.py:203
  3033.6 134.5 %slice-start = ((s8[5767168]{0:T(1024)(128)(4,1)}), s8[1572864]{0:T(1024)(128)(4,1)S(1)}, s32[]{:S(2)}) async-start(s8[5767168]{0:T(1024)(128)(4,1)} %bitcast.290), calls=%async_computation.28 | async-start | bytes 3145728 | tf_op jit(solution)/shard_map/while
  3174.7 432.5 %reduce-scatter.29.cloned.1.call-start = ((), (), s32[]{:S(2)}) async-start(), calls=%async_computation.26 | async-start | bytes 18874368 | tf_op jit(solution)/shard_map/while/body/eval_jaxpr/reduce_scatter | solution.py:200
  3622.4 59.2 %reduce-scatter.15.cloned.1.call-start = ((), (), s32[]{:S(2)}) async-start(), calls=%async_computation.16 | async-start | bytes 2621440 | tf_op jit(solution)/shard_map/reduce_scatter | solution.py:222
  3631.4 64.5 %reduce-scatter.17.cloned.1.call-start = ((), (), s32[]{:S(2)}) async-start(), calls=%async_computation.17 | async-start | bytes 2621440 | tf_op jit(solution)/shard_map/reduce_scatter | solution.py:228
  3640.8 82.3 %all-gather.27.cloned.1.call-start = ((), (), s32[]{:S(2)}) async-start(), calls=%async_computation.18 | async-start | bytes 2621440 | tf_op jit(solution)/shard_map/all_gather | solution.py:261
  3642.6 53.3 %copy-start.11 = (f32[64,2,2048]{2,0,1:T(8,128)S(1)}, f32[64,2,2048]{2,0,1:T(8,128)}, u32[]{:S(2)}) copy-start(f32[64,2,2048]{2,0,1:T(8,128)} %copy-done.10) | copy-start | bytes 3145732
  3642.7 53.3 %copy-start.64 = (f32[64,2]{0,1:T(2,128)S(1)}, f32[64,2]{0,1:T(2,128)}, u32[]{:S(2)}) copy-start(f32[64,2]{0,1:T(2,128)} %copy-done.63) | copy-start | bytes 1540
  3668.3 30.1 copy-start.21
  3668.3 30.1 copy-start.47
  3668.3 30.1 copy-start.70
  3700.4 96.6 %reduce-scatter.27.cloned.1.call-start = ((), (), s32[]{:S(2)}) async-start(), calls=%async_computation.23 | async-start | bytes 36864
  3700.6 28.1 copy-start.6
  3734.2 15.2 copy-start.68
  3734.2 15.2 copy-start.69
  3743.3 86.7 %reduce-scatter.19.cloned.1.call-start = ((), (), s32[]{:S(2)}) async-start(), calls=%async_computation.19 | async-start | bytes 2621440 | tf_op jit(solution)/shard_map/reduce_scatter | solution.py:332
  3759.8 135.4 %reduce-scatter.25.cloned.1.call-start = ((), (), s32[]{:S(2)}) async-start(), calls=%async_computation.22 | async-start | bytes 147456 | tf_op jit(solution)/shard_map/reduce_scatter | solution.py:356
  3760.8 204.8 %reduce-scatter.23.cloned.1.call-start = ((), (), s32[]{:S(2)}) async-start(), calls=%async_computation.21 | async-start | bytes 2359296 | tf_op jit(solution)/shard_map/reduce_scatter | solution.py:353
  3765.2 321.2 %reduce-scatter.21.cloned.1.call-start = ((), (), s32[]{:S(2)}) async-start(), calls=%async_computation.20 | async-start | bytes 7077888 | tf_op jit(solution)/shard_map/reduce_scatter | solution.py:350
  3772.3 57.6 %copy-start.15 = (bf16[64,2,2048]{2,1,0:T(2,128)(2,1)S(1)}, bf16[64,2,2048]{2,1,0:T(2,128)(2,1)}, u32[]{:S(2)}) copy-start(bf16[64,2,2048]{2,1,0:T(2,128)(2,1)} %param.14) | copy-start | bytes 1572868
  3772.3 57.6 %copy-start.24 = (f32[64,2,2048]{2,0,1:T(8,128)S(1)}, f32[64,2,2048]{2,0,1:T(8,128)}, u32[]{:S(2)}) copy-start(f32[64,2,2048]{2,0,1:T(8,128)} %get-tuple-element.277) | copy-start | bytes 3145732
  3772.3 57.6 %copy-start.57 = (f32[8,1,256]{2,1,0:T(1,128)S(1)}, f32[8,1,256]{2,1,0:T(1,128)}, u32[]{:S(2)}) copy-start(f32[8,1,256]{2,1,0:T(1,128)} %copy-done.56) | copy-start | bytes 24580
  3772.4 57.6 %copy-start.66 = (f32[64,2]{0,1:T(2,128)S(1)}, f32[64,2]{0,1:T(2,128)}, u32[]{:S(2)}) copy-start(f32[64,2]{0,1:T(2,128)} %copy-done.65) | copy-start | bytes 1540
  3772.4 57.6 %copy-start.72 = (f32[64,2]{0,1:T(2,128)S(1)}, f32[64,2]{0,1:T(2,128)}, u32[]{:S(2)}) copy-start(f32[64,2]{0,1:T(2,128)} %get-tuple-element.265) | copy-start | bytes 1540
  (82 other events, 342.2 us)
Sparse Core Ops, SparseCore 0:
  34.8 19.8 all-gather.16
  56.9 99.0 all-gather.18
  158.1 47.6 all-gather.20
  210.8 43.0 reduce-scatter.12
  255.4 22.5 all-gather.24
  280.1 22.5 all-gather.22
  370.1 227.5 all-gather.28
  599.8 123.0 all-gather.30
  739.0 147.2 reduce-scatter.30
  890.4 281.0 reduce-scatter.28
  1183.0 226.6 all-gather.28
  1411.7 123.0 all-gather.30
  1550.9 147.1 reduce-scatter.30
  1702.2 280.8 reduce-scatter.28
  1994.9 226.6 all-gather.28
  2223.7 123.0 all-gather.30
  2362.9 147.2 reduce-scatter.30
  2514.3 281.0 reduce-scatter.28
  2806.9 226.5 all-gather.28
  3035.6 123.0 all-gather.30
  3174.8 147.2 reduce-scatter.30
  3326.3 280.8 reduce-scatter.28
  3631.6 30.4 reduce-scatter.14
  3664.4 31.4 reduce-scatter.16
  3700.5 22.5 all-gather.26
  3743.4 53.5 reduce-scatter.26
  3799.5 30.4 reduce-scatter.18
  3833.9 61.2 reduce-scatter.24
  3898.7 66.8 reduce-scatter.22
  3969.1 117.3 reduce-scatter.20
where the time goes:
time: 4100 us
  waiting for transfers between devices  3030 us (74%)
  matrix products  302 us (7%)
  other arithmetic  296 us (7%)
  local copies, waits for them, and re-layouts  284 us (7%)
  blocking collectives  159 us (4%)
    reduce_scatter x4, waiting for transfers between devices, expert_step(): lax.psum_scatter(grad_in_part.astype(jnp.bfloat16), 'dp', scatter_dimensi...  1130 us
    all_gather x4, waiting for transfers between devices, expert_step(): lax.all_gather(part_in, 'dp', axis=1, tiled=True)  807 us
    all_gather x4, waiting for transfers between devices, expert_step(): lax.all_gather(part_out, 'dp', axis=1, tiled=True)  451 us
    reduce_scatter x4, waiting for transfers between devices, expert_step(): lax.psum_scatter(grad_out_part.astype(jnp.bfloat16), 'dp', scatter_dimens...  193 us
    reduce_scatter x1, waiting for transfers between devices, body(): lax.psum_scatter(grad_qkv.astype(jnp.bfloat16), 'dp', scatter_dimension=0...  119 us
    scatter-add x4, other arithmetic, expert_step(): mixture_acc.at[where_from].add(expert_rows * gate_slice[:, None])  102 us
    scatter-add x4, other arithmetic, expert_step(): return_acc.at[where_from].add(d_chosen.reshape(group_slots, features))  102 us
    all_gather x1, waiting for transfers between devices, body(): lax.all_gather(w_qkv, 'dp', axis=0, tiled=True)  88.3 us
  transfers between devices with their start and end apart: 30, of which 26 were waited for; matrix products, arithmetic and copies ran while one was open for 17% of the time, Pallas kernels for 0%

commit v1 on v0

v1 whole, which is shorter than its diff:
```python
import functools

import jax
import jax.numpy as jnp
from jax import lax
from jax.sharding import PartitionSpec as P

WINDOW = 128
CAP = 176
EPSILON = 1e-05
MASKED = -1e30

F32 = jnp.float32
BF16 = jnp.bfloat16


def norm_factor(values):
    return lax.rsqrt(jnp.mean(values * values, axis=-1, keepdims=True) + EPSILON)


def norm_back(values, factor, gain_row, upstream):
    features = values.shape[-1]
    inner = jnp.sum(values * gain_row * upstream, axis=-1, keepdims=True)
    return factor * gain_row * upstream - values * factor**3 * inner / features


def softmax_rows(logits):
    highest = jnp.max(logits, axis=-1, keepdims=True)
    raised = jnp.exp(logits - highest)
    return raised / jnp.sum(raised, axis=-1, keepdims=True)


def dot(spec, left, right):
    return jnp.einsum(spec, left, right, preferred_element_type=F32)


def swap_blocks(blocks, ranks):
    own = lax.axis_index("dp")
    result = jnp.zeros_like(blocks)
    kept = lax.dynamic_index_in_dim(blocks, own, 0, keepdims=True)
    result = lax.dynamic_update_slice_in_dim(result, kept, own, 0)
    for shift in range(1, ranks):
        target = lax.rem(own + shift, ranks)
        origin = lax.rem(own + ranks - shift, ranks)
        block = lax.dynamic_index_in_dim(blocks, target, 0, keepdims=True)
        moved = lax.ppermute(block, "dp", [(j, (j + shift) % ranks) for j in range(ranks)])
        result = lax.dynamic_update_slice_in_dim(result, moved, origin, 0)
    return result


def body(
    ranks,
    quarters,
    tokens,
    cotangent,
    segments,
    expert_ids,
    attn_gain,
    w_qkv,
    qk_gain,
    w_out,
    mlp_gain,
    router,
    expert_in,
    expert_out,
):
    everyone = ("dp", "tensor")
    rank = lax.axis_index("dp")
    quarter = lax.axis_index("tensor")
    local_rows, micro_count, features = tokens.shape
    experts, depth, _, width = expert_in.shape
    owned = experts // ranks
    local_tokens = local_rows * micro_count
    group_tokens = quarters * local_tokens
    all_tokens = ranks * group_tokens
    head_dim = qk_gain.shape[0] * ranks
    local_heads = qk_gain.shape[2]
    local_width = local_heads * head_dim
    seq_len = local_rows * quarters
    scale = head_dim ** (-0.5)

    in_blocks = expert_in.reshape(ranks, owned, depth, 2 * width)
    out_blocks = expert_out.reshape(ranks, owned, depth, width)
    held_in = swap_blocks(in_blocks, ranks)
    held_out = swap_blocks(out_blocks, ranks)

    full_qkv = lax.all_gather(w_qkv, "dp", axis=0, tiled=True)
    full_out = lax.all_gather(w_out, "dp", axis=0, tiled=True)
    small = jnp.concatenate(
        [router, attn_gain[:, None], mlp_gain[:, None]], axis=1
    ).reshape(1, -1)
    small = jnp.concatenate([small, qk_gain.reshape(1, -1)], axis=1)
    small = lax.all_gather(small, "dp", axis=0, tiled=True)
    columns = experts + 2
    small_rows = small[:, : depth * columns].reshape(features, columns)
    full_router = small_rows[:, :experts]
    gain_one = small_rows[:, experts].astype(F32)
    gain_two = small_rows[:, experts + 1].astype(F32)
    full_qk = small[:, depth * columns :].reshape(head_dim, 2, local_heads)
    all_ids = lax.all_gather(expert_ids, "dp", axis=0, tiled=True)

    raw_rows = lax.all_gather(tokens, "tensor", axis=0, tiled=True).astype(F32)
    rows_one = (raw_rows * norm_factor(raw_rows) * gain_one).astype(BF16)
    projected = dot("smd,djf->jmsf", rows_one, full_qkv)
    query_raw = projected[0]
    key_raw = projected[1]
    value_rows = projected[2].astype(BF16)
    square_q, square_k = lax.psum(
        (jnp.sum(query_raw * query_raw, axis=-1), jnp.sum(key_raw * key_raw, axis=-1)), "tensor"
    )
    factor_q = lax.rsqrt(square_q[..., None] / features + EPSILON)
    factor_k = lax.rsqrt(square_k[..., None] / features + EPSILON)
    qk_rows = jnp.transpose(full_qk.astype(F32), (1, 2, 0)).reshape(2, local_width)
    heads_shape = (micro_count, seq_len, local_heads, head_dim)
    query_heads = (query_raw * factor_q * qk_rows[0]).astype(BF16).reshape(heads_shape)
    key_heads = (key_raw * factor_k * qk_rows[1]).astype(BF16).reshape(heads_shape)
    value_heads = value_rows.reshape(heads_shape)
    seq_major = segments.T
    positions = jnp.arange(seq_len)
    distance = positions[:, None] - positions[None, :]
    same_doc = seq_major[:, :, None] == seq_major[:, None, :]
    allowed = (same_doc & (distance >= 0) & (distance < WINDOW))[:, None]
    scores = jnp.where(allowed, dot("mqhc,mkhc->mhqk", query_heads, key_heads) * scale, MASKED)
    weights_full = softmax_rows(scores)
    weights_low = weights_full.astype(BF16)
    head_out = dot("mhqk,mkhc->mqhc", weights_low, value_heads).astype(BF16)
    head_out = head_out.reshape(micro_count, seq_len, local_width)
    attended = lax.psum_scatter(
        dot("msf,df->smd", head_out, full_out), "tensor", scatter_dimension=0, tiled=True
    )
    inputs = tokens.astype(F32)
    residual = inputs + attended
    factor_two = norm_factor(residual)
    normed_two = (residual * factor_two * gain_two).astype(BF16)

    rows_all = lax.all_gather(
        normed_two.reshape(local_tokens, features), everyone, axis=0, tiled=True
    )
    pull_all = lax.all_gather(
        cotangent.reshape(local_tokens, features), everyone, axis=0, tiled=True
    )
    router_probs = softmax_rows(dot("td,de->te", rows_all, full_router))

    first = rank * owned
    routes = all_ids.reshape(ranks, group_tokens, -1)
    names = first + jnp.arange(owned, dtype=jnp.int32)
    member = jnp.any(routes[None] == names[:, None, None, None], axis=-1)
    order = jnp.arange(group_tokens)
    earlier = (order[:, None] < order[None, :]).astype(BF16)
    position = dot("egs,st->egt", member.astype(BF16), earlier)
    position = jnp.where(member, position, -1.0).astype(jnp.int32)
    place = position[:, :, None, :] == jnp.arange(CAP, dtype=jnp.int32)[:, None]
    gate_own = lax.dynamic_slice_in_dim(router_probs, first, owned, 1)
    gate_own = gate_own.T.reshape(owned, ranks, 1, group_tokens)
    gate_slot = jnp.sum(jnp.where(place, gate_own, 0.0), axis=-1)
    place = place.astype(BF16)
    grouped_rows = rows_all.reshape(ranks, group_tokens, features)
    grouped_pull = pull_all.reshape(ranks, group_tokens, features)

    mixed_rows = []
    returned_rows = []
    slot_dots = []
    grads_in = []
    grads_out = []
    for e in range(owned):
        weight_in = held_in[:, e].reshape(features, 2 * width)
        weight_out = held_out[:, e].reshape(features, width)
        slots = ranks * CAP
        chosen = dot("gpt,gtd->gpd", place[e], grouped_rows).astype(BF16).reshape(slots, features)
        pulled = dot("gpt,gtd->gpd", place[e], grouped_pull).astype(BF16).reshape(slots, features)
        gate = gate_slot[e].reshape(slots, 1)
        gate_up = dot("sd,df->sf", chosen, weight_in)
        gate_part = gate_up[:, :width]
        up_part = gate_up[:, width:]
        sigmoid_gate = jax.nn.sigmoid(gate_part)
        activated = gate_part * sigmoid_gate
        hidden = activated * up_part
        d_plain = dot("sd,df->sf", pulled, weight_out)
        slot_dots.append(jnp.sum(hidden * d_plain, axis=-1))
        d_hidden = d_plain * gate
        d_gate_part = d_hidden * up_part * sigmoid_gate * (1.0 + gate_part * (1.0 - sigmoid_gate))
        d_gate_up = jnp.concatenate([d_gate_part, d_hidden * activated], axis=1).astype(BF16)
        hidden_gated = (hidden * gate).astype(BF16)
        mixed_rows.append(
            dot("sf,df->sd", hidden_gated, weight_out).astype(BF16).reshape(ranks, CAP, features)
        )
        returned_rows.append(
            dot("sf,df->sd", d_gate_up, weight_in).astype(BF16).reshape(ranks, CAP, features)
        )
        grads_in.append(dot("sd,sf->df", chosen, d_gate_up).astype(BF16))
        grads_out.append(dot("sd,sf->df", pulled, hidden_gated).astype(BF16))
    slot_dots = jnp.stack(slot_dots).reshape(owned, ranks, CAP, 1)
    d_gate_token = jnp.sum(jnp.where(place > 0, slot_dots, 0.0), axis=2)
    d_gate_token = d_gate_token.reshape(owned, all_tokens).T
    spread = lax.dynamic_update_slice(
        jnp.zeros((all_tokens, 128), F32), d_gate_token, (0, first)
    ).astype(BF16)
    mixed = jnp.stack(mixed_rows)
    returned = jnp.stack(returned_rows)
    mixture_all = dot("egpt,egpd->gtd", place, mixed).astype(BF16)
    returned_all = dot("egpt,egpd->gtd", place, returned).astype(BF16)
    returned_all = jnp.concatenate([returned_all.reshape(all_tokens, features), spread], axis=1)
    returned_own = lax.psum_scatter(returned_all, everyone, scatter_dimension=0, tiled=True)
    mixture_own = lax.psum_scatter(
        mixture_all.reshape(all_tokens, features), everyone, scatter_dimension=0, tiled=True
    )
    layer_out = (
        residual + mixture_own.astype(F32).reshape(local_rows, micro_count, features)
    ).astype(BF16)

    def home(parts):
        stacked = jnp.stack([part.reshape(ranks, depth, -1) for part in parts], axis=1)
        return swap_blocks(stacked, ranks).reshape(experts, depth, -1).astype(F32)

    grad_expert_in = home(grads_in).reshape(experts, depth, 2, width)
    grad_expert_out = home(grads_out)

    returned_f = returned_own[:, :features].astype(F32).reshape(local_rows, micro_count, features)
    d_probs = returned_own[:, features : features + experts].astype(F32)
    first_token = (rank * quarters + quarter) * local_tokens
    probs_own = lax.dynamic_slice_in_dim(router_probs, first_token, local_tokens, 0)
    d_logits = (
        probs_own * (d_probs - jnp.sum(d_probs * probs_own, axis=-1, keepdims=True))
    ).astype(BF16)
    d_normed_two = returned_f + dot("te,de->td", d_logits, full_router).reshape(residual.shape)
    grad_router = dot("td,te->de", normed_two.reshape(local_tokens, features), d_logits)
    d_residual = cotangent.astype(F32) + norm_back(residual, factor_two, gain_two, d_normed_two)
    grad_gain_two = jnp.sum(residual * factor_two * d_normed_two, axis=(0, 1))
    d_attended = d_residual.astype(BF16)

    rows_back = lax.all_gather(d_attended, "tensor", axis=0, tiled=True)
    d_head_out = dot("smd,df->msf", rows_back, full_out).astype(BF16)
    grad_w_out = dot("smd,msf->df", rows_back, head_out)
    d_heads = d_head_out.reshape(heads_shape)
    d_weights = dot("mqhc,mkhc->mhqk", d_heads, value_heads)
    d_scores = (
        weights_full * (d_weights - jnp.sum(d_weights * weights_full, axis=-1, keepdims=True))
    ).astype(BF16)
    flat_shape = (micro_count, seq_len, local_width)
    d_queries = (dot("mhqk,mkhc->mqhc", d_scores, key_heads) * scale).reshape(flat_shape)
    d_keys = (dot("mhqk,mqhc->mkhc", d_scores, query_heads) * scale).reshape(flat_shape)
    d_values = dot("mhqk,mqhc->mkhc", weights_low, d_heads).reshape(flat_shape).astype(BF16)
    inner_q, inner_k = lax.psum(
        (
            jnp.sum(query_raw * qk_rows[0] * d_queries, axis=-1),
            jnp.sum(key_raw * qk_rows[1] * d_keys, axis=-1),
        ),
        "tensor",
    )
    d_query_raw = (
        factor_q * qk_rows[0] * d_queries - query_raw * factor_q**3 * inner_q[..., None] / features
    )
    d_key_raw = (
        factor_k * qk_rows[1] * d_keys - key_raw * factor_k**3 * inner_k[..., None] / features
    )
    grad_qk_rows = jnp.stack(
        [
            jnp.sum(query_raw * factor_q * d_queries, axis=(0, 1)),
            jnp.sum(key_raw * factor_k * d_keys, axis=(0, 1)),
        ]
    )
    grad_qk = jnp.transpose(grad_qk_rows.reshape(2, local_heads, head_dim), (2, 0, 1))
    d_projected = jnp.stack([d_query_raw.astype(BF16), d_key_raw.astype(BF16), d_values])
    grad_qkv = dot("smd,jmsf->djf", rows_one, d_projected)
    d_normed_one = lax.psum_scatter(
        dot("jmsf,djf->smd", d_projected, full_qkv).astype(BF16),
        "tensor",
        scatter_dimension=0,
        tiled=True,
    ).astype(F32)
    factor_one = norm_factor(inputs)
    grad_tokens = (d_residual + norm_back(inputs, factor_one, gain_one, d_normed_one)).astype(BF16)
    grad_gain_one = jnp.sum(inputs * factor_one * d_normed_one, axis=(0, 1))

    grad_qkv_own = lax.psum_scatter(
        grad_qkv.astype(BF16), "dp", scatter_dimension=0, tiled=True
    ).astype(F32)
    grad_out_own = lax.psum_scatter(
        grad_w_out.astype(BF16), "dp", scatter_dimension=0, tiled=True
    ).astype(F32)
    small_grads = jnp.concatenate(
        [grad_router, grad_gain_one[:, None], grad_gain_two[:, None]], axis=1
    ).reshape(ranks, -1)
    small_grads = jnp.concatenate([small_grads, grad_qk.reshape(ranks, -1)], axis=1)
    small_own = lax.psum_scatter(small_grads, "dp", scatter_dimension=0, tiled=True)[0]
    grad_qk_own = small_own[depth * columns :].reshape(qk_gain.shape)
    shared_own = lax.psum(small_own[: depth * columns], "tensor").reshape(depth, columns)
    return (
        layer_out,
        grad_tokens,
        shared_own[:, experts],
        grad_qkv_own,
        grad_qk_own,
        grad_out_own,
        shared_own[:, experts + 1],
        shared_own[:, :experts],
        grad_expert_in,
        grad_expert_out,
    )


def solution(mesh):
    placed = (
        P(("dp", "tensor"), None, None),
        P(("dp", "tensor"), None, None),
        P("dp", None),
        P("dp", None, None),
        P("dp"),
        P("dp", None, "tensor"),
        P("dp", None, "tensor"),
        P("dp", "tensor"),
        P("dp"),
        P("dp", None),
        P(None, "dp", None, "tensor"),
        P(None, "dp", "tensor"),
    )
    return jax.shard_map(
        functools.partial(body, mesh.shape["dp"], mesh.shape["tensor"]),
        mesh=mesh,
        in_specs=placed,
        out_specs=(
            P(("dp", "tensor"), None, None),
            P(("dp", "tensor"), None, None),
            P("dp"),
            P("dp", None, "tensor"),
            P("dp", None, "tensor"),
            P("dp", "tensor"),
            P("dp"),
            P("dp", None),
            P(None, "dp", None, "tensor"),
            P(None, "dp", "tensor"),
        ),
        check_vma=False,
    )
```

time: 4100 us -> 1870 us (0.46)
  waiting for transfers between devices: 3030 us -> 857 us
  other arithmetic: 296 us -> 64.7 us
  starting transfers between devices: 2.45 us -> 223 us
  local copies, waits for them, and re-layouts: 284 us -> 183 us
  blocking collectives: 159 us -> 203 us
    all_gather x13 -> x5, waiting for transfers between devices: 1370 us -> 107 us  [the longest x1 85.1 us: body(): full_qkv = lax.all_gather(w_qkv, 'dp', axis=0, tiled=True)]
    reduce_scatter x15 -> x6, waiting for transfers between devices: 1610 us -> 429 us  [the longest x1 224 us: body(): lax.psum_scatter(returned_all, everyone, scatter_dimension=0, tiled=True)]
    ppermute x0 -> x28, waiting for transfers between devices: none -> 315 us  [swap_blocks(): lax.ppermute(block, 'dp', [(j, (j + shift) % ranks) for j in range(ranks)])]
    ppermute x0 -> x28, starting transfers between devices: none -> 221 us  [swap_blocks(): lax.ppermute(block, 'dp', [(j, (j + shift) % ranks) for j in range(ranks)])]
    scatter-add x8 -> x0, other arithmetic: 204 us -> none  [the longest x4 102 us: expert_step(): mixture_acc.at[where_from].add(expert_rows * gate_slice[:, None])]
    gather x9 -> x0, local copies, waits for them, and re-layouts: 111 us -> none  [the longest x4 57.5 us: expert_step(): chosen = padded_rows[where_from].reshape(EG, CAP, features)]
    all_gather x4 -> x2, blocking collectives: 102 us -> 177 us  [the longest x1 145 us: body(): all_ids = lax.all_gather(expert_ids, 'dp', axis=0, tiled=True)]
    dot_general x39 -> x50, matrix products: 301 us -> 307 us  [dot(): return jnp.einsum(spec, left, right, preferred_element_type=F32)]
  transfers between devices with their start and end apart: 30 -> 41, of which waited for: 26 -> 18; matrix products, arithmetic and copies ran while one was open for 17% -> 17% of each run, Pallas kernels for 0% -> 0%
where the time goes in v1:
time: 1870 us; the launch traced here: 1860 us
  waiting for transfers between devices  857 us (46%)
  matrix products  307 us (16%)
  starting transfers between devices  223 us (12%)
  blocking collectives  203 us (11%)
  local copies, waits for them, and re-layouts  183 us (10%)
  other arithmetic  64.7 us (3%)
    ppermute x28, waiting for transfers between devices, swap_blocks(): lax.ppermute(block, 'dp', [(j, (j + shift) % ranks) for j in range(ranks)])  315 us
    dot_general x50, matrix products, dot(): return jnp.einsum(spec, left, right, preferred_element_type=F32)  307 us
    reduce_scatter x1, waiting for transfers between devices, body(): lax.psum_scatter(returned_all, everyone, scatter_dimension=0, tiled=True)  224 us
    ppermute x28, starting transfers between devices, swap_blocks(): lax.ppermute(block, 'dp', [(j, (j + shift) % ranks) for j in range(ranks)])  221 us
    all_gather x1, blocking collectives, body(): all_ids = lax.all_gather(expert_ids, 'dp', axis=0, tiled=True)  145 us
    reduce_scatter x1, waiting for transfers between devices, body(): lax.psum_scatter(mixture_all.reshape(all_tokens, features), everyone, sca...  136 us
    all_gather x1, waiting for transfers between devices, body(): full_qkv = lax.all_gather(w_qkv, 'dp', axis=0, tiled=True)  85.1 us
    unnamed x289, local copies, waits for them, and re-layouts  46.9 us
  transfers between devices with their start and end apart: 41, of which 18 were waited for; matrix products, arithmetic and copies ran while one was open for 17% of the time, Pallas kernels for 0%

profile of v1, /device:TPU:0, one launch (start us, length us, event | category | flops | bytes accessed | tf_op | source)
XLA Modules:
  0.0 1855.6 jit_solution(2075808107385731570)
XLA Ops:
  13.6 32.6 %all-gather = bf16[8,1,8832]{2,1,0:T(2,128)(2,1)S(1)} all-gather(bf16[1,1,8832]{2,1,0:T(2,128)(2,1)S(1)} %maximum_bitcast_fusion), channel_id=1, replica_groups=mesh['dp'=8,'tensor'=4] {'dp'}, dimensions={0}, use_global_device_ids=true | all-gather | bytes 158976 | tf_op jit(solution)/shard_map/all_gather | solution.py:93
  51.9 85.1 %all-gather.10.cloned.1.call-done = bf16[2048,3,512]{2,0,1:T(8,128)(2,1)} async-done(((bf16[256,3,512]{2,0,1:T(8,128)(2,1)}), bf16[2048,3,512]{2,0,1:T(8,128)(2,1)}) %all-gather.10.cloned.1.call-update) | async-done | bytes 6291472 | tf_op jit(solution)/shard_map/all_gather | solution.py:87
  137.0 7.9 fusion.51
  152.1 6.5 all-reduce.2
  164.4 22.4 %all-gather.12.cloned.1.call-done = bf16[2048,512]{1,0:T(8,128)(2,1)} async-done(((bf16[256,512]{1,0:T(8,128)(2,1)}), bf16[2048,512]{1,0:T(8,128)(2,1)}) %all-gather.12.cloned.1.call-update) | async-done | bytes 2097168 | tf_op jit(solution)/shard_map/all_gather | solution.py:88
  186.8 4.9 convolution_bitcast_fusion
  194.0 41.1 %reduce-scatter.9.cloned.1.call-done = f32[64,2,2048]{2,0,1:T(8,128)} async-done(((f32[256,2,2048]{2,0,1:T(8,128)}), f32[64,2,2048]{2,0,1:T(8,128)}) %reduce-scatter.9.cloned.1.call-update) | async-done | bytes 1048592 | tf_op jit(solution)/shard_map/reduce_scatter | solution.py:128
  255.0 144.7 %all_gather.28 = s32[2048,2,8]{0,2,1:T(8,128)S(1)} all-gather(s32[256,2,8]{0,2,1:T(8,128)S(1)} %copy-done.108), channel_id=1, replica_groups=mesh['dp'=8,'tensor'=4] {'dp'}, dimensions={0}, use_global_device_ids=true | all-gather | bytes 147456 | tf_op jit(solution)/shard_map/all_gather | solution.py:100
  401.3 14.0 reshape.335
  430.5 24.7 %collective-permute-done.7 = bf16[1,4,256,256]{3,2,1,0:T(8,128)(2,1)} collective-permute-done((bf16[1,4,256,256]{3,2,1,0:T(8,128)(2,1)}, bf16[1,4,256,256]{3,2,1,0:T(8,128)(2,1)}, u32[]{:S(2)}, u32[]{:S(2)}) %collective-permute-start.7) | collective-permute-done | bytes 524320 | tf_op jit(solution)/shard_map/ppermute | solution.py:46
  465.0 8.7 collective-permute-done.12
  473.7 50.9 %collective-permute-start.4 = (bf16[1,4,256,512]{3,2,1,0:T(8,128)(2,1)S(1)}, bf16[1,4,256,512]{3,2,1,0:T(8,128)(2,1)S(1)}, u32[]{:S(2)}, u32[]{:S(2)}) collective-permute-start(bf16[1,4,256,512]{3,2,1,0:T(8,128)(2,1)S(1)} %copy-done.56), channel_id=1, source_target_pairs={{0,20},{4,24},{8,28},{12,0},{16,4},{20,8},{24,12},{28,16},{1,21},{... | collective-permute-start | bytes 3145736 | tf_op jit(solution)/shard_map/ppermute | solution.py:46
  527.4 8.2 collective-permute-start.5
  542.4 74.9 %collective-permute-done.2 = bf16[1,4,256,512]{3,2,1,0:T(8,128)(2,1)S(1)} collective-permute-done((bf16[1,4,256,512]{3,2,1,0:T(8,128)(2,1)}, bf16[1,4,256,512]{3,2,1,0:T(8,128)(2,1)S(1)}, u32[]{:S(2)}, u32[]{:S(2)}) %collective-permute-start.2) | collective-permute-done | bytes 1048608 | tf_op jit(solution)/shard_map/ppermute | solution.py:46
  617.7 20.6 %collective-permute-done.5 = bf16[1,4,256,512]{3,2,1,0:T(8,128)(2,1)S(1)} collective-permute-done((bf16[1,4,256,512]{3,2,1,0:T(8,128)(2,1)S(1)}, bf16[1,4,256,512]{3,2,1,0:T(8,128)(2,1)S(1)}, u32[]{:S(2)}, u32[]{:S(2)}) %collective-permute-start.5) | collective-permute-done | bytes 1048608 | tf_op jit(solution)/shard_map/ppermute | solution.py:46
  642.3 11.3 convolution_convert_fusion.8
  653.7 11.3 convolution_convert_fusion.9
  665.0 11.4 convolution_convert_fusion.10
  676.4 11.7 convolution_convert_fusion.11
  688.0 11.5 convolution_convert_fusion.12
  699.5 11.4 convolution_convert_fusion.13
  710.9 11.4 convolution_convert_fusion.14
  722.3 11.6 convolution_convert_fusion.15
  733.9 10.9 fusion.120
  745.9 7.0 fusion.128
  755.2 6.9 fusion.125
  762.1 7.5 multiply_reduce_fusion.4
  770.3 5.8 fusion.127
  776.2 7.5 multiply_reduce_fusion.2
  785.1 5.8 fusion.126
  790.9 6.9 multiply_reduce_fusion.3
  798.0 5.2 select_reduce_fusion
  822.2 5.1 convolution_convert_fusion.4
  827.3 5.1 convolution_convert_fusion.7
  832.4 18.4 bitcast_convert_fusion
  850.8 21.3 %copy.345 = bf16[4096,2048]{0,1:T(8,128)(2,1)} copy(bf16[4096,2048]{1,0:T(8,128)(2,1)} %bitcast.285) | data formatting | bytes 33554432 | tf_op jit(solution)/shard_map/reshape | solution.py:202
  872.3 14.2 pad_maximum_fusion
  886.5 22.1 %copy.404 = bf16[4096,2176]{1,0:T(8,128)(2,1)} copy(bf16[4096,2176]{0,1:T(8,128)(2,1)} %pad_maximum_fusion) | data formatting | bytes 35651584
  908.6 5.6 convolution_convert_fusion.2
  926.9 223.8 %reduce-scatter.19.cloned.1.call-done = bf16[128,2176]{1,0:T(8,128)(2,1)} async-done(((bf16[4096,2176]{1,0:T(8,128)(2,1)}), bf16[128,2176]{1,0:T(8,128)(2,1)}) %reduce-scatter.19.cloned.1.call-update) | async-done | bytes 557072 | tf_op jit(solution)/shard_map/reduce_scatter | solution.py:203
  1158.7 20.0 %bitcast_convert_fusion.1 = bf16[8,512,2048]{2,1,0:T(8,128)(2,1)} fusion(bf16[1,8,176,2048]{3,2,1,0:T(8,128)(2,1)} %bitcast.288, bf16[1,8,176,2048]{3,2,1,0:T(8,128)(2,1)} %bitcast.287, bf16[1,8,176,2048]{3,2,1,0:T(8,128)(2,1)} %bitcast.286, bf16[1,8,176,2048]{3,2,1,0:T(8,128)(2,1)} %bitcast.289, s32[4,8,512]{2,1,0:T(8,128)S(1)} %copy-done.93), kind=kOutput, calls=%fused_computation.4 | convolution fusion | flops 11857035264 | bytes 39911424 | tf_op jit(solution)/shard_map/egpt,egpd->gtd/dot_general | solution.py:34
  1205.8 6.6 all-reduce.1
  1214.7 8.2 fusion.35
  1227.4 135.6 %reduce-scatter.11.cloned.1.call-done = bf16[128,2048]{1,0:T(8,128)(2,1)} async-done(((bf16[4096,2048]{1,0:T(8,128)(2,1)}), bf16[128,2048]{1,0:T(8,128)(2,1)}) %reduce-scatter.11.cloned.1.call-update) | async-done | bytes 524304 | tf_op jit(solution)/shard_map/reduce_scatter | solution.py:204
  1370.2 28.6 %reduce-scatter.13.cloned.1.call-done = bf16[64,2,2048]{2,0,1:T(8,128)(2,1)} async-done(((bf16[256,2,2048]{2,0,1:T(8,128)(2,1)}), bf16[64,2,2048]{2,0,1:T(8,128)(2,1)}) %reduce-scatter.13.cloned.1.call-update) | async-done | bytes 524304 | tf_op jit(solution)/shard_map/reduce_scatter | solution.py:265
  1402.3 9.2 bitcast_convert_fusion.2
  1412.8 4.7 convolution_convert_fusion.23
  1432.7 4.3 convolution_convert_fusion.19
  1437.1 4.3 convolution_convert_fusion.16
  1441.5 4.3 convolution_convert_fusion.17
  1460.2 10.2 collective-permute-done.21
  1470.4 57.1 %collective-permute-start.24 = (bf16[1,4,256,256]{3,2,0,1:T(8,128)(2,1)S(1)}, bf16[1,4,256,256]{3,2,0,1:T(8,128)(2,1)S(1)}, u32[]{:S(2)}, u32[]{:S(2)}) collective-permute-start(bf16[1,4,256,256]{3,2,0,1:T(8,128)(2,1)S(1)} %copy-done.84), channel_id=1, source_target_pairs={{0,16},{4,20},{8,24},{12,28},{16,0},{20,4},{24,8},{28,12},{1,17},{... | collective-permute-start | bytes 1572872 | tf_op jit(solution)/shard_map/ppermute | solution.py:46
  1533.2 36.0 %collective-permute-done.24 = bf16[1,4,256,256]{3,2,0,1:T(8,128)(2,1)S(1)} collective-permute-done((bf16[1,4,256,256]{3,2,0,1:T(8,128)(2,1)S(1)}, bf16[1,4,256,256]{3,2,0,1:T(8,128)(2,1)S(1)}, u32[]{:S(2)}, u32[]{:S(2)}) %collective-permute-start.24) | collective-permute-done | bytes 524320 | tf_op jit(solution)/shard_map/ppermute | solution.py:46
  1569.2 7.7 collective-permute-done.25
  1577.0 9.4 collective-permute-start.14
  1586.5 49.2 %collective-permute-start.15 = (bf16[1,4,256,512]{3,2,0,1:T(8,128)(2,1)S(1)}, bf16[1,4,256,512]{3,2,0,1:T(8,128)(2,1)S(1)}, u32[]{:S(2)}, u32[]{:S(2)}) collective-permute-start(bf16[1,4,256,512]{3,2,0,1:T(8,128)(2,1)S(1)} %get-tuple-element.93), channel_id=1, source_target_pairs={{0,8},{4,12},{8,16},{12,20},{16,24},{20,28},{24,0},{28,4},{1,9},{5... | collective-permute-start | bytes 3145736 | tf_op jit(solution)/shard_map/ppermute | solution.py:46
  1636.8 4.7 bitcast_convert_fusion.3
  1641.5 33.8 %collective-permute-done.14 = bf16[1,4,256,512]{3,2,0,1:T(8,128)(2,1)S(1)} collective-permute-done((bf16[1,4,256,512]{3,2,0,1:T(8,128)(2,1)S(1)}, bf16[1,4,256,512]{3,2,0,1:T(8,128)(2,1)S(1)}, u32[]{:S(2)}, u32[]{:S(2)}) %collective-permute-start.14) | collective-permute-done | bytes 1048608 | tf_op jit(solution)/shard_map/ppermute | solution.py:46
  1676.3 30.9 %collective-permute-done.15 = bf16[1,4,256,512]{3,2,0,1:T(8,128)(2,1)S(1)} collective-permute-done((bf16[1,4,256,512]{3,2,0,1:T(8,128)(2,1)S(1)}, bf16[1,4,256,512]{3,2,0,1:T(8,128)(2,1)S(1)}, u32[]{:S(2)}, u32[]{:S(2)}) %collective-permute-start.15) | collective-permute-done | bytes 1048608 | tf_op jit(solution)/shard_map/ppermute | solution.py:46
  1707.2 22.3 %collective-permute-start.19 = (bf16[1,4,256,512]{3,2,0,1:T(8,128)(2,1)S(1)}, bf16[1,4,256,512]{3,2,0,1:T(8,128)(2,1)S(1)}, u32[]{:S(2)}, u32[]{:S(2)}) collective-permute-start(bf16[1,4,256,512]{3,2,0,1:T(8,128)(2,1)S(1)} %get-tuple-element.89), channel_id=1, source_target_pairs={{0,24},{4,28},{8,0},{12,4},{16,8},{20,12},{24,16},{28,20},{1,25},{... | collective-permute-start | bytes 3145736 | tf_op jit(solution)/shard_map/ppermute | solution.py:46
  1731.6 19.0 %collective-permute-done.17 = bf16[1,4,256,512]{3,2,0,1:T(8,128)(2,1)S(1)} collective-permute-done((bf16[1,4,256,512]{3,2,0,1:T(8,128)(2,1)S(1)}, bf16[1,4,256,512]{3,2,0,1:T(8,128)(2,1)S(1)}, u32[]{:S(2)}, u32[]{:S(2)}) %collective-permute-start.17) | collective-permute-done | bytes 1048608 | tf_op jit(solution)/shard_map/ppermute | solution.py:46
  1752.7 49.0 %collective-permute-done.19 = bf16[1,4,256,512]{3,2,0,1:T(8,128)(2,1)S(1)} collective-permute-done((bf16[1,4,256,512]{3,2,0,1:T(8,128)(2,1)S(1)}, bf16[1,4,256,512]{3,2,0,1:T(8,128)(2,1)S(1)}, u32[]{:S(2)}, u32[]{:S(2)}) %collective-permute-start.19) | collective-permute-done | bytes 1048608 | tf_op jit(solution)/shard_map/ppermute | solution.py:46
  1803.8 18.3 reshape.363
  1831.4 12.6 psum.39
  (519 shorter events, 234.0 us)
Async XLA Ops:
  8.0 41.1 %all-gather.8.cloned.1.call-start = ((), (), s32[]{:S(2)}) async-start(), calls=%async_computation.6 | async-start | bytes 2621440 | tf_op jit(solution)/shard_map/all_gather | solution.py:102
  8.8 128.2 %all-gather.10.cloned.1.call-start = ((), (), s32[]{:S(2)}) async-start(), calls=%async_computation.7 | async-start | bytes 7077888 | tf_op jit(solution)/shard_map/all_gather | solution.py:87
  9.5 177.3 %all-gather.12.cloned.1.call-start = ((), (), s32[]{:S(2)}) async-start(), calls=%async_computation.8 | async-start | bytes 2359296 | tf_op jit(solution)/shard_map/all_gather | solution.py:88
  10.2 224.9 %reduce-scatter.9.cloned.1.call-start = ((), (), s32[]{:S(2)}) async-start(), calls=%async_computation.9 | async-start | bytes 5242880 | tf_op jit(solution)/shard_map/reduce_scatter | solution.py:128
  46.6 90.4 %copy-start.75 = (f32[1,4,128]{1,0,2:T(1,128)}, f32[1,4,128]{1,0,2:T(1,128)S(1)}, u32[]{:S(2)}) copy-start(f32[1,4,128]{1,0,2:T(1,128)S(1)} %get-tuple-element.146) | copy-start | bytes 6148
  46.6 90.4 %copy-start.77 = (f32[1,4,128]{1,0,2:T(1,128)}, f32[1,4,128]{1,0,2:T(1,128)S(1)}, u32[]{:S(2)}) copy-start(f32[1,4,128]{1,0,2:T(1,128)S(1)} %get-tuple-element.145) | copy-start | bytes 6148
  46.6 112.5 %copy-start.101 = (f32[4,128]{1,0:T(4,128)}, f32[4,128]{1,0:T(4,128)S(1)}, u32[]{:S(2)}) copy-start(f32[4,128]{1,0:T(4,128)S(1)} %copy.332) | copy-start | bytes 6148
  46.7 112.5 %copy-start.103 = (f32[4,128]{1,0:T(4,128)}, f32[4,128]{1,0:T(4,128)S(1)}, u32[]{:S(2)}) copy-start(f32[4,128]{1,0:T(4,128)S(1)} %copy.334) | copy-start | bytes 6148
  48.1 685.8 %copy-start.8 = (bf16[2048,34]{1,0:T(8,128)(2,1)}, bf16[2048,34]{1,0:T(8,128)(2,1)S(1)}, u32[]{:S(2)}) copy-start(bf16[2048,34]{1,0:T(8,128)(2,1)S(1)} %reshape.330) | copy-start | bytes 417796
  48.8 96.1 %copy-start.113 = (f32[2048]{0:T(1024)}, f32[2048]{0:T(1024)S(1)}, u32[]{:S(2)}) copy-start(f32[2048]{0:T(1024)S(1)} %get-tuple-element.77) | copy-start | bytes 24580
  48.8 189.1 %copy-start.95 = (f32[2048]{0:T(1024)}, f32[2048]{0:T(1024)S(1)}, u32[]{:S(2)}) copy-start(f32[2048]{0:T(1024)S(1)} %get-tuple-element.76) | copy-start | bytes 24580
  49.1 112.8 %copy-start.86 = (pred[2,256,256]{1,2,0:T(8,128)(4,1)}, pred[2,256,256]{1,2,0:T(8,128)(4,1)S(1)}, u32[]{:S(2)}) copy-start(pred[2,256,256]{1,2,0:T(8,128)(4,1)S(1)} %and_and_fusion) | copy-start | bytes 393220
  51.9 93.1 %copy-start.118 = (f32[256,2]{0,1:T(2,128)}, f32[256,2]{0,1:T(2,128)S(1)}, u32[]{:S(2)}) copy-start(f32[256,2]{0,1:T(2,128)S(1)} %add_rsqrt_fusion.2) | copy-start | bytes 6148
  191.7 450.6 %all-gather.16.cloned.1.call-start = ((), (), s32[]{:S(2)}) async-start(), calls=%async_computation.12 | async-start | bytes 17301504 | tf_op jit(solution)/shard_map/all_gather | solution.py:139
  193.7 494.3 %all-gather.14.cloned.1.call-start = ((), (), s32[]{:S(2)}) async-start(), calls=%async_computation.10 | async-start | bytes 17301504 | tf_op jit(solution)/shard_map/all_gather | solution.py:136
  240.0 910.7 %reduce-scatter.19.cloned.1.call-start = ((), (), s32[]{:S(2)}) async-start(), calls=%async_computation.17 | async-start | bytes 18382848 | tf_op jit(solution)/shard_map/reduce_scatter | solution.py:203
  245.9 179.9 %collective-permute-start.13 = (bf16[1,4,256,256]{3,2,1,0:T(8,128)(2,1)}, bf16[1,4,256,256]{3,2,1,0:T(8,128)(2,1)S(1)}, u32[]{:S(2)}, u32[]{:S(2)}) collective-permute-start(bf16[1,4,256,256]{3,2,1,0:T(8,128)(2,1)} %get-tuple-element.126), channel_id=1, source_target_pairs={{0,28},{4,0},{8,4},{12,8},{16,12},{20,16},{24,20},{28,24},{1,29},{... | collective-permute-start | bytes 1572872 | tf_op jit(solution)/shard_map/ppermute | solution.py:46
  250.1 212.8 %collective-permute-start.11 = (bf16[1,4,256,256]{3,2,1,0:T(8,128)(2,1)}, bf16[1,4,256,256]{3,2,1,0:T(8,128)(2,1)}, u32[]{:S(2)}, u32[]{:S(2)}) collective-permute-start(bf16[1,4,256,256]{3,2,1,0:T(8,128)(2,1)} %get-tuple-element.128), channel_id=1, source_target_pairs={{0,20},{4,24},{8,28},{12,0},{16,4},{20,8},{24,12},{28,16},{1,21},{... | collective-permute-start | bytes 1572872 | tf_op jit(solution)/shard_map/ppermute | solution.py:46
  250.1 211.0 %collective-permute-start.10 = (bf16[1,4,256,256]{3,2,1,0:T(8,128)(2,1)}, bf16[1,4,256,256]{3,2,1,0:T(8,128)(2,1)}, u32[]{:S(2)}, u32[]{:S(2)}) collective-permute-start(bf16[1,4,256,256]{3,2,1,0:T(8,128)(2,1)} %get-tuple-element.129), channel_id=1, source_target_pairs={{0,16},{4,20},{8,24},{12,28},{16,0},{20,4},{24,8},{28,12},{1,17},{... | collective-permute-start | bytes 1572872 | tf_op jit(solution)/shard_map/ppermute | solution.py:46
  250.3 177.9 %collective-permute-start.9 = (bf16[1,4,256,256]{3,2,1,0:T(8,128)(2,1)}, bf16[1,4,256,256]{3,2,1,0:T(8,128)(2,1)}, u32[]{:S(2)}, u32[]{:S(2)}) collective-permute-start(bf16[1,4,256,256]{3,2,1,0:T(8,128)(2,1)} %get-tuple-element.130), channel_id=1, source_target_pairs={{0,12},{4,16},{8,20},{12,24},{16,28},{20,0},{24,4},{28,8},{1,13},{... | collective-permute-start | bytes 1572872 | tf_op jit(solution)/shard_map/ppermute | solution.py:46
  253.0 175.7 %collective-permute-start.8 = (bf16[1,4,256,256]{3,2,1,0:T(8,128)(2,1)}, bf16[1,4,256,256]{3,2,1,0:T(8,128)(2,1)}, u32[]{:S(2)}, u32[]{:S(2)}) collective-permute-start(bf16[1,4,256,256]{3,2,1,0:T(8,128)(2,1)} %get-tuple-element.131), channel_id=1, source_target_pairs={{0,8},{4,12},{8,16},{12,20},{16,24},{20,28},{24,0},{28,4},{1,9},{5... | collective-permute-start | bytes 1572872 | tf_op jit(solution)/shard_map/ppermute | solution.py:46
  425.8 29.4 %collective-permute-start.7 = (bf16[1,4,256,256]{3,2,1,0:T(8,128)(2,1)}, bf16[1,4,256,256]{3,2,1,0:T(8,128)(2,1)}, u32[]{:S(2)}, u32[]{:S(2)}) collective-permute-start(bf16[1,4,256,256]{3,2,1,0:T(8,128)(2,1)} %get-tuple-element.132), channel_id=1, source_target_pairs={{0,4},{4,8},{8,12},{12,16},{16,20},{20,24},{24,28},{28,0},{1,5},{5... | collective-permute-start | bytes 1572872 | tf_op jit(solution)/shard_map/ppermute | solution.py:46
  428.2 99.2 %collective-permute-start.1 = (bf16[1,4,256,512]{3,2,1,0:T(8,128)(2,1)}, bf16[1,4,256,512]{3,2,1,0:T(8,128)(2,1)}, u32[]{:S(2)}, u32[]{:S(2)}) collective-permute-start(bf16[1,4,256,512]{3,2,1,0:T(8,128)(2,1)} %get-tuple-element.104), channel_id=1, source_target_pairs={{0,8},{4,12},{8,16},{12,20},{16,24},{20,28},{24,0},{28,4},{1,9},{5... | collective-permute-start | bytes 3145736 | tf_op jit(solution)/shard_map/ppermute | solution.py:46
  428.7 98.6 %collective-permute-start = (bf16[1,4,256,512]{3,2,1,0:T(8,128)(2,1)}, bf16[1,4,256,512]{3,2,1,0:T(8,128)(2,1)}, u32[]{:S(2)}, u32[]{:S(2)}) collective-permute-start(bf16[1,4,256,512]{3,2,1,0:T(8,128)(2,1)} %get-tuple-element.105), channel_id=1, source_target_pairs={{0,4},{4,8},{8,12},{12,16},{16,20},{20,24},{24,28},{28,0},{1,5},{5... | collective-permute-start | bytes 3145736 | tf_op jit(solution)/shard_map/ppermute | solution.py:46
  455.2 18.6 %collective-permute-start.12 = (bf16[1,4,256,256]{3,2,1,0:T(8,128)(2,1)}, bf16[1,4,256,256]{3,2,1,0:T(8,128)(2,1)S(1)}, u32[]{:S(2)}, u32[]{:S(2)}) collective-permute-start(bf16[1,4,256,256]{3,2,1,0:T(8,128)(2,1)} %get-tuple-element.127), channel_id=1, source_target_pairs={{0,24},{4,28},{8,0},{12,4},{16,8},{20,12},{24,16},{28,20},{1,25},{... | collective-permute-start | bytes 1572872 | tf_op jit(solution)/shard_map/ppermute | solution.py:46
  455.2 84.6 %slice-start = ((s8[8388608]{0:T(1024)(128)(4,1)}), s8[4194304]{0:T(1024)(128)(4,1)S(1)}, s32[]{:S(2)}) async-start(s8[8388608]{0:T(1024)(128)(4,1)} %bitcast.276), calls=%async_computation.19 | async-start | bytes 8388608
  461.1 156.3 %collective-permute-start.2 = (bf16[1,4,256,512]{3,2,1,0:T(8,128)(2,1)}, bf16[1,4,256,512]{3,2,1,0:T(8,128)(2,1)S(1)}, u32[]{:S(2)}, u32[]{:S(2)}) collective-permute-start(bf16[1,4,256,512]{3,2,1,0:T(8,128)(2,1)} %get-tuple-element.103), channel_id=1, source_target_pairs={{0,12},{4,16},{8,20},{12,24},{16,28},{20,0},{24,4},{28,8},{1,13},{... | collective-permute-start | bytes 3145736 | tf_op jit(solution)/shard_map/ppermute | solution.py:46
  463.0 154.5 %collective-permute-start.3 = (bf16[1,4,256,512]{3,2,1,0:T(8,128)(2,1)}, bf16[1,4,256,512]{3,2,1,0:T(8,128)(2,1)S(1)}, u32[]{:S(2)}, u32[]{:S(2)}) collective-permute-start(bf16[1,4,256,512]{3,2,1,0:T(8,128)(2,1)} %get-tuple-element.102), channel_id=1, source_target_pairs={{0,16},{4,20},{8,24},{12,28},{16,0},{20,4},{24,8},{28,12},{1,17},{... | collective-permute-start | bytes 3145736 | tf_op jit(solution)/shard_map/ppermute | solution.py:46
  473.7 143.9 %collective-permute-start.4 = (bf16[1,4,256,512]{3,2,1,0:T(8,128)(2,1)S(1)}, bf16[1,4,256,512]{3,2,1,0:T(8,128)(2,1)S(1)}, u32[]{:S(2)}, u32[]{:S(2)}) collective-permute-start(bf16[1,4,256,512]{3,2,1,0:T(8,128)(2,1)S(1)} %copy-done.56), channel_id=1, source_target_pairs={{0,20},{4,24},{8,28},{12,0},{16,4},{20,8},{24,12},{28,16},{1,21},{... | collective-permute-start | bytes 3145736 | tf_op jit(solution)/shard_map/ppermute | solution.py:46
  527.3 111.0 %collective-permute-start.6 = (bf16[1,4,256,512]{3,2,1,0:T(8,128)(2,1)S(1)}, bf16[1,4,256,512]{3,2,1,0:T(8,128)(2,1)S(1)}, u32[]{:S(2)}, u32[]{:S(2)}) collective-permute-start(bf16[1,4,256,512]{3,2,1,0:T(8,128)(2,1)S(1)} %copy-done.54), channel_id=1, source_target_pairs={{0,28},{4,0},{8,4},{12,8},{16,12},{20,16},{24,20},{28,24},{1,29},{... | collective-permute-start | bytes 3145736 | tf_op jit(solution)/shard_map/ppermute | solution.py:46
  527.4 110.9 %collective-permute-start.5 = (bf16[1,4,256,512]{3,2,1,0:T(8,128)(2,1)S(1)}, bf16[1,4,256,512]{3,2,1,0:T(8,128)(2,1)S(1)}, u32[]{:S(2)}, u32[]{:S(2)}) collective-permute-start(bf16[1,4,256,512]{3,2,1,0:T(8,128)(2,1)S(1)} %copy-done.55), channel_id=1, source_target_pairs={{0,24},{4,28},{8,0},{12,4},{16,8},{20,12},{24,16},{28,20},{1,25},{... | collective-permute-start | bytes 3145736 | tf_op jit(solution)/shard_map/ppermute | solution.py:46
  806.8 115.8 %copy-start.20 = (bf16[1408,256]{0,1:T(8,128)(2,1)}, bf16[1408,256]{0,1:T(8,128)(2,1)S(1)}, u32[]{:S(2)}) copy-start(bf16[1408,256]{0,1:T(8,128)(2,1)S(1)} %get-tuple-element.138) | copy-start | bytes 2162692
  807.9 110.6 %copy-start.22 = (bf16[1408,256]{0,1:T(8,128)(2,1)}, bf16[1408,256]{0,1:T(8,128)(2,1)S(1)}, u32[]{:S(2)}) copy-start(bf16[1408,256]{0,1:T(8,128)(2,1)S(1)} %get-tuple-element.141) | copy-start | bytes 2162692
  811.6 102.6 %copy-start.24 = (bf16[1408,256]{0,1:T(8,128)(2,1)}, bf16[1408,256]{0,1:T(8,128)(2,1)S(1)}, u32[]{:S(2)}) copy-start(bf16[1408,256]{0,1:T(8,128)(2,1)S(1)} %get-tuple-element.140) | copy-start | bytes 2162692
  814.6 94.1 %copy-start.26 = (bf16[1408,256]{0,1:T(8,128)(2,1)}, bf16[1408,256]{0,1:T(8,128)(2,1)S(1)}, u32[]{:S(2)}) copy-start(bf16[1408,256]{0,1:T(8,128)(2,1)S(1)} %get-tuple-element.139) | copy-start | bytes 2162692
  908.6 273.9 %all-gather.18.cloned.1.call-start = ((), (), s32[]{:S(2)}) async-start(), calls=%async_computation.13 | async-start | bytes 2621440 | tf_op jit(solution)/shard_map/all_gather | solution.py:231
  922.7 229.6 %copy-start.9 = (bf16[2048,34]{1,0:T(8,128)(2,1)S(1)}, bf16[2048,34]{1,0:T(8,128)(2,1)}, u32[]{:S(2)}) copy-start(bf16[2048,34]{1,0:T(8,128)(2,1)} %copy-done.8) | copy-start | bytes 417796
  926.9 227.4 %copy-start.7 = (f32[64,2,2048]{2,0,1:T(8,128)S(1)}, f32[64,2,2048]{2,0,1:T(8,128)}, u32[]{:S(2)}) copy-start(f32[64,2,2048]{2,0,1:T(8,128)} %copy-done.6) | copy-start | bytes 3145732
  926.9 227.4 %copy-start.96 = (f32[2048]{0:T(1024)S(1)}, f32[2048]{0:T(1024)}, u32[]{:S(2)}) copy-start(f32[2048]{0:T(1024)} %copy-done.95) | copy-start | bytes 24580
  926.9 227.4 %copy-start.110 = (f32[64,2]{0,1:T(2,128)S(1)}, f32[64,2]{0,1:T(2,128)}, u32[]{:S(2)}) copy-start(f32[64,2]{0,1:T(2,128)} %copy-done.109) | copy-start | bytes 1540
  926.9 227.5 %copy-start.117 = (f32[64,2]{0,1:T(2,128)S(1)}, f32[64,2]{0,1:T(2,128)}, u32[]{:S(2)}) copy-start(f32[64,2]{0,1:T(2,128)} %get-tuple-element.157) | copy-start | bytes 1540
  1158.5 204.5 %reduce-scatter.11.cloned.1.call-start = ((), (), s32[]{:S(2)}) async-start(), calls=%async_computation.11 | async-start | bytes 17301504 | tf_op jit(solution)/shard_map/reduce_scatter | solution.py:204
  1178.8 220.0 %reduce-scatter.13.cloned.1.call-start = ((), (), s32[]{:S(2)}) async-start(), calls=%async_computation.14 | async-start | bytes 2621440 | tf_op jit(solution)/shard_map/reduce_scatter | solution.py:265
  1223.0 602.5 %reduce-scatter.17.cloned.1.call-start = ((), (), s32[]{:S(2)}) async-start(), calls=%async_computation.16 | async-start | bytes 2359296 | tf_op jit(solution)/shard_map/reduce_scatter | solution.py:278
  1227.3 138.3 %copy-start.17 = (bf16[128,2048]{1,0:T(8,128)(2,1)S(1)}, bf16[128,2048]{1,0:T(8,128)(2,1)}, u32[]{:S(2)}) copy-start(bf16[128,2048]{1,0:T(8,128)(2,1)} %reshape.332) | copy-start | bytes 1572868
  1227.3 139.3 %copy-start.12 = (f32[64,2,2048]{2,1,0:T(2,128)S(1)}, f32[64,2,2048]{2,1,0:T(2,128)}, u32[]{:S(2)}) copy-start(f32[64,2,2048]{2,1,0:T(2,128)} %copy-done.11) | copy-start | bytes 3145732
  1227.3 600.0 %all-reduce.5.cloned.1.call-start = ((), (), s32[]{:S(2)}) async-start(), calls=%async_computation.18 | async-start | bytes 565248
  1227.4 171.4 %copy-start.19 = (bf16[64,2,2048]{2,1,0:T(2,128)(2,1)S(1)}, bf16[64,2,2048]{2,1,0:T(2,128)(2,1)}, u32[]{:S(2)}) copy-start(bf16[64,2,2048]{2,1,0:T(2,128)(2,1)} %param.12) | copy-start | bytes 1572868
  1401.8 443.7 %reduce-scatter.15.cloned.1.call-start = ((), (), s32[]{:S(2)}) async-start(), calls=%async_computation.15 | async-start | bytes 7077888 | tf_op jit(solution)/shard_map/reduce_scatter | solution.py:275
  1425.8 160.7 %collective-permute-start.27 = (bf16[1,4,256,256]{3,2,0,1:T(8,128)(2,1)S(1)}, bf16[1,4,256,256]{3,2,0,1:T(8,128)(2,1)}, u32[]{:S(2)}, u32[]{:S(2)}) collective-permute-start(bf16[1,4,256,256]{3,2,0,1:T(8,128)(2,1)S(1)} %get-tuple-element.115), channel_id=1, source_target_pairs={{0,28},{4,0},{8,4},{12,8},{16,12},{20,16},{24,20},{28,24},{1,29},{... | collective-permute-start | bytes 1572872 | tf_op jit(solution)/shard_map/ppermute | solution.py:46
  1430.0 99.8 %collective-permute-start.23 = (bf16[1,4,256,256]{3,2,0,1:T(8,128)(2,1)}, bf16[1,4,256,256]{3,2,0,1:T(8,128)(2,1)}, u32[]{:S(2)}, u32[]{:S(2)}) collective-permute-start(bf16[1,4,256,256]{3,2,0,1:T(8,128)(2,1)} %get-tuple-element.119), channel_id=1, source_target_pairs={{0,12},{4,16},{8,20},{12,24},{16,28},{20,0},{24,4},{28,8},{1,13},{... | collective-permute-start | bytes 1572872 | tf_op jit(solution)/shard_map/ppermute | solution.py:46
  1430.0 98.5 %collective-permute-start.22 = (bf16[1,4,256,256]{3,2,0,1:T(8,128)(2,1)}, bf16[1,4,256,256]{3,2,0,1:T(8,128)(2,1)}, u32[]{:S(2)}, u32[]{:S(2)}) collective-permute-start(bf16[1,4,256,256]{3,2,0,1:T(8,128)(2,1)} %get-tuple-element.120), channel_id=1, source_target_pairs={{0,8},{4,12},{8,16},{12,20},{16,24},{20,28},{24,0},{28,4},{1,9},{5... | collective-permute-start | bytes 1572872 | tf_op jit(solution)/shard_map/ppermute | solution.py:46
  1430.2 40.2 %collective-permute-start.21 = (bf16[1,4,256,256]{3,2,0,1:T(8,128)(2,1)}, bf16[1,4,256,256]{3,2,0,1:T(8,128)(2,1)}, u32[]{:S(2)}, u32[]{:S(2)}) collective-permute-start(bf16[1,4,256,256]{3,2,0,1:T(8,128)(2,1)} %get-tuple-element.121), channel_id=1, source_target_pairs={{0,4},{4,8},{8,12},{12,16},{16,20},{20,24},{24,28},{28,0},{1,5},{5... | collective-permute-start | bytes 1572872 | tf_op jit(solution)/shard_map/ppermute | solution.py:46
  1457.4 71.2 %copy-start.79 = (bf16[1,4,256,256]{3,2,0,1:T(8,128)(2,1)S(1)}, bf16[1,4,256,256]{3,2,0,1:T(8,128)(2,1)}, u32[]{:S(2)}) copy-start(bf16[1,4,256,256]{3,2,0,1:T(8,128)(2,1)} %get-tuple-element.117) | copy-start | bytes 1572868
  1457.9 128.5 %collective-permute-start.26 = (bf16[1,4,256,256]{3,2,0,1:T(8,128)(2,1)S(1)}, bf16[1,4,256,256]{3,2,0,1:T(8,128)(2,1)S(1)}, u32[]{:S(2)}, u32[]{:S(2)}) collective-permute-start(bf16[1,4,256,256]{3,2,0,1:T(8,128)(2,1)S(1)} %get-tuple-element.116), channel_id=1, source_target_pairs={{0,24},{4,28},{8,0},{12,4},{16,8},{20,12},{24,16},{28,20},{1,25},{... | collective-permute-start | bytes 1572872 | tf_op jit(solution)/shard_map/ppermute | solution.py:46
  1470.4 98.8 %collective-permute-start.24 = (bf16[1,4,256,256]{3,2,0,1:T(8,128)(2,1)S(1)}, bf16[1,4,256,256]{3,2,0,1:T(8,128)(2,1)S(1)}, u32[]{:S(2)}, u32[]{:S(2)}) collective-permute-start(bf16[1,4,256,256]{3,2,0,1:T(8,128)(2,1)S(1)} %copy-done.84), channel_id=1, source_target_pairs={{0,16},{4,20},{8,24},{12,28},{16,0},{20,4},{24,8},{28,12},{1,17},{... | collective-permute-start | bytes 1572872 | tf_op jit(solution)/shard_map/ppermute | solution.py:46
  1528.6 48.4 %collective-permute-start.25 = (bf16[1,4,256,256]{3,2,0,1:T(8,128)(2,1)S(1)}, bf16[1,4,256,256]{3,2,0,1:T(8,128)(2,1)S(1)}, u32[]{:S(2)}, u32[]{:S(2)}) collective-permute-start(bf16[1,4,256,256]{3,2,0,1:T(8,128)(2,1)S(1)} %copy-done.79), channel_id=1, source_target_pairs={{0,20},{4,24},{8,28},{12,0},{16,4},{20,8},{24,12},{28,16},{1,21},{... | collective-permute-start | bytes 1572872 | tf_op jit(solution)/shard_map/ppermute | solution.py:46
  1529.9 272.8 %collective-permute-start.20 = (bf16[1,4,256,512]{3,2,0,1:T(8,128)(2,1)S(1)}, bf16[1,4,256,512]{3,2,0,1:T(8,128)(2,1)S(1)}, u32[]{:S(2)}, u32[]{:S(2)}) collective-permute-start(bf16[1,4,256,512]{3,2,0,1:T(8,128)(2,1)S(1)} %get-tuple-element.88), channel_id=1, source_target_pairs={{0,28},{4,0},{8,4},{12,8},{16,12},{20,16},{24,20},{28,24},{1,29},{... | collective-permute-start | bytes 3145736 | tf_op jit(solution)/shard_map/ppermute | solution.py:46
  1569.2 181.4 %collective-permute-start.17 = (bf16[1,4,256,512]{3,2,0,1:T(8,128)(2,1)S(1)}, bf16[1,4,256,512]{3,2,0,1:T(8,128)(2,1)S(1)}, u32[]{:S(2)}, u32[]{:S(2)}) collective-permute-start(bf16[1,4,256,512]{3,2,0,1:T(8,128)(2,1)S(1)} %get-tuple-element.91), channel_id=1, source_target_pairs={{0,16},{4,20},{8,24},{12,28},{16,0},{20,4},{24,8},{28,12},{1,17},{... | collective-permute-start | bytes 3145736 | tf_op jit(solution)/shard_map/ppermute | solution.py:46
  1577.0 98.3 %collective-permute-start.14 = (bf16[1,4,256,512]{3,2,0,1:T(8,128)(2,1)S(1)}, bf16[1,4,256,512]{3,2,0,1:T(8,128)(2,1)S(1)}, u32[]{:S(2)}, u32[]{:S(2)}) collective-permute-start(bf16[1,4,256,512]{3,2,0,1:T(8,128)(2,1)S(1)} %get-tuple-element.94), channel_id=1, source_target_pairs={{0,4},{4,8},{8,12},{12,16},{16,20},{20,24},{24,28},{28,0},{1,5},{5... | collective-permute-start | bytes 3145736 | tf_op jit(solution)/shard_map/ppermute | solution.py:46
  1586.4 144.2 %collective-permute-start.16 = (bf16[1,4,256,512]{3,2,0,1:T(8,128)(2,1)S(1)}, bf16[1,4,256,512]{3,2,0,1:T(8,128)(2,1)S(1)}, u32[]{:S(2)}, u32[]{:S(2)}) collective-permute-start(bf16[1,4,256,512]{3,2,0,1:T(8,128)(2,1)S(1)} %get-tuple-element.92), channel_id=1, source_target_pairs={{0,12},{4,16},{8,20},{12,24},{16,28},{20,0},{24,4},{28,8},{1,13},{... | collective-permute-start | bytes 3145736 | tf_op jit(solution)/shard_map/ppermute | solution.py:46
  1586.5 120.7 %collective-permute-start.15 = (bf16[1,4,256,512]{3,2,0,1:T(8,128)(2,1)S(1)}, bf16[1,4,256,512]{3,2,0,1:T(8,128)(2,1)S(1)}, u32[]{:S(2)}, u32[]{:S(2)}) collective-permute-start(bf16[1,4,256,512]{3,2,0,1:T(8,128)(2,1)S(1)} %get-tuple-element.93), channel_id=1, source_target_pairs={{0,8},{4,12},{8,16},{12,20},{16,24},{20,28},{24,0},{28,4},{1,9},{5... | collective-permute-start | bytes 3145736 | tf_op jit(solution)/shard_map/ppermute | solution.py:46
  1675.3 76.3 %collective-permute-start.18 = (bf16[1,4,256,512]{3,2,0,1:T(8,128)(2,1)S(1)}, bf16[1,4,256,512]{3,2,0,1:T(8,128)(2,1)S(1)}, u32[]{:S(2)}, u32[]{:S(2)}) collective-permute-start(bf16[1,4,256,512]{3,2,0,1:T(8,128)(2,1)S(1)} %get-tuple-element.90), channel_id=1, source_target_pairs={{0,20},{4,24},{8,28},{12,0},{16,4},{20,8},{24,12},{28,16},{1,21},{... | collective-permute-start | bytes 3145736 | tf_op jit(solution)/shard_map/ppermute | solution.py:46
  1707.2 94.5 %collective-permute-start.19 = (bf16[1,4,256,512]{3,2,0,1:T(8,128)(2,1)S(1)}, bf16[1,4,256,512]{3,2,0,1:T(8,128)(2,1)S(1)}, u32[]{:S(2)}, u32[]{:S(2)}) collective-permute-start(bf16[1,4,256,512]{3,2,0,1:T(8,128)(2,1)S(1)} %get-tuple-element.89), channel_id=1, source_target_pairs={{0,24},{4,28},{8,0},{12,4},{16,8},{20,12},{24,16},{28,20},{1,25},{... | collective-permute-start | bytes 3145736 | tf_op jit(solution)/shard_map/ppermute | solution.py:46
  (116 other events, 1099.9 us)
Sparse Core Ops, SparseCore 0:
  10.4 25.2 all-gather.7
  37.9 99.0 all-gather.9
  139.1 47.6 all-gather.11
  191.8 43.2 reduce-scatter.8
  1158.6 23.7 all-gather.17
  1401.9 121.1 all-reduce.4
Sparse Core Ops, SparseCore 1:
  196.0 188.6 all-gather.15
  388.5 248.3 all-gather.13
  908.7 242.0 reduce-scatter.18
  1178.9 184.0 reduce-scatter.10
  1365.7 33.0 reduce-scatter.12
  1402.7 112.0 reduce-scatter.16
  1518.7 302.7 reduce-scatter.14

commit v2 on v1

v2 whole, which is shorter than its diff:
```python
import functools
import itertools

import jax
import jax.numpy as jnp
from jax import lax
from jax.experimental import pallas as pl
from jax.experimental.pallas import tpu as pltpu
from jax.sharding import PartitionSpec as P

WINDOW = 128
CAP = 176
EPSILON = 1e-05
MASKED = -1e30

MESH = pl.DeviceIdType.MESH
F32 = jnp.float32
BF16 = jnp.bfloat16


def norm_factor(values):
    return lax.rsqrt(jnp.mean(values * values, axis=-1, keepdims=True) + EPSILON)


def norm_back(values, factor, gain_row, upstream):
    features = values.shape[-1]
    inner = jnp.sum(values * gain_row * upstream, axis=-1, keepdims=True)
    return factor * gain_row * upstream - values * factor**3 * inner / features


def softmax_rows(logits):
    highest = jnp.max(logits, axis=-1, keepdims=True)
    raised = jnp.exp(logits - highest)
    return raised / jnp.sum(raised, axis=-1, keepdims=True)


def dot(spec, left, right):
    return jnp.einsum(spec, left, right, preferred_element_type=F32)


def mesh_places(ranks):
    rank = lax.axis_index("dp")
    quarter = lax.axis_index("tensor")
    return rank // 2, {
        "inner": lax.rem(rank, 2),
        "side": quarter // 2,
        "core": lax.rem(quarter, 2),
    }


def device_at(ranks, steps, flips):
    outer, pairs = mesh_places(ranks)
    place = {name: 1 - at if name in flips else at for name, at in pairs.items()}
    return (outer + steps) * 2 + place["inner"], place["side"] * 2 + place["core"]


def run_if(conditions, action):
    conditions = [condition for condition in conditions if condition is not None]
    if not conditions:
        action()
        return
    pl.when(functools.reduce(jnp.logical_and, conditions))(action)


def on_chain(ranks, steps):
    outer, _ = mesh_places(ranks)
    if steps == 0:
        return None
    return outer + steps < ranks // 2 if steps > 0 else outer + steps >= 0


def greet(ranks, pieces):
    barrier = pltpu.get_barrier_semaphore()
    pairs = sorted({name for piece in pieces for name in piece[4]})
    targets = [(None, 0, (name,)) for name in pairs]
    if any(piece[3] for piece in pieces):
        targets += [(on_chain(ranks, steps), steps, ()) for steps in (-1, 1)]

    def signal(steps, flips):
        target = device_at(ranks, steps, flips)
        pl.semaphore_signal(barrier, inc=1, device_id=target, device_id_type=MESH)

    expected = len(pairs)
    for condition, steps, flips in targets:
        run_if([condition], functools.partial(signal, steps, flips))
        if condition is not None:
            expected = expected + condition.astype(jnp.int32)
    pl.semaphore_wait(barrier, expected)


def chain_steps(ranks, outer):
    count = ranks // 2
    return [0] + [sign * k for k in range(1, count) for sign in (-1, 1)] if outer else [0]


def row_start(ranks, piece, steps, flips, rows):
    rank, quarter = device_at(ranks, steps, flips)
    if not piece[3]:
        index = quarter
    elif "side" not in piece[4]:
        index = rank
    else:
        index = rank * 4 + quarter
    return pl.ds(pl.multiple_of(index * rows, rows), rows)


def all_bits(dims):
    return list(itertools.product((0, 1), repeat=len(dims)))


def level_of(bits):
    return max((n + 1 for n, bit in enumerate(bits) if bit), default=0)


def gather_kernel(ranks, arrays, pieces, *refs):
    in_refs, out_refs = refs[:arrays], refs[arrays : 2 * arrays]
    send_sem, recv_sem, local_sem = refs[2 * arrays :]
    count = ranks // 2
    greet(ranks, pieces)
    started = []

    def flips_of(p, bits):
        return tuple(name for name, bit in zip(pieces[p][4], bits) if bit)

    def copy(p, steps, bits, as_seen, target_steps, target_flips):
        array, start, width, _, dims = pieces[p]
        rows = in_refs[array].shape[0]
        columns = pl.ds(start, width)
        place = out_refs[array].at[
            row_start(ranks, pieces[p], steps, flips_of(p, bits), rows), columns
        ]
        own = steps == 0 and not any(bits)
        seen_steps, seen_bits = as_seen
        sem = (seen_steps + count - 1) * 2 ** len(dims) + all_bits(dims).index(seen_bits)
        return pltpu.make_async_remote_copy(
            src_ref=in_refs[array].at[:, columns] if own else place,
            dst_ref=place,
            send_sem=send_sem.at[p, sem],
            recv_sem=recv_sem.at[p, sem],
            device_id=device_at(ranks, target_steps, target_flips),
            device_id_type=MESH,
        )

    def send(conditions, *description):
        run_if(conditions, lambda: copy(*description).start())
        started.append((conditions, description))

    def forward(p, steps, bits):
        outer, dims = pieces[p][3:]
        here = on_chain(ranks, steps)
        level = level_of(bits)
        if outer and level == 0:
            for direction in (-1, 1):
                if steps * direction <= 0 and abs(steps) < count - 1:
                    there = on_chain(ranks, direction)
                    seen = (steps - direction, bits)
                    send([here, there], p, steps, bits, seen, direction, ())
        for n in range(level, len(dims)):
            seen = (steps, bits[:n] + (1,) + bits[n + 1 :])
            send([here], p, steps, bits, seen, 0, (dims[n],))

    def receive(p, steps, bits):
        here = on_chain(ranks, steps)
        run_if([here], lambda: copy(p, steps, bits, (steps, bits), 0, (pieces[p][4][0],)).wait_recv())
        forward(p, steps, bits)

    kept = []
    for array in range(arrays):
        piece = next(piece for piece in pieces if piece[0] == array)
        rows = in_refs[array].shape[0]
        keep = pltpu.make_async_copy(
            in_refs[array],
            out_refs[array].at[row_start(ranks, piece, 0, (), rows)],
            local_sem.at[array],
        )
        keep.start()
        kept.append(keep)
    events = []
    for p, (_, _, _, outer, dims) in enumerate(pieces):
        for n, steps in enumerate(chain_steps(ranks, outer)):
            for bits in all_bits(dims):
                level = level_of(bits)
                turn = len(dims) + 1 if level == len(dims) else max(level - 1, 0)
                events.append((turn, abs(steps), n, level, p, steps, bits))
    for event in sorted(event for event in events if event[1] == 0 and event[3] == 0):
        forward(*event[4:])
    for event in sorted(event for event in events if event[1] or event[3]):
        receive(*event[4:])
    for conditions, description in started:
        run_if(conditions, lambda: copy(*description).wait_send())
    for keep in kept:
        keep.wait()


def gather_blocks(blocks, results, pieces, ranks, collective_id):
    arrays = len(blocks)
    transfers = (ranks - 1) * 8
    return pl.pallas_call(
        functools.partial(gather_kernel, ranks, arrays, pieces),
        out_shape=tuple(
            jax.ShapeDtypeStruct((number * block.shape[0], block.shape[1]), block.dtype)
            for block, number in zip(blocks, results)
        ),
        in_specs=[pl.BlockSpec(memory_space=pl.ANY)] * arrays,
        out_specs=(pl.BlockSpec(memory_space=pl.ANY),) * arrays,
        scratch_shapes=[
            pltpu.SemaphoreType.DMA((len(pieces), transfers)),
            pltpu.SemaphoreType.DMA((len(pieces), transfers)),
            pltpu.SemaphoreType.DMA((arrays,)),
        ],
        compiler_params=pltpu.CompilerParams(collective_id=collective_id, has_side_effects=True),
        cost_estimate=pl.CostEstimate(
            flops=0,
            bytes_accessed=sum(2 * n * block.size for block, n in zip(blocks, results)),
            transcendentals=0,
        ),
    )(*blocks)


def gather_everywhere(block, ranks, collective_id):
    half = block.shape[1] // 2
    pieces = (
        (0, 0, half, True, ("inner", "side", "core")),
        (0, half, half, True, ("side", "inner", "core")),
    )
    return gather_blocks([block], [4 * ranks], pieces, ranks, collective_id)[0]


def scatter_kernel(ranks, pieces, in_ref, out_ref, *scratch):
    buffers, (send_sem, recv_sem, load_sem) = scratch[:-3], scratch[-3:]
    rows = out_ref.shape[0]
    count = ranks // 2
    tile = min(rows, 32)
    greet(ranks, pieces)
    outer_place, _ = mesh_places(ranks)
    started = []
    held = []
    for _, _, _, _, dims in pieces:
        depth = len(dims)
        own, *paired = buffers[: depth + 1]
        up, down = buffers[depth + 1 : depth + 3]
        held.append((own, paired, up, down))
        buffers = buffers[depth + 3 :]

    def region(p, steps, bits):
        _, start, width, _, dims = pieces[p]
        flips = tuple(name for name, bit in zip(dims, bits) if bit)
        return in_ref.at[row_start(ranks, pieces[p], steps, flips, rows), pl.ds(start, width)]

    def slot(steps, bits):
        place = outer_place + steps if pieces[0][3] else 0
        number = 0
        for bit in bits:
            number = 2 * number + bit
        return place * 2 ** len(bits) + number

    def sem_of(steps, bits, kind):
        code = 0
        for bit in bits:
            code = 2 * code + bit
        return ((steps + count - 1) * 2 ** len(bits) + code) * 2 + kind

    def own_at(p, steps, bits):
        return held[p][0].at[slot(steps, bits)]

    def load(p, steps, bits):
        return pltpu.make_async_copy(
            region(p, steps, bits + (0,)),
            own_at(p, steps, bits),
            load_sem.at[p, sem_of(steps, bits, 0) // 2],
        )

    def pair_copy(p, steps, bits, n):
        dims = pieces[p][4]
        whole = bits[:n] + (1,) + (0,) * (len(dims) - n - 1)
        last = n == len(dims) - 1
        return pltpu.make_async_remote_copy(
            src_ref=region(p, steps, whole) if last else own_at(p, steps, whole[:-1]),
            dst_ref=held[p][1][n].at[slot(steps, bits[:n])],
            send_sem=send_sem.at[p, sem_of(steps, whole, 0)],
            recv_sem=recv_sem.at[p, sem_of(steps, whole, 0)],
            device_id=device_at(ranks, 0, (dims[n],)),
            device_id_type=MESH,
        )

    def chain_copy(p, steps, direction):
        zeros = (0,) * (len(pieces[p][4]) - 1)
        sem = sem_of(steps - direction, zeros + (0,), 1)
        return pltpu.make_async_remote_copy(
            src_ref=own_at(p, steps, zeros),
            dst_ref=held[p][2 if direction > 0 else 3].at[slot(steps, ())],
            send_sem=send_sem.at[p, sem + (0 if direction > 0 else 2)],
            recv_sem=recv_sem.at[p, sem + (0 if direction > 0 else 2)],
            device_id=device_at(ranks, direction, ()),
            device_id_type=MESH,
        )

    def chain_arrival(p, steps, direction):
        zeros = (0,) * (len(pieces[p][4]) - 1)
        sem = sem_of(steps, zeros + (0,), 1) + (0 if direction > 0 else 2)
        place = held[p][2 if direction > 0 else 3].at[slot(steps, ())]
        return pltpu.make_async_remote_copy(
            src_ref=place,
            dst_ref=place,
            send_sem=send_sem.at[p, sem],
            recv_sem=recv_sem.at[p, sem],
            device_id=device_at(ranks, -direction, ()),
            device_id_type=MESH,
        )

    def add(target, sources):
        def step(n, carry):
            part = pl.ds(pl.multiple_of(n * tile, tile), tile)
            total = sources[0][part].astype(F32)
            for source in sources[1:]:
                total = total + source[part].astype(F32)
            target[part] = total.astype(target.dtype)
            return carry

        lax.fori_loop(0, rows // tile, step, 0)

    order = []
    for p, (_, _, _, outer, dims) in enumerate(pieces):
        for n, steps in enumerate(chain_steps(ranks, outer)):
            for bits in all_bits(dims[:-1]):
                order.append((-level_of(bits), -abs(steps), n, p, steps, bits))
    order = [entry[3:] for entry in sorted(order)]
    for p, steps, bits in order:
        here = on_chain(ranks, steps)
        last = len(pieces[p][4]) - 1

        def begin(p=p, steps=steps, bits=bits, last=last):
            pair_copy(p, steps, bits, last).start()
            load(p, steps, bits).start()

        run_if([here], begin)
        started.append(([here], functools.partial(pair_copy, p, steps, bits, last)))
    for p, steps, bits in order:
        here = on_chain(ranks, steps)
        dims = pieces[p][4]
        level = level_of(bits)
        own, paired, up, down = held[p]

        def gather_terms(p=p, steps=steps, bits=bits, level=level, dims=dims, paired=paired):
            load(p, steps, bits).wait()
            sources = [own_at(p, steps, bits)]
            for n in range(len(dims) - 1, level - 1, -1):
                pair_copy(p, steps, bits, n).wait_recv()
                sources.append(paired[n].at[slot(steps, bits[:n])])
            add(own_at(p, steps, bits), sources)

        run_if([here], gather_terms)
        if level:

            def send_pair(p=p, steps=steps, bits=bits, level=level):
                return pair_copy(p, steps, bits, level - 1)

            run_if([here], lambda: send_pair().start())
            started.append(([here], send_pair))
            continue
        if pieces[p][3]:
            for direction in (1, -1):
                if steps * direction < 0 or abs(steps) == count - 1:
                    continue
                behind = on_chain(ranks, -direction)

                def take(p=p, steps=steps, bits=bits, direction=direction):
                    chain_arrival(p, steps, direction).wait_recv()
                    arrived = held[p][2 if direction > 0 else 3].at[slot(steps, ())]
                    add(own_at(p, steps, bits), [own_at(p, steps, bits), arrived])

                run_if([here, behind], take)
        if steps:
            direction = 1 if steps > 0 else -1

            def send_chain(p=p, steps=steps, direction=direction):
                return chain_copy(p, steps, direction)

            run_if([here], lambda: send_chain().start())
            started.append(([here], send_chain))
        else:
            start, width = pieces[p][1:3]
            begin_column = start - pieces[0][1]
            add(out_ref.at[:, pl.ds(begin_column, width)], [own_at(p, 0, bits)])
    for conditions, build in started:
        run_if(conditions, lambda: build().wait_send())


def scatter_blocks(array, pieces, blocks, ranks, collective_id):
    rows = array.shape[0] // blocks
    columns = sum(piece[2] for piece in pieces)
    count = ranks // 2
    scratch = []
    for _, _, width, outer, dims in pieces:
        chain = count if outer else 1
        sizes = [chain * 2 ** (len(dims) - 1)]
        sizes += [chain * 2**n for n in range(len(dims))]
        sizes += [chain, chain] if outer else [1, 1]
        scratch += [pltpu.VMEM((size, rows, width), array.dtype) for size in sizes]
    transfers = ranks * 8 * 2
    return pl.pallas_call(
        functools.partial(scatter_kernel, ranks, pieces),
        out_shape=jax.ShapeDtypeStruct((rows, columns), array.dtype),
        in_specs=[pl.BlockSpec(memory_space=pl.ANY)],
        out_specs=pl.BlockSpec(memory_space=pltpu.VMEM),
        scratch_shapes=[
            *scratch,
            pltpu.SemaphoreType.DMA((len(pieces), transfers)),
            pltpu.SemaphoreType.DMA((len(pieces), transfers)),
            pltpu.SemaphoreType.DMA((len(pieces), transfers)),
        ],
        compiler_params=pltpu.CompilerParams(
            collective_id=collective_id,
            has_side_effects=True,
            vmem_limit_bytes=56 * 1024 * 1024,
        ),
        cost_estimate=pl.CostEstimate(
            flops=array.shape[0] * columns,
            bytes_accessed=2 * array.shape[0] * columns,
            transcendentals=0,
        ),
    )(array)


def scatter_everywhere(array, ranks, collective_id):
    tiles = array.shape[1] // 128
    calls = max(1, ranks // 8)
    results = []
    for call in range(calls):
        first, last = tiles * call // calls, tiles * (call + 1) // calls
        middle = (first + last + 1) // 2
        pieces = (
            (0, first * 128, (middle - first) * 128, True, ("inner", "side", "core")),
            (0, middle * 128, (last - middle) * 128, True, ("side", "inner", "core")),
        )
        results.append(scatter_blocks(array, pieces, 4 * ranks, ranks, collective_id + call))
    return results[0] if calls == 1 else jnp.concatenate(results, axis=1)


def send_blocks(blocks, ranks):
    own = lax.axis_index("dp")
    received = []
    for shift in range(1, ranks):
        target = lax.rem(own + shift, ranks)
        origin = lax.rem(own + ranks - shift, ranks)
        block = lax.dynamic_index_in_dim(blocks, target, 0, keepdims=True)
        moved = lax.ppermute(block, "dp", [(j, (j + shift) % ranks) for j in range(ranks)])
        received.append((origin, moved))
    return received


def join_blocks(blocks, received):
    for origin, block in received:
        blocks = lax.dynamic_update_slice_in_dim(blocks, block, origin, 0)
    return blocks


def tie(value, received, first, last):
    blocks = [block for _, block in received[first:last]]
    if not blocks:
        return value, received
    value, blocks = lax.optimization_barrier((value, blocks))
    renewed = [(origin, block) for (origin, _), block in zip(received[first:last], blocks)]
    return value, received[:first] + renewed + received[last:]


def expert_kernel(
    owned,
    width,
    rows_ref,
    pull_ref,
    position_ref,
    gate_ref,
    column_ref,
    weight_ref,
    mixture_ref,
    returned_ref,
    chosen_ref,
    pulled_ref,
    d_gate_up_ref,
    hidden_ref,
    place_ref,
    mixed_ref,
    back_ref,
):
    group_tokens, features = rows_ref.shape
    chunk = min(features, 512)
    slot = lax.broadcasted_iota(jnp.int32, (CAP, group_tokens), 0)
    last = (((1,), (1,)), ((), ()))
    first = (((0,), (0,)), ((), ()))
    for e in range(owned):
        place_ref[e * CAP : (e + 1) * CAP] = (position_ref[0, e : e + 1] == slot).astype(BF16)
    for start in range(0, features, chunk):
        columns = slice(start, start + chunk)
        chosen = jnp.dot(place_ref[...], rows_ref[:, columns], preferred_element_type=F32)
        chosen_ref[:, 0, :, columns] = chosen.astype(BF16).reshape(owned, CAP, chunk)
        pulled = jnp.dot(place_ref[...], pull_ref[:, columns], preferred_element_type=F32)
        pulled_ref[:, 0, :, columns] = pulled.astype(BF16).reshape(owned, CAP, chunk)
    spread = jnp.zeros((group_tokens, 128), F32)
    for e in range(owned):
        weight_in = weight_ref[:, e, :, : 2 * width].reshape(features, 2 * width)
        weight_out = weight_ref[:, e, :, 2 * width :].reshape(features, width)
        here = position_ref[0, e : e + 1] == slot
        gate = jnp.sum(jnp.where(here, gate_ref[0, e : e + 1], 0.0), axis=1, keepdims=True)
        gate_up = jnp.dot(chosen_ref[e, 0], weight_in, preferred_element_type=F32)
        d_plain = jnp.dot(pulled_ref[e, 0], weight_out, preferred_element_type=F32)
        gate_part = gate_up[:, :width]
        up_part = gate_up[:, width:]
        sigmoid_gate = jax.nn.sigmoid(gate_part)
        activated = gate_part * sigmoid_gate
        hidden = activated * up_part
        slot_dots = jnp.sum(hidden * d_plain, axis=1, keepdims=True)
        spread = spread + lax.dot_general(
            place_ref[e * CAP : (e + 1) * CAP],
            (slot_dots * column_ref[e : e + 1]).astype(BF16),
            first,
            preferred_element_type=F32,
        )
        d_hidden = d_plain * gate
        d_gate_part = d_hidden * up_part * sigmoid_gate * (1.0 + gate_part * (1.0 - sigmoid_gate))
        d_up_part = d_hidden * activated
        hidden_ref[e, 0] = (hidden * gate).astype(BF16)
        d_gate_up_ref[e, 0, :, :width] = d_gate_part.astype(BF16)
        d_gate_up_ref[e, 0, :, width:] = d_up_part.astype(BF16)
        mixed_ref[e * CAP : (e + 1) * CAP] = lax.dot_general(
            hidden_ref[e, 0], weight_out, last, preferred_element_type=F32
        ).astype(BF16)
        back_ref[e * CAP : (e + 1) * CAP] = lax.dot_general(
            d_gate_up_ref[e, 0], weight_in, last, preferred_element_type=F32
        ).astype(BF16)
    returned_ref[:, features:] = spread.astype(BF16)
    for start in range(0, features, chunk):
        columns = slice(start, start + chunk)
        mixture_ref[:, columns] = lax.dot_general(
            place_ref[...], mixed_ref[:, columns], first, preferred_element_type=F32
        ).astype(BF16)
        returned_ref[:, columns] = lax.dot_general(
            place_ref[...], back_ref[:, columns], first, preferred_element_type=F32
        ).astype(BF16)


def expert_math(rows, pull, position, gate, column, weights):
    groups, owned, group_tokens = position.shape
    tokens, features = rows.shape
    ranks, _, depth, _ = weights.shape
    width = weights.shape[3] // 3
    slots = owned * CAP
    by_rows = pl.BlockSpec((group_tokens, features), lambda g: (g, 0))
    by_group = pl.BlockSpec((1, owned, group_tokens), lambda g: (g, 0, 0))

    def by_slots(columns):
        return pl.BlockSpec((owned, 1, CAP, columns), lambda g: (0, g, 0, 0))

    def slot_array(columns):
        return jax.ShapeDtypeStruct((owned, groups, CAP, columns), BF16)

    flops = 2 * groups * slots * features * (4 * group_tokens + 6 * width)
    return pl.pallas_call(
        functools.partial(expert_kernel, owned, width),
        grid=(groups,),
        out_shape=(
            jax.ShapeDtypeStruct((tokens, features), BF16),
            jax.ShapeDtypeStruct((tokens, features + 128), BF16),
            slot_array(features),
            slot_array(features),
            slot_array(2 * width),
            slot_array(width),
        ),
        in_specs=[
            by_rows,
            by_rows,
            by_group,
            by_group,
            pl.BlockSpec((owned, 128), lambda g: (0, 0)),
            pl.BlockSpec(
                (ranks, owned, depth, 3 * width),
                lambda g: (0, 0, 0, 0),
                pipeline_mode=pl.Buffered(1),
            ),
        ],
        out_specs=(
            by_rows,
            pl.BlockSpec((group_tokens, features + 128), lambda g: (g, 0)),
            by_slots(features),
            by_slots(features),
            by_slots(2 * width),
            by_slots(width),
        ),
        scratch_shapes=[
            pltpu.VMEM((slots, group_tokens), BF16),
            pltpu.VMEM((slots, features), BF16),
            pltpu.VMEM((slots, features), BF16),
        ],
        input_output_aliases={1: 0},
        compiler_params=pltpu.CompilerParams(vmem_limit_bytes=60 * 1024 * 1024),
        cost_estimate=pl.CostEstimate(
            flops=flops, bytes_accessed=4 * tokens * features * 2 + slots * groups * features * 4, transcendentals=0
        ),
    )(rows, pull, position, gate, column, weights)


def body(
    ranks,
    quarters,
    tokens,
    cotangent,
    segments,
    expert_ids,
    attn_gain,
    w_qkv,
    qk_gain,
    w_out,
    mlp_gain,
    router,
    expert_in,
    expert_out,
):
    rank = lax.axis_index("dp")
    quarter = lax.axis_index("tensor")
    local_rows, micro_count, features = tokens.shape
    experts, depth, _, width = expert_in.shape
    top_count = expert_ids.shape[2]
    owned = experts // ranks
    local_tokens = local_rows * micro_count
    group_tokens = quarters * local_tokens
    all_tokens = ranks * group_tokens
    head_dim = qk_gain.shape[0] * ranks
    local_heads = qk_gain.shape[2]
    local_width = local_heads * head_dim
    seq_len = local_rows * quarters
    scale = head_dim ** (-0.5)
    own_shape = (micro_count, local_rows, features)

    def by_micro(array):
        return jnp.swapaxes(array, 0, 1).reshape(local_tokens, features)

    def to_sequences(array):
        array = array.reshape(quarters, micro_count, local_rows, -1)
        return jnp.swapaxes(array, 0, 1).reshape(micro_count, seq_len, -1)

    def from_sequences(array):
        array = array.reshape(micro_count, quarters, local_rows, -1)
        return jnp.swapaxes(array, 0, 1).reshape(group_tokens, -1)

    small_parts = [router, attn_gain, mlp_gain, qk_gain, expert_ids.astype(BF16)]
    sizes = [part.size for part in small_parts]
    small = jnp.concatenate([part.reshape(-1) for part in small_parts])
    small_width = -(-small.size // (depth * 128)) * 128
    small = jnp.pad(small, (0, depth * small_width - small.size)).reshape(depth, small_width)
    own_tokens = by_micro(tokens)
    sources = [w_qkv[:, 0], w_qkv[:, 1], w_qkv[:, 2], small, w_out, own_tokens]
    pieces = tuple((n, 0, sources[n].shape[1], True, ("inner",)) for n in range(5))
    pieces += ((5, 0, features, False, ("side", "core")),)
    full_q, full_k, full_v, small_all, full_out, raw_rows = gather_blocks(
        sources, [ranks] * 5 + [quarters], pieces, ranks, 1
    )
    small_all = small_all.reshape(ranks, depth * small_width)
    ends = [sum(sizes[: n + 1]) for n in range(len(sizes))]
    full_router = small_all[:, : ends[0]].reshape(features, experts)
    gain_one = small_all[:, ends[0] : ends[1]].reshape(features).astype(F32)
    gain_two = small_all[:, ends[1] : ends[2]].reshape(features).astype(F32)
    full_qk = small_all[:, ends[2] : ends[3]].reshape(head_dim, 2, local_heads).astype(F32)
    all_ids = small_all[:, ends[3] : ends[4]].astype(jnp.int32)
    qk_rows = jnp.transpose(full_qk, (1, 2, 0)).reshape(2, local_width)

    blocks = jnp.concatenate(
        [
            expert_in.reshape(ranks, owned, depth, 2 * width),
            expert_out.reshape(ranks, owned, depth, width),
        ],
        axis=3,
    )
    blocks, raw_rows = lax.optimization_barrier((blocks, raw_rows))
    held = send_blocks(blocks, ranks)

    raw_rows = raw_rows.astype(F32)
    rows_one = (raw_rows * norm_factor(raw_rows) * gain_one).astype(BF16)
    query_raw = to_sequences(dot("td,df->tf", rows_one, full_q))
    key_raw = to_sequences(dot("td,df->tf", rows_one, full_k))
    value_rows = to_sequences(dot("td,df->tf", rows_one, full_v).astype(BF16))
    square_q, square_k = lax.psum(
        (jnp.sum(query_raw * query_raw, axis=-1), jnp.sum(key_raw * key_raw, axis=-1)), "tensor"
    )
    factor_q = lax.rsqrt(square_q[..., None] / features + EPSILON)
    factor_k = lax.rsqrt(square_k[..., None] / features + EPSILON)
    heads_shape = (micro_count, seq_len, local_heads, head_dim)
    query_heads = (query_raw * factor_q * qk_rows[0]).astype(BF16).reshape(heads_shape)
    key_heads = (key_raw * factor_k * qk_rows[1]).astype(BF16).reshape(heads_shape)
    value_heads = value_rows.reshape(heads_shape)
    seq_major = segments.T
    positions = jnp.arange(seq_len)
    distance = positions[:, None] - positions[None, :]
    same_doc = seq_major[:, :, None] == seq_major[:, None, :]
    allowed = (same_doc & (distance >= 0) & (distance < WINDOW))[:, None]
    scores = jnp.where(allowed, dot("mqhc,mkhc->mhqk", query_heads, key_heads) * scale, MASKED)
    weights_full = softmax_rows(scores)
    weights_low = weights_full.astype(BF16)
    head_out = dot("mhqk,mkhc->mqhc", weights_low, value_heads).astype(BF16)
    head_out = from_sequences(head_out.reshape(micro_count, seq_len, local_width))

    def scatter_quarters(array):
        across = ((0, 0, features, False, ("side", "core")),)
        return scatter_blocks(array, across, quarters, ranks, 2).astype(F32).reshape(own_shape)

    attended = scatter_quarters(dot("tf,df->td", head_out, full_out).astype(BF16))
    attended, held = tie(attended, held, 0, ranks // 4)
    inputs = own_tokens.astype(F32).reshape(own_shape)
    residual = inputs + attended
    factor_two = norm_factor(residual)
    normed_two = (residual * factor_two * gain_two).astype(BF16).reshape(local_tokens, features)

    rows_all = gather_everywhere(normed_two, ranks, 3)
    pull_own = by_micro(cotangent)
    pull_own, rows_all = lax.optimization_barrier((pull_own, rows_all))
    pull_all = gather_everywhere(pull_own, ranks, 3)
    router_probs = softmax_rows(dot("td,de->te", rows_all, full_router))

    first = rank * owned
    routes = all_ids.reshape(ranks, quarters, local_rows, micro_count, top_count)
    routes = jnp.swapaxes(routes, 2, 3).reshape(ranks, 1, group_tokens, top_count)
    names = first + jnp.arange(owned, dtype=jnp.int32)
    member = jnp.any(routes == names[:, None, None], axis=-1)
    order = jnp.arange(group_tokens)
    earlier = (order[:, None] < order[None, :]).astype(BF16)
    position = dot("ges,st->get", member.astype(BF16), earlier)
    position = jnp.where(member, position, -1.0).astype(jnp.int32)
    gate_own = lax.dynamic_slice_in_dim(router_probs, first, owned, 1)
    gate_own = jnp.swapaxes(gate_own.reshape(ranks, group_tokens, owned), 1, 2)
    lanes = jnp.arange(128, dtype=jnp.int32)
    column = (names[:, None] == lanes).astype(F32)
    mixture_all, returned_all, chosen, pulled, d_gate_up, hidden = expert_math(
        rows_all, pull_all, position, gate_own, column, join_blocks(blocks, held)
    )

    grad_in = dot("egsrk,egsf->rekf", chosen.reshape(owned, ranks, CAP, ranks, depth), d_gate_up)
    grad_out = dot("egsrk,egsf->rekf", pulled.reshape(owned, ranks, CAP, ranks, depth), hidden)
    grad_blocks = jnp.concatenate([grad_in.astype(BF16), grad_out.astype(BF16)], axis=3)
    returned_all, grad_blocks = lax.optimization_barrier((returned_all, grad_blocks))
    sent = send_blocks(grad_blocks, ranks)
    returned_own = scatter_everywhere(returned_all, ranks, 4)

    returned_f = returned_own[:, :features].astype(F32)
    d_probs = returned_own[:, features : features + experts].astype(F32)
    first_token = (rank * quarters + quarter) * local_tokens
    probs_own = lax.dynamic_slice_in_dim(router_probs, first_token, local_tokens, 0)
    d_logits = (
        probs_own * (d_probs - jnp.sum(d_probs * probs_own, axis=-1, keepdims=True))
    ).astype(BF16)
    d_normed_two = (returned_f + dot("te,de->td", d_logits, full_router)).reshape(own_shape)
    grad_router = dot("td,te->de", normed_two, d_logits)
    pull_f = pull_own.astype(F32).reshape(own_shape)
    d_residual = pull_f + norm_back(residual, factor_two, gain_two, d_normed_two)
    grad_gain_two = jnp.sum(residual * factor_two * d_normed_two, axis=(0, 1))
    d_attended = d_residual.astype(BF16).reshape(local_tokens, features)

    (rows_back,) = gather_blocks(
        [d_attended], [quarters], ((0, 0, features, False, ("side", "core")),), ranks, 8
    )
    rows_back, sent = tie(rows_back, sent, 0, ranks // 4)
    d_heads = to_sequences(dot("td,df->tf", rows_back, full_out).astype(BF16)).reshape(heads_shape)
    grad_w_out = dot("td,tf->df", rows_back, head_out)
    d_weights = dot("mqhc,mkhc->mhqk", d_heads, value_heads)
    d_scores = (
        weights_full * (d_weights - jnp.sum(d_weights * weights_full, axis=-1, keepdims=True))
    ).astype(BF16)
    flat_shape = (micro_count, seq_len, local_width)
    d_queries = (dot("mhqk,mkhc->mqhc", d_scores, key_heads) * scale).reshape(flat_shape)
    d_keys = (dot("mhqk,mqhc->mkhc", d_scores, query_heads) * scale).reshape(flat_shape)
    d_values = dot("mhqk,mqhc->mkhc", weights_low, d_heads).reshape(flat_shape).astype(BF16)
    inner_q, inner_k = lax.psum(
        (
            jnp.sum(query_raw * qk_rows[0] * d_queries, axis=-1),
            jnp.sum(key_raw * qk_rows[1] * d_keys, axis=-1),
        ),
        "tensor",
    )
    d_query_raw = (
        factor_q * qk_rows[0] * d_queries - query_raw * factor_q**3 * inner_q[..., None] / features
    )
    d_key_raw = (
        factor_k * qk_rows[1] * d_keys - key_raw * factor_k**3 * inner_k[..., None] / features
    )
    grad_qk_rows = jnp.stack(
        [
            jnp.sum(query_raw * factor_q * d_queries, axis=(0, 1)),
            jnp.sum(key_raw * factor_k * d_keys, axis=(0, 1)),
        ]
    )
    grad_qk = jnp.transpose(grad_qk_rows.reshape(2, local_heads, head_dim), (2, 0, 1))
    d_q = from_sequences(d_query_raw.astype(BF16))
    d_k = from_sequences(d_key_raw.astype(BF16))
    d_v = from_sequences(d_values)
    d_normed_one = scatter_quarters(
        (
            dot("tf,df->td", d_q, full_q)
            + dot("tf,df->td", d_k, full_k)
            + dot("tf,df->td", d_v, full_v)
        ).astype(BF16)
    )
    factor_one = norm_factor(inputs)
    grad_tokens = (d_residual + norm_back(inputs, factor_one, gain_one, d_normed_one)).astype(BF16)
    grad_gain_one = jnp.sum(inputs * factor_one * d_normed_one, axis=(0, 1))

    small_grads = [
        part.reshape(ranks, -1) for part in (grad_router, grad_gain_one, grad_gain_two, grad_qk)
    ]
    small_grads = jnp.concatenate(small_grads, axis=1)
    shared = depth * (experts + 2)
    slim = -(-small_grads.shape[1] // (depth * 128)) * 128
    small_grads = jnp.pad(small_grads, ((0, 0), (0, depth * slim - small_grads.shape[1])))
    grads = [dot("td,tf->df", rows_one, part).astype(BF16) for part in (d_q, d_k, d_v)]
    grads += [grad_w_out.astype(BF16), small_grads.reshape(features, slim).astype(BF16)]
    grads = jnp.concatenate(grads, axis=1)
    cut = 2 * local_width
    pieces = (
        (0, 0, cut, True, ("inner",)),
        (0, cut, grads.shape[1] - cut, True, ("inner",)),
    )
    grads_own = scatter_blocks(grads, pieces, ranks, ranks, 9).astype(F32)
    grad_qkv_own = grads_own[:, : 3 * local_width].reshape(depth, 3, local_width)
    grad_out_own = grads_own[:, 3 * local_width : 4 * local_width]
    small_own = grads_own[:, 4 * local_width :].reshape(-1)
    shared_own = lax.psum(small_own[:shared], "tensor")
    grad_qk_own = small_own[shared : shared + qk_gain.size].reshape(qk_gain.shape)

    mixture_all, _ = lax.optimization_barrier((mixture_all, rows_back))
    mixture_own = scatter_everywhere(mixture_all, ranks, 10)
    layer_out = (residual + mixture_own.astype(F32).reshape(own_shape)).astype(BF16)
    expert_grads = join_blocks(grad_blocks, sent).astype(F32).reshape(experts, depth, 3 * width)
    grad_expert_in = expert_grads[:, :, : 2 * width].reshape(experts, depth, 2, width)
    grad_expert_out = expert_grads[:, :, 2 * width :]
    return (
        jnp.swapaxes(layer_out, 0, 1),
        jnp.swapaxes(grad_tokens, 0, 1),
        shared_own[depth * experts : depth * experts + depth],
        grad_qkv_own,
        grad_qk_own,
        grad_out_own,
        shared_own[depth * (experts + 1) :],
        shared_own[: depth * experts].reshape(depth, experts),
        grad_expert_in,
        grad_expert_out,
    )


def solution(mesh):
    placed = (
        P(("dp", "tensor"), None, None),
        P(("dp", "tensor"), None, None),
        P("dp", None),
        P("dp", None, None),
        P("dp"),
        P("dp", None, "tensor"),
        P("dp", None, "tensor"),
        P("dp", "tensor"),
        P("dp"),
        P("dp", None),
        P(None, "dp", None, "tensor"),
        P(None, "dp", "tensor"),
    )
    return jax.shard_map(
        functools.partial(body, mesh.shape["dp"], mesh.shape["tensor"]),
        mesh=mesh,
        in_specs=placed,
        out_specs=(
            P(("dp", "tensor"), None, None),
            P(("dp", "tensor"), None, None),
            P("dp"),
            P("dp", None, "tensor"),
            P("dp", None, "tensor"),
            P("dp", "tensor"),
            P("dp"),
            P("dp", None),
            P(None, "dp", None, "tensor"),
            P(None, "dp", "tensor"),
        ),
        check_vma=False,
    )
```

time: 1870 us -> 1540 us (0.82)
  Pallas kernels: 0 us -> 1130 us
  waiting for transfers between devices: 857 us -> 2.97 us
  matrix products: 307 us -> 96.7 us
  starting transfers between devices: 223 us -> 30 us
  blocking collectives: 203 us -> 23.7 us
  other arithmetic: 64.7 us -> 44.4 us
    pallas_call x0 -> x10, Pallas kernels: none -> 1130 us  [the longest x5 512 us: scatter_blocks(): pl.pallas_call(functools.partial(scatter_kernel, ranks, pieces), out_shap...]
    reduce_scatter x6 -> x0, waiting for transfers between devices: 429 us -> none  [the longest x1 224 us: body(): lax.psum_scatter(returned_all, everyone, scatter_dimension=0, tiled=True)]
    ppermute x28 -> x14, waiting for transfers between devices: 315 us -> 2.97 us  [send_blocks(): lax.ppermute(block, 'dp', [(j, (j + shift) % ranks) for j in range(ranks)])]
    dot_general x50 -> x24, matrix products: 307 us -> 96.7 us  [dot(): return jnp.einsum(spec, left, right, preferred_element_type=F32)]
    ppermute x28 -> x14, starting transfers between devices: 221 us -> 30 us  [send_blocks(): lax.ppermute(block, 'dp', [(j, (j + shift) % ranks) for j in range(ranks)])]
    all_gather x2 -> x0, blocking collectives: 177 us -> none  [the longest x1 145 us: body(): all_ids = lax.all_gather(expert_ids, 'dp', axis=0, tiled=True)]
    all_gather x6 -> x0, waiting for transfers between devices: 110 us -> none  [the longest x1 85.1 us: body(): full_qkv = lax.all_gather(w_qkv, 'dp', axis=0, tiled=True)]
    unnamed x289 -> x158, local copies, waits for them, and re-layouts: 46.9 us -> 24.4 us
  transfers between devices with their start and end apart: 41 -> 14, of which waited for: 18 -> 1; matrix products, arithmetic and copies ran while one was open for 17% -> 8% of each run, Pallas kernels for 0% -> 52%
where the time goes in v2:
time: 1540 us; the launch traced here: 1520 us
  Pallas kernels  1130 us (73%)
  local copies, waits for them, and re-layouts  187 us (12%)
  matrix products  96.7 us (6%)
  other arithmetic  44.4 us (3%)
  starting transfers between devices  30 us (2%)
  blocking collectives  23.7 us (2%)
    pallas_call x5, Pallas kernels, scatter_blocks(): pl.pallas_call(functools.partial(scatter_kernel, ranks, pieces), out_shap...  512 us
    pallas_call x4, Pallas kernels, gather_blocks(): pl.pallas_call(functools.partial(gather_kernel, ranks, arrays, pieces), o...  503 us
    pallas_call x1, Pallas kernels, expert_math(): pl.pallas_call(functools.partial(expert_kernel, owned, width), grid=(grou...  119 us
    dot_general x24, matrix products, dot(): return jnp.einsum(spec, left, right, preferred_element_type=F32)  96.7 us
    dynamic_update_slice x12, local copies, waits for them, and re-layouts, join_blocks(): blocks = lax.dynamic_update_slice_in_dim(blocks, block, origin, 0)  31.8 us
  transfers between devices with their start and end apart: 14, of which 1 were waited for; matrix products, arithmetic and copies ran while one was open for 8% of the time, Pallas kernels for 52%

profile of v2, /device:TPU:0, one launch (start us, length us, event | category | flops | bytes accessed | tf_op | source)
XLA Modules:
  0.0 1521.3 jit_solution(40865697411362474)
XLA Ops:
  9.3 14.0 reshape.359
  23.3 10.4 pad_maximum_fusion
  33.7 106.9 %shard_map.195 = (bf16[2048,512]{1,0:T(8,128)(2,1)}, bf16[2048,512]{1,0:T(8,128)(2,1)}, bf16[2048,512]{1,0:T(8,128)(2,1)}, bf16[2048,128]{1,0:T(8,128)(2,1)}, bf...) custom-call(bf16[256,512]{1,0:T(8,128)(2,1)} %get-tuple-element.139.refs_0_, ...), custom_call_target="tpu_custom_call" | custom-call | bytes 11010048 | tf_op jit(solution)/shard_map/pallas_call | solution.py:198
  140.7 3.8 constant_dynamic-slice_fusion.13
  151.8 3.1 convolution_convert_fusion.7
  156.6 2.9 fusion.86
  160.7 3.5 fusion.88
  171.3 4.5 reshape.420
  175.8 2.7 copy.277
  178.8 5.9 all-reduce.3
  188.2 2.5 fusion.39
  191.2 4.4 convolution_convert_fusion.4.in_ref
  195.6 20.9 %shard_map.196 = bf16[128,2048]{1,0:T(8,128)(2,1)} custom-call(bf16[512,2048]{1,0:T(8,128)(2,1)} %convolution_convert_fusion.4.in_ref), custom_call_target="tpu_custom_call" | custom-call | flops 1048576 | bytes 2097152 | tf_op jit(solution)/shard_map/pallas_call | solution.py:401
  221.0 7.5 constant_dynamic-slice_fusion.7
  228.4 4.2 collective-permute-start.6
  233.3 2.2 collective-permute-start.3
  237.8 291.2 %shard_map.197.rows_ref = bf16[4096,2048]{1,0:T(8,128)(2,1)} custom-call(bf16[128,2048]{1,0:T(8,128)(2,1)} %bitcast.204), custom_call_target="tpu_custom_call" | custom-call | bytes 16777216 | tf_op jit(solution)/shard_map/pallas_call | solution.py:198
  529.0 10.8 fusion.94
  541.7 2.3 fusion.35
  546.6 86.1 %shard_map.198.pull_ref = bf16[4096,2048]{1,0:T(8,128)(2,1)} custom-call(bf16[128,2048]{1,0:T(8,128)(2,1)} %bitcast.206), custom_call_target="tpu_custom_call" | custom-call | bytes 16777216 | tf_op jit(solution)/shard_map/pallas_call | solution.py:198
  632.7 2.7 constant_dynamic-update-slice_fusion.14
  635.4 2.7 constant_dynamic-update-slice_fusion.13
  638.0 2.7 constant_dynamic-update-slice_fusion.12
  640.7 2.7 constant_dynamic-update-slice_fusion.11
  643.3 2.7 constant_dynamic-update-slice_fusion.10
  646.0 2.7 constant_dynamic-update-slice_fusion.9.weight_ref
  648.6 119.1 %shard_map.199 = (bf16[4096,2048]{1,0:T(8,128)(2,1)}, bf16[4096,2176]{1,0:T(8,128)(2,1)}, bf16[4,8,176,2048]{3,2,1,0:T(8,128)(2,1)}, bf16[4,8,176,2048]{3,2,1,0:...) custom-call(bf16[4096,2048]{1,0:T(8,128)(2,1)} %shard_map.197.rows_r, ...), custom_call_target="tpu_custom_call", output_to_operand_aliasing={{0}: (1, {})} | custom-call | flops 82678120448 | bytes 113246208 | tf_op jit(solution)/shard_map/pallas_call | solution.py:558
  767.7 13.7 fusion.20
  781.4 20.7 %fusion.12 = bf16[8,4,256,512]{2,3,0,1:T(8,128)(2,1)} fusion(bf16[4,8,22,8,8,256]{5,4,3,2,1,0:T(8,128)(2,1)} %bitcast.245, bf16[4,8,176,512]{3,2,1,0:T(8,128)(2,1)} %get-tuple-element.50), kind=kOutput, calls=%fused_computation.14 | convolution fusion | flops 11815354368 | bytes 37224448 | tf_op jit(solution)/shard_map/egsrk,egsf->rekf/dot_general | solution.py:38
  802.1 8.9 pad_maximum_fusion.1
  811.1 4.8 copy-done
  819.0 140.4 %shard_map.200 = bf16[128,2176]{1,0:T(8,128)(2,1)} custom-call(bf16[4096,2176]{1,0:T(8,128)(2,1)} %get-tuple-element.54.in_ref), custom_call_target="tpu_custom_call" | custom-call | flops 8912896 | bytes 17825792 | tf_op jit(solution)/shard_map/pallas_call | solution.py:401
  965.6 18.8 %shard_map.201 = bf16[512,2048]{1,0:T(8,128)(2,1)} custom-call(bf16[128,2048]{1,0:T(8,128)(2,1)} %bitcast.221), custom_call_target="tpu_custom_call" | custom-call | bytes 2097152 | tf_op jit(solution)/shard_map/pallas_call | solution.py:198
  984.5 3.5 convolution_convert_fusion.6
  989.2 3.5 fusion.40
  999.8 2.6 copy.290
  1002.4 2.6 reshape.389
  1005.0 6.3 all-reduce.2
  1013.2 3.3 fusion.98
  1016.5 2.9 fusion.26
  1020.8 96.8 %shard_map.202 = bf16[128,2048]{1,0:T(8,128)(2,1)} custom-call(bf16[4096,2048]{1,0:T(8,128)(2,1)} %get-tuple-element.57.in_ref), custom_call_target="tpu_custom_call" | custom-call | flops 8388608 | bytes 16777216 | tf_op jit(solution)/shard_map/pallas_call | solution.py:401
  1117.6 2.2 multiply_reduce_fusion.3
  1125.5 2.7 add_convert_fusion.in_ref
  1128.2 21.0 %shard_map.203 = bf16[128,2048]{1,0:T(8,128)(2,1)} custom-call(bf16[512,2048]{1,0:T(8,128)(2,1)} %add_convert_fusion.in_ref), custom_call_target="tpu_custom_call" | custom-call | flops 1048576 | bytes 2097152 | tf_op jit(solution)/shard_map/pallas_call | solution.py:401
  1150.6 7.6 constant_dynamic-slice_fusion
  1158.3 8.6 collective-permute-start.12
  1166.9 3.2 collective-permute-start.10
  1170.3 3.0 fusion.25
  1173.3 2.9 fusion.24
  1176.3 2.8 fusion.23
  1181.0 232.8 %shard_map.204 = bf16[256,2176]{1,0:T(8,128)(2,1)} custom-call(bf16[2048,2176]{1,0:T(8,128)(2,1)} %constant_dynamic-update-slice_fusion.1.in_ref), custom_call_target="tpu_custom_call" | custom-call | flops 4456448 | bytes 8912896 | tf_op jit(solution)/shard_map/pallas_call | solution.py:401
  1421.2 6.6 collective-permute-start.13
  1430.7 11.6 psum.39
  1444.6 2.7 constant_dynamic-update-slice_fusion.7
  1447.8 2.7 constant_dynamic-update-slice_fusion.6
  1450.5 2.7 constant_dynamic-update-slice_fusion.5
  1453.1 2.7 constant_dynamic-update-slice_fusion.4
  1455.8 2.7 constant_dynamic-update-slice_fusion.3
  1458.4 2.9 collective-permute-done.13
  1461.4 2.7 constant_dynamic-update-slice_fusion.2
  1464.0 17.8 %copy.309 = f32[8,4,256,768]{3,2,1,0:T(8,128)} copy(bf16[8,4,256,768]{2,3,0,1:T(8,128)(2,1)} %constant_dynamic-update-slice_fusion.2) | data formatting | bytes 37748736 | tf_op jit(solution)/shard_map/reshape | solution.py:829
  1481.8 7.7 slice.121
  1489.5 11.6 slice.120
  1501.1 19.9 %reshape.405 = f32[32,256,2,256]{3,2,1,0:T(2,128)} reshape(f32[32,256,512]{2,1,0:T(8,128)} %slice.120) | data formatting | bytes 33554432 | tf_op jit(solution)/shard_map/reshape | solution.py:830
  (286 shorter events, 84.7 us)
Async XLA Ops:
  0.6 7.8 copy-start.35
  140.7 6.2 copy-start.46
  144.5 2.6 copy-start.41
  144.5 74.9 %collective-permute-start.1 = (bf16[1,4,256,768]{3,2,1,0:T(8,128)(2,1)}, bf16[1,4,256,768]{3,2,1,0:T(8,128)(2,1)}, u32[]{:S(2)}, u32[]{:S(2)}) collective-permute-start(bf16[1,4,256,768]{3,2,1,0:T(8,128)(2,1)} %get-tuple-element.134), channel_id=1, source_target_pairs={{0,8},{4,12},{8,16},{12,20},{16,24},{20,28},{24,0},{28,4},{1,9},{5... | collective-permute-start | bytes 4718600 | tf_op jit(solution)/shard_map/ppermute | solution.py:447
  146.2 73.3 %collective-permute-start = (bf16[1,4,256,768]{3,2,1,0:T(8,128)(2,1)}, bf16[1,4,256,768]{3,2,1,0:T(8,128)(2,1)}, u32[]{:S(2)}, u32[]{:S(2)}) collective-permute-start(bf16[1,4,256,768]{3,2,1,0:T(8,128)(2,1)} %get-tuple-element.135), channel_id=1, source_target_pairs={{0,4},{4,8},{8,12},{12,16},{16,20},{20,24},{24,28},{28,0},{1,5},{5... | collective-permute-start | bytes 4718600 | tf_op jit(solution)/shard_map/ppermute | solution.py:447
  147.2 4.6 copy-start.23
  150.2 10.5 copy-start.70
  150.2 86.6 %copy-start.49 = (f32[1,2,8,128]{3,1,2,0:T(2,128)}, f32[1,2,8,128]{3,1,2,0:T(2,128)S(1)}, u32[]{:S(2)}) copy-start(f32[1,2,8,128]{3,1,2,0:T(2,128)S(1)} %copy.336) | copy-start | bytes 24580
  150.3 10.5 copy-start.64
  150.7 34.7 %copy-start.57 = (f32[4,128]{1,0:T(4,128)}, f32[4,128]{1,0:T(4,128)S(1)}, u32[]{:S(2)}) copy-start(f32[4,128]{1,0:T(4,128)S(1)} %copy.266) | copy-start | bytes 6148
  151.3 34.1 %copy-start.59 = (f32[4,128]{1,0:T(4,128)}, f32[4,128]{1,0:T(4,128)S(1)}, u32[]{:S(2)}) copy-start(f32[4,128]{1,0:T(4,128)S(1)} %copy.269) | copy-start | bytes 6148
  151.7 377.3 %copy-start.20 = (bf16[2048,32]{1,0:T(8,128)(2,1)}, bf16[2048,32]{1,0:T(8,128)(2,1)S(1)}, u32[]{:S(2)}) copy-start(bf16[2048,32]{1,0:T(8,128)(2,1)S(1)} %reshape.378) | copy-start | bytes 393220
  168.3 17.1 %copy-start.5 = (f32[2,256,4,128]{1,3,2,0:T(8,128)}, f32[2,256,4,128]{1,3,2,0:T(8,128)S(1)}, u32[]{:S(2)}) copy-start(f32[2,256,4,128]{1,3,2,0:T(8,128)S(1)} %copy.265) | copy-start | bytes 3145732
  171.2 14.2 copy-start.7
  171.3 14.0 copy-start.63
  185.4 2.8 copy-start.40
  188.2 2.5 copy-start.55
  191.2 4.4 copy-start.42
  195.6 23.8 %copy-start.17 = (bf16[64,2,2048]{2,1,0:T(2,128)(2,1)S(1)}, bf16[64,2,2048]{2,1,0:T(2,128)(2,1)}, u32[]{:S(2)}) copy-start(bf16[64,2,2048]{2,1,0:T(2,128)(2,1)} %param.12) | copy-start | bytes 1572868
  220.3 16.5 %copy-start.3 = (f32[2,64,2048]{2,1,0:T(8,128)}, f32[2,64,2048]{2,1,0:T(8,128)S(1)}, u32[]{:S(2)}) copy-start(f32[2,64,2048]{2,1,0:T(8,128)S(1)} %get-tuple-element.119) | copy-start | bytes 3145732
  221.0 15.9 %copy-start.61 = (f32[2,64]{1,0:T(2,128)}, f32[2,64]{1,0:T(2,128)S(1)}, u32[]{:S(2)}) copy-start(f32[2,64]{1,0:T(2,128)S(1)} %get-tuple-element.155) | copy-start | bytes 1540
  228.4 417.5 %collective-permute-start.6 = (bf16[1,4,256,768]{3,2,1,0:T(8,128)(2,1)}, bf16[1,4,256,768]{3,2,1,0:T(8,128)(2,1)}, u32[]{:S(2)}, u32[]{:S(2)}) collective-permute-start(bf16[1,4,256,768]{3,2,1,0:T(8,128)(2,1)} %get-tuple-element.128), channel_id=1, source_target_pairs={{0,28},{4,0},{8,4},{12,8},{16,12},{20,16},{24,20},{28,24},{1,29},{... | collective-permute-start | bytes 4718600 | tf_op jit(solution)/shard_map/ppermute | solution.py:447
  232.7 410.7 %collective-permute-start.5 = (bf16[1,4,256,768]{3,2,1,0:T(8,128)(2,1)}, bf16[1,4,256,768]{3,2,1,0:T(8,128)(2,1)}, u32[]{:S(2)}, u32[]{:S(2)}) collective-permute-start(bf16[1,4,256,768]{3,2,1,0:T(8,128)(2,1)} %get-tuple-element.129), channel_id=1, source_target_pairs={{0,24},{4,28},{8,0},{12,4},{16,8},{20,12},{24,16},{28,20},{1,25},{... | collective-permute-start | bytes 4718600 | tf_op jit(solution)/shard_map/ppermute | solution.py:447
  233.0 407.6 %collective-permute-start.4 = (bf16[1,4,256,768]{3,2,1,0:T(8,128)(2,1)}, bf16[1,4,256,768]{3,2,1,0:T(8,128)(2,1)}, u32[]{:S(2)}, u32[]{:S(2)}) collective-permute-start(bf16[1,4,256,768]{3,2,1,0:T(8,128)(2,1)} %get-tuple-element.130), channel_id=1, source_target_pairs={{0,20},{4,24},{8,28},{12,0},{16,4},{20,8},{24,12},{28,16},{1,21},{... | collective-permute-start | bytes 4718600 | tf_op jit(solution)/shard_map/ppermute | solution.py:447
  233.3 404.7 %collective-permute-start.3 = (bf16[1,4,256,768]{3,2,1,0:T(8,128)(2,1)}, bf16[1,4,256,768]{3,2,1,0:T(8,128)(2,1)}, u32[]{:S(2)}, u32[]{:S(2)}) collective-permute-start(bf16[1,4,256,768]{3,2,1,0:T(8,128)(2,1)} %get-tuple-element.131), channel_id=1, source_target_pairs={{0,16},{4,20},{8,24},{12,28},{16,0},{20,4},{24,8},{28,12},{1,17},{... | collective-permute-start | bytes 4718600 | tf_op jit(solution)/shard_map/ppermute | solution.py:447
  235.6 399.8 %collective-permute-start.2 = (bf16[1,4,256,768]{3,2,1,0:T(8,128)(2,1)}, bf16[1,4,256,768]{3,2,1,0:T(8,128)(2,1)}, u32[]{:S(2)}, u32[]{:S(2)}) collective-permute-start(bf16[1,4,256,768]{3,2,1,0:T(8,128)(2,1)} %get-tuple-element.132), channel_id=1, source_target_pairs={{0,12},{4,16},{8,20},{12,24},{16,28},{20,0},{24,4},{28,8},{1,13},{... | collective-permute-start | bytes 4718600 | tf_op jit(solution)/shard_map/ppermute | solution.py:447
  811.1 4.8 copy-start
  815.8 2.6 copy-start.39
  815.9 2.7 copy-start.37
  815.9 2.8 copy-start.52
  815.9 2.9 copy-start.54
  815.9 2.9 copy-start.67
  815.9 3.0 copy-start.66
  815.9 3.1 copy-start.68
  817.8 166.7 %collective-permute-start.8 = (bf16[1,4,256,768]{2,3,0,1:T(8,128)(2,1)}, bf16[1,4,256,768]{2,3,0,1:T(8,128)(2,1)}, u32[]{:S(2)}, u32[]{:S(2)}) collective-permute-start(bf16[1,4,256,768]{2,3,0,1:T(8,128)(2,1)} %get-tuple-element.126), channel_id=1, source_target_pairs={{0,8},{4,12},{8,16},{12,20},{16,24},{20,28},{24,0},{28,4},{1,9},{5... | collective-permute-start | bytes 4718600 | tf_op jit(solution)/shard_map/ppermute | solution.py:447
  817.8 166.7 %collective-permute-start.7 = (bf16[1,4,256,768]{2,3,0,1:T(8,128)(2,1)}, bf16[1,4,256,768]{2,3,0,1:T(8,128)(2,1)}, u32[]{:S(2)}, u32[]{:S(2)}) collective-permute-start(bf16[1,4,256,768]{2,3,0,1:T(8,128)(2,1)} %get-tuple-element.127), channel_id=1, source_target_pairs={{0,4},{4,8},{8,12},{12,16},{16,20},{20,24},{24,28},{28,0},{1,5},{5... | collective-permute-start | bytes 4718600 | tf_op jit(solution)/shard_map/ppermute | solution.py:447
  819.0 141.5 %copy-start.16 = (bf16[2,64,2048]{2,1,0:T(8,128)(2,1)S(1)}, bf16[2,64,2048]{2,1,0:T(8,128)(2,1)}, u32[]{:S(2)}) copy-start(bf16[2,64,2048]{2,1,0:T(8,128)(2,1)} %multiply_convert_fusion.1) | copy-start | bytes 1572868
  959.4 3.2 copy-start.21
  959.4 4.6 copy-start.4
  959.4 4.6 copy-start.19
  959.4 4.6 copy-start.50
  959.4 4.6 copy-start.62
  959.4 4.6 copy-start.69
  989.2 3.5 copy-start.45
  989.2 3.5 copy-start.48
  999.8 11.5 copy-start.12
  1013.2 3.3 copy-start.29
  1013.2 3.3 copy-start.65
  1013.2 3.3 copy-start.71
  1016.5 2.9 copy-start.47
  1122.6 2.9 copy-start.24
  1122.6 2.9 copy-start.27
  1128.2 21.0 %copy-start.18 = (bf16[64,2,2048]{2,1,0:T(2,128)(2,1)S(1)}, bf16[64,2,2048]{2,1,0:T(2,128)(2,1)}, u32[]{:S(2)}) copy-start(bf16[64,2,2048]{2,1,0:T(2,128)(2,1)} %param.12) | copy-start | bytes 1572868
  1150.6 19.7 %copy-start.30 = (bf16[512,2048]{1,0:T(8,128)(2,1)S(1)}, bf16[512,2048]{1,0:T(8,128)(2,1)}, u32[]{:S(2)}) copy-start(bf16[512,2048]{1,0:T(8,128)(2,1)} %get-tuple-element.36) | copy-start | bytes 6291460
  1158.3 297.5 %collective-permute-start.12 = (bf16[1,4,256,768]{2,3,0,1:T(8,128)(2,1)}, bf16[1,4,256,768]{2,3,0,1:T(8,128)(2,1)}, u32[]{:S(2)}, u32[]{:S(2)}) collective-permute-start(bf16[1,4,256,768]{2,3,0,1:T(8,128)(2,1)} %get-tuple-element.121), channel_id=1, source_target_pairs={{0,24},{4,28},{8,0},{12,4},{16,8},{20,12},{24,16},{28,20},{1,25},{... | collective-permute-start | bytes 4718600 | tf_op jit(solution)/shard_map/ppermute | solution.py:447
  1166.9 286.2 %collective-permute-start.11 = (bf16[1,4,256,768]{2,3,0,1:T(8,128)(2,1)}, bf16[1,4,256,768]{2,3,0,1:T(8,128)(2,1)}, u32[]{:S(2)}, u32[]{:S(2)}) collective-permute-start(bf16[1,4,256,768]{2,3,0,1:T(8,128)(2,1)} %get-tuple-element.122), channel_id=1, source_target_pairs={{0,20},{4,24},{8,28},{12,0},{16,4},{20,8},{24,12},{28,16},{1,21},{... | collective-permute-start | bytes 4718600 | tf_op jit(solution)/shard_map/ppermute | solution.py:447
  1166.9 283.6 %collective-permute-start.10 = (bf16[1,4,256,768]{2,3,0,1:T(8,128)(2,1)}, bf16[1,4,256,768]{2,3,0,1:T(8,128)(2,1)}, u32[]{:S(2)}, u32[]{:S(2)}) collective-permute-start(bf16[1,4,256,768]{2,3,0,1:T(8,128)(2,1)} %get-tuple-element.123), channel_id=1, source_target_pairs={{0,16},{4,20},{8,24},{12,28},{16,0},{20,4},{24,8},{28,12},{1,17},{... | collective-permute-start | bytes 4718600 | tf_op jit(solution)/shard_map/ppermute | solution.py:447
  1170.1 277.7 %collective-permute-start.9 = (bf16[1,4,256,768]{2,3,0,1:T(8,128)(2,1)}, bf16[1,4,256,768]{2,3,0,1:T(8,128)(2,1)}, u32[]{:S(2)}, u32[]{:S(2)}) collective-permute-start(bf16[1,4,256,768]{2,3,0,1:T(8,128)(2,1)} %get-tuple-element.124), channel_id=1, source_target_pairs={{0,12},{4,16},{8,20},{12,24},{16,28},{20,0},{24,4},{28,8},{1,13},{... | collective-permute-start | bytes 4718600 | tf_op jit(solution)/shard_map/ppermute | solution.py:447
  1173.3 2.9 copy-start.26
  1173.3 2.9 copy-start.43
  1176.3 2.8 copy-start.25
  1176.3 2.8 copy-start.34
  1413.8 3.2 copy-start.2
  1421.2 40.1 %collective-permute-start.13 = (bf16[1,4,256,768]{2,3,0,1:T(8,128)(2,1)}, bf16[1,4,256,768]{2,3,0,1:T(8,128)(2,1)}, u32[]{:S(2)}, u32[]{:S(2)}) collective-permute-start(bf16[1,4,256,768]{2,3,0,1:T(8,128)(2,1)} %get-tuple-element.120), channel_id=1, source_target_pairs={{0,28},{4,0},{8,4},{12,8},{16,12},{20,16},{24,20},{28,24},{1,29},{... | collective-permute-start | bytes 4718600 | tf_op jit(solution)/shard_map/ppermute | solution.py:447
  (22 other events, 32.6 us)

commit v3 on v2

--- a/solution.py
+++ b/solution.py
@@ -38,20 +38,47 @@
     return jnp.einsum(spec, left, right, preferred_element_type=F32)
 
 
-def mesh_places(ranks):
-    rank = lax.axis_index("dp")
-    quarter = lax.axis_index("tensor")
-    return rank // 2, {
-        "inner": lax.rem(rank, 2),
-        "side": quarter // 2,
-        "core": lax.rem(quarter, 2),
-    }
-
-
-def device_at(ranks, steps, flips):
-    outer, pairs = mesh_places(ranks)
-    place = {name: 1 - at if name in flips else at for name, at in pairs.items()}
-    return (outer + steps) * 2 + place["inner"], place["side"] * 2 + place["core"]
+class Places:
+    def __init__(self, ranks, pieces):
+        rank = lax.axis_index("dp")
+        quarter = lax.axis_index("tensor")
+        count = ranks // 2
+        self.count = count
+        self.outer = rank // 2
+        self.rank_base = self.outer * 2
+        pairs = {
+            "inner": lax.rem(rank, 2),
+            "side": quarter // 2,
+            "core": lax.rem(quarter, 2),
+        }
+        self.exists = {0: None}
+        if any(piece[3] for piece in pieces):
+            for steps in range(1, count):
+                self.exists[steps] = self.outer + steps < count
+                self.exists[-steps] = self.outer - steps >= 0
+        self.inner = {}
+        self.quarter = {}
+        self.whole = {}
+        for flips in itertools.product((0, 1), repeat=3):
+            names = frozenset(name for name, bit in zip(("inner", "side", "core"), flips) if bit)
+            place = {name: 1 - at if name in names else at for name, at in pairs.items()}
+            self.inner[names] = self.rank_base + place["inner"]
+            self.quarter[names] = place["side"] * 2 + place["core"]
+            self.whole[names] = self.inner[names] * 4 + self.quarter[names]
+
+    def device(self, steps, flips):
+        names = frozenset(flips)
+        return self.inner[names] + 2 * steps if steps else self.inner[names], self.quarter[names]
+
+    def rows(self, piece, steps, flips, rows):
+        names = frozenset(flips)
+        if not piece[3]:
+            index = self.quarter[names]
+        elif "side" not in piece[4]:
+            index = self.inner[names] + 2 * steps
+        else:
+            index = self.whole[names] + 8 * steps
+        return pl.ds(pl.multiple_of(index * rows, rows), rows)
 
 
 def run_if(conditions, action):
@@ -62,22 +89,15 @@
     pl.when(functools.reduce(jnp.logical_and, conditions))(action)
 
 
-def on_chain(ranks, steps):
-    outer, _ = mesh_places(ranks)
-    if steps == 0:
-        return None
-    return outer + steps < ranks // 2 if steps > 0 else outer + steps >= 0
-
-
-def greet(ranks, pieces):
+def greet(places, pieces):
     barrier = pltpu.get_barrier_semaphore()
     pairs = sorted({name for piece in pieces for name in piece[4]})
     targets = [(None, 0, (name,)) for name in pairs]
     if any(piece[3] for piece in pieces):
-        targets += [(on_chain(ranks, steps), steps, ()) for steps in (-1, 1)]
+        targets += [(places.exists[steps], steps, ()) for steps in (-1, 1)]
 
     def signal(steps, flips):
-        target = device_at(ranks, steps, flips)
+        target = places.device(steps, flips)
         pl.semaphore_signal(barrier, inc=1, device_id=target, device_id_type=MESH)
 
     expected = len(pairs)
@@ -93,19 +113,19 @@
     return [0] + [sign * k for k in range(1, count) for sign in (-1, 1)] if outer else [0]
 
 
-def row_start(ranks, piece, steps, flips, rows):
-    rank, quarter = device_at(ranks, steps, flips)
-    if not piece[3]:
-        index = quarter
-    elif "side" not in piece[4]:
-        index = rank
-    else:
-        index = rank * 4 + quarter
-    return pl.ds(pl.multiple_of(index * rows, rows), rows)
-
-
 def all_bits(dims):
     return list(itertools.product((0, 1), repeat=len(dims)))
+
+
+def semaphores(ranks, pieces):
+    starts = [0]
+    for _, _, _, outer, dims in pieces:
+        starts.append(starts[-1] + len(chain_steps(ranks, outer)) * 2 ** len(dims))
+    return starts
+
+
+def chain_number(ranks, piece, steps):
+    return steps + ranks // 2 - 1 if piece[3] else 0
 
 
 def level_of(bits):
@@ -116,7 +136,9 @@
     in_refs, out_refs = refs[:arrays], refs[arrays : 2 * arrays]
     send_sem, recv_sem, local_sem = refs[2 * arrays :]
     count = ranks // 2
-    greet(ranks, pieces)
+    starts = semaphores(ranks, pieces)
+    places = Places(ranks, pieces)
+    greet(places, pieces)
     started = []
 
     def flips_of(p, bits):
@@ -127,17 +149,18 @@
         rows = in_refs[array].shape[0]
         columns = pl.ds(start, width)
         place = out_refs[array].at[
-            row_start(ranks, pieces[p], steps, flips_of(p, bits), rows), columns
+            places.rows(pieces[p], steps, flips_of(p, bits), rows), columns
         ]
         own = steps == 0 and not any(bits)
         seen_steps, seen_bits = as_seen
-        sem = (seen_steps + count - 1) * 2 ** len(dims) + all_bits(dims).index(seen_bits)
+        sem = chain_number(ranks, pieces[p], seen_steps) * 2 ** len(dims)
+        sem += starts[p] + all_bits(dims).index(seen_bits)
         return pltpu.make_async_remote_copy(
             src_ref=in_refs[array].at[:, columns] if own else place,
             dst_ref=place,
-            send_sem=send_sem.at[p, sem],
-            recv_sem=recv_sem.at[p, sem],
-            device_id=device_at(ranks, target_steps, target_flips),
+            send_sem=send_sem.at[sem],
+            recv_sem=recv_sem.at[sem],
+            device_id=places.device(target_steps, target_flips),
             device_id_type=MESH,
         )
 
@@ -147,12 +170,12 @@
 
     def forward(p, steps, bits):
         outer, dims = pieces[p][3:]
-        here = on_chain(ranks, steps)
+        here = places.exists[steps]
         level = level_of(bits)
         if outer and level == 0:
             for direction in (-1, 1):
                 if steps * direction <= 0 and abs(steps) < count - 1:
-                    there = on_chain(ranks, direction)
+                    there = places.exists[direction]
                     seen = (steps - direction, bits)
                     send([here, there], p, steps, bits, seen, direction, ())
         for n in range(level, len(dims)):
@@ -160,7 +183,7 @@
             send([here], p, steps, bits, seen, 0, (dims[n],))
 
     def receive(p, steps, bits):
-        here = on_chain(ranks, steps)
+        here = places.exists[steps]
         run_if([here], lambda: copy(p, steps, bits, (steps, bits), 0, (pieces[p][4][0],)).wait_recv())
         forward(p, steps, bits)
 
@@ -170,7 +193,7 @@
         rows = in_refs[array].shape[0]
         keep = pltpu.make_async_copy(
             in_refs[array],
-            out_refs[array].at[row_start(ranks, piece, 0, (), rows)],
+            out_refs[array].at[places.rows(piece, 0, (), rows)],
             local_sem.at[array],
         )
         keep.start()
@@ -194,7 +217,7 @@
 
 def gather_blocks(blocks, results, pieces, ranks, collective_id):
     arrays = len(blocks)
-    transfers = (ranks - 1) * 8
+    transfers = semaphores(ranks, pieces)[-1]
     return pl.pallas_call(
         functools.partial(gather_kernel, ranks, arrays, pieces),
         out_shape=tuple(
@@ -204,8 +227,8 @@
         in_specs=[pl.BlockSpec(memory_space=pl.ANY)] * arrays,
         out_specs=(pl.BlockSpec(memory_space=pl.ANY),) * arrays,
         scratch_shapes=[
-            pltpu.SemaphoreType.DMA((len(pieces), transfers)),
-            pltpu.SemaphoreType.DMA((len(pieces), transfers)),
+            pltpu.SemaphoreType.DMA((transfers,)),
+            pltpu.SemaphoreType.DMA((transfers,)),
             pltpu.SemaphoreType.DMA((arrays,)),
         ],
         compiler_params=pltpu.CompilerParams(collective_id=collective_id, has_side_effects=True),
@@ -226,13 +249,13 @@
     return gather_blocks([block], [4 * ranks], pieces, ranks, collective_id)[0]
 
 
-def scatter_kernel(ranks, pieces, in_ref, out_ref, *scratch):
+def scatter_kernel(ranks, arrays, pieces, *refs):
+    in_refs, out_refs, scratch = refs[:arrays], refs[arrays : 2 * arrays], refs[2 * arrays :]
     buffers, (send_sem, recv_sem, load_sem) = scratch[:-3], scratch[-3:]
-    rows = out_ref.shape[0]
     count = ranks // 2
-    tile = min(rows, 32)
-    greet(ranks, pieces)
-    outer_place, _ = mesh_places(ranks)
+    starts = semaphores(ranks, pieces)
+    places = Places(ranks, pieces)
+    greet(places, pieces)
     started = []
     held = []
     for _, _, _, _, dims in pieces:
@@ -243,31 +266,33 @@
         buffers = buffers[depth + 3 :]
 
     def region(p, steps, bits):
-        _, start, width, _, dims = pieces[p]
+        array, start, width, _, dims = pieces[p]
         flips = tuple(name for name, bit in zip(dims, bits) if bit)
-        return in_ref.at[row_start(ranks, pieces[p], steps, flips, rows), pl.ds(start, width)]
-
-    def slot(steps, bits):
-        place = outer_place + steps if pieces[0][3] else 0
+        rows = out_refs[array].shape[0]
+        return in_refs[array].at[places.rows(pieces[p], steps, flips, rows), pl.ds(start, width)]
+
+    def slot(p, steps, bits):
+        place = places.outer + steps if pieces[p][3] else 0
         number = 0
         for bit in bits:
             number = 2 * number + bit
         return place * 2 ** len(bits) + number
 
-    def sem_of(steps, bits, kind):
+    def sem_of(p, steps, bits, kind):
         code = 0
         for bit in bits:
             code = 2 * code + bit
-        return ((steps + count - 1) * 2 ** len(bits) + code) * 2 + kind
+        number = chain_number(ranks, pieces[p], steps) * 2 ** len(bits) + code
+        return (starts[p] + number) * 2 + kind
 
     def own_at(p, steps, bits):
-        return held[p][0].at[slot(steps, bits)]
+        return held[p][0].at[slot(p, steps, bits)]
 
     def load(p, steps, bits):
         return pltpu.make_async_copy(
             region(p, steps, bits + (0,)),
             own_at(p, steps, bits),
-            load_sem.at[p, sem_of(steps, bits, 0) // 2],
+            load_sem.at[sem_of(p, steps, bits + (0,), 0) // 2],
         )
 
     def pair_copy(p, steps, bits, n):
@@ -276,39 +301,42 @@
         last = n == len(dims) - 1
         return pltpu.make_async_remote_copy(
             src_ref=region(p, steps, whole) if last else own_at(p, steps, whole[:-1]),
-            dst_ref=held[p][1][n].at[slot(steps, bits[:n])],
-            send_sem=send_sem.at[p, sem_of(steps, whole, 0)],
-            recv_sem=recv_sem.at[p, sem_of(steps, whole, 0)],
-            device_id=device_at(ranks, 0, (dims[n],)),
+            dst_ref=held[p][1][n].at[slot(p, steps, bits[:n])],
+            send_sem=send_sem.at[sem_of(p, steps, whole, 0)],
+            recv_sem=recv_sem.at[sem_of(p, steps, whole, 0)],
+            device_id=places.device(0, (dims[n],)),
             device_id_type=MESH,
         )
 
     def chain_copy(p, steps, direction):
         zeros = (0,) * (len(pieces[p][4]) - 1)
-        sem = sem_of(steps - direction, zeros + (0,), 1)
+        sem = sem_of(p, steps - direction, zeros + (0,), 1)
         return pltpu.make_async_remote_copy(
             src_ref=own_at(p, steps, zeros),
-            dst_ref=held[p][2 if direction > 0 else 3].at[slot(steps, ())],
-            send_sem=send_sem.at[p, sem + (0 if direction > 0 else 2)],
-            recv_sem=recv_sem.at[p, sem + (0 if direction > 0 else 2)],
-            device_id=device_at(ranks, direction, ()),
+            dst_ref=held[p][2 if direction > 0 else 3].at[slot(p, steps, ())],
+            send_sem=send_sem.at[sem + (0 if direction > 0 else 2)],
+            recv_sem=recv_sem.at[sem + (0 if direction > 0 else 2)],
+            device_id=places.device(direction, ()),
             device_id_type=MESH,
         )
 
     def chain_arrival(p, steps, direction):
         zeros = (0,) * (len(pieces[p][4]) - 1)
-        sem = sem_of(steps, zeros + (0,), 1) + (0 if direction > 0 else 2)
-        place = held[p][2 if direction > 0 else 3].at[slot(steps, ())]
+        sem = sem_of(p, steps, zeros + (0,), 1) + (0 if direction > 0 else 2)
+        place = held[p][2 if direction > 0 else 3].at[slot(p, steps, ())]
         return pltpu.make_async_remote_copy(
             src_ref=place,
             dst_ref=place,
-            send_sem=send_sem.at[p, sem],
-            recv_sem=recv_sem.at[p, sem],
-            device_id=device_at(ranks, -direction, ()),
+            send_sem=send_sem.at[sem],
+            recv_sem=recv_sem.at[sem],
+            device_id=places.device(-direction, ()),
             device_id_type=MESH,
         )
 
     def add(target, sources):
+        rows = target.shape[0]
+        tile = min(rows, 32)
+
         def step(n, carry):
             part = pl.ds(pl.multiple_of(n * tile, tile), tile)
             total = sources[0][part].astype(F32)
@@ -320,13 +348,18 @@
         lax.fori_loop(0, rows // tile, step, 0)
 
     order = []
-    for p, (_, _, _, outer, dims) in enumerate(pieces):
-        for n, steps in enumerate(chain_steps(ranks, outer)):
-            for bits in all_bits(dims[:-1]):
-                order.append((-level_of(bits), -abs(steps), n, p, steps, bits))
-    order = [entry[3:] for entry in sorted(order)]
+    for array in range(arrays):
+        entries = []
+        for p, (of, _, _, outer, dims) in enumerate(pieces):
+            if of == array:
+                for n, steps in enumerate(chain_steps(ranks, outer)):
+                    for bits in all_bits(dims[:-1]):
+                        entries.append((-level_of(bits), -abs(steps), n, p, steps, bits))
+        for n, entry in enumerate(sorted(entries)):
+            order.append(((n + 1) / len(entries), array, n, entry[3:]))
+    order = [entry[3] for entry in sorted(order)]
     for p, steps, bits in order:
-        here = on_chain(ranks, steps)
+        here = places.exists[steps]
         last = len(pieces[p][4]) - 1
 
         def begin(p=p, steps=steps, bits=bits, last=last):
@@ -336,7 +369,7 @@
         run_if([here], begin)
         started.append(([here], functools.partial(pair_copy, p, steps, bits, last)))
     for p, steps, bits in order:
-        here = on_chain(ranks, steps)
+        here = places.exists[steps]
         dims = pieces[p][4]
         level = level_of(bits)
         own, paired, up, down = held[p]
@@ -346,7 +379,7 @@
             sources = [own_at(p, steps, bits)]
             for n in range(len(dims) - 1, level - 1, -1):
                 pair_copy(p, steps, bits, n).wait_recv()
-                sources.append(paired[n].at[slot(steps, bits[:n])])
+                sources.append(paired[n].at[slot(p, steps, bits[:n])])
             add(own_at(p, steps, bits), sources)
 
         run_if([here], gather_terms)
@@ -362,11 +395,11 @@
             for direction in (1, -1):
                 if steps * direction < 0 or abs(steps) == count - 1:
                     continue
-                behind = on_chain(ranks, -direction)
+                behind = places.exists[-direction]
 
                 def take(p=p, steps=steps, bits=bits, direction=direction):
                     chain_arrival(p, steps, direction).wait_recv()
-                    arrived = held[p][2 if direction > 0 else 3].at[slot(steps, ())]
+                    arrived = held[p][2 if direction > 0 else 3].at[slot(p, steps, ())]
                     add(own_at(p, steps, bits), [own_at(p, steps, bits), arrived])
 
                 run_if([here, behind], take)
@@ -379,110 +412,183 @@
             run_if([here], lambda: send_chain().start())
             started.append(([here], send_chain))
         else:
-            start, width = pieces[p][1:3]
-            begin_column = start - pieces[0][1]
-            add(out_ref.at[:, pl.ds(begin_column, width)], [own_at(p, 0, bits)])
+            array, start, width = pieces[p][:3]
+            columns = pl.ds(start - min(piece[1] for piece in pieces if piece[0] == array), width)
+            add(out_refs[array].at[:, columns], [own_at(p, 0, bits)])
     for conditions, build in started:
         run_if(conditions, lambda: build().wait_send())
 
 
-def scatter_blocks(array, pieces, blocks, ranks, collective_id):
-    rows = array.shape[0] // blocks
-    columns = sum(piece[2] for piece in pieces)
+def scatter_blocks(sources, pieces, blocks, ranks, collective_id):
+    arrays = len(sources)
     count = ranks // 2
+    out_shape = []
+    for n, (source, number) in enumerate(zip(sources, blocks)):
+        columns = sum(piece[2] for piece in pieces if piece[0] == n)
+        out_shape.append(jax.ShapeDtypeStruct((source.shape[0] // number, columns), source.dtype))
     scratch = []
-    for _, _, width, outer, dims in pieces:
+    for array, _, width, outer, dims in pieces:
         chain = count if outer else 1
         sizes = [chain * 2 ** (len(dims) - 1)]
         sizes += [chain * 2**n for n in range(len(dims))]
         sizes += [chain, chain] if outer else [1, 1]
-        scratch += [pltpu.VMEM((size, rows, width), array.dtype) for size in sizes]
-    transfers = ranks * 8 * 2
+        rows = out_shape[array].shape[0]
+        scratch += [pltpu.VMEM((size, rows, width), sources[array].dtype) for size in sizes]
+    transfers = semaphores(ranks, pieces)[-1]
     return pl.pallas_call(
-        functools.partial(scatter_kernel, ranks, pieces),
-        out_shape=jax.ShapeDtypeStruct((rows, columns), array.dtype),
-        in_specs=[pl.BlockSpec(memory_space=pl.ANY)],
-        out_specs=pl.BlockSpec(memory_space=pltpu.VMEM),
+        functools.partial(scatter_kernel, ranks, arrays, pieces),
+        out_shape=tuple(out_shape),
+        in_specs=[pl.BlockSpec(memory_space=pl.ANY)] * arrays,
+        out_specs=(pl.BlockSpec(memory_space=pltpu.VMEM),) * arrays,
         scratch_shapes=[
             *scratch,
-            pltpu.SemaphoreType.DMA((len(pieces), transfers)),
-            pltpu.SemaphoreType.DMA((len(pieces), transfers)),
-            pltpu.SemaphoreType.DMA((len(pieces), transfers)),
+            pltpu.SemaphoreType.DMA((2 * transfers,)),
+            pltpu.SemaphoreType.DMA((2 * transfers,)),
+            pltpu.SemaphoreType.DMA((transfers,)),
         ],
         compiler_params=pltpu.CompilerParams(
             collective_id=collective_id,
             has_side_effects=True,
-            vmem_limit_bytes=56 * 1024 * 1024,
+            vmem_limit_bytes=58 * 1024 * 1024,
         ),
         cost_estimate=pl.CostEstimate(
-            flops=array.shape[0] * columns,
-            bytes_accessed=2 * array.shape[0] * columns,
+            flops=sum(source.size for source in sources),
+            bytes_accessed=sum(2 * source.size for source in sources),
             transcendentals=0,
         ),
-    )(array)
-
-
-def scatter_everywhere(array, ranks, collective_id):
+    )(*sources)
+
+
+def scatter_everywhere(array, ranks, collective_id, beside=None):
     tiles = array.shape[1] // 128
     calls = max(1, ranks // 8)
     results = []
+    other = None
     for call in range(calls):
         first, last = tiles * call // calls, tiles * (call + 1) // calls
         middle = (first + last + 1) // 2
+        dims = ("inner", "side", "core")
+        second = dims if beside is not None else ("side", "inner", "core")
         pieces = (
-            (0, first * 128, (middle - first) * 128, True, ("inner", "side", "core")),
-            (0, middle * 128, (last - middle) * 128, True, ("side", "inner", "core")),
+            (0, first * 128, (middle - first) * 128, True, dims),
+            (0, middle * 128, (last - middle) * 128, True, second),
         )
-        results.append(scatter_blocks(array, pieces, 4 * ranks, ranks, collective_id + call))
-    return results[0] if calls == 1 else jnp.concatenate(results, axis=1)
-
-
-def send_blocks(blocks, ranks):
+        if beside is None or call:
+            (result,) = scatter_blocks([array], pieces, [4 * ranks], ranks, collective_id + call)
+        else:
+            cut = beside.shape[1] // 256 * 128
+            pieces += (
+                (1, 0, cut, True, ("inner",)),
+                (1, cut, beside.shape[1] - cut, True, ("inner",)),
+            )
+            result, other = scatter_blocks(
+                [array, beside], pieces, [4 * ranks, ranks], ranks, collective_id
+            )
+        results.append(result)
+    result = results[0] if calls == 1 else jnp.concatenate(results, axis=1)
+    return (result, other) if beside is not None else result
+
+
+def send_blocks(block_for, ranks):
     own = lax.axis_index("dp")
-    received = []
+    received = [(own, block_for(own))]
     for shift in range(1, ranks):
         target = lax.rem(own + shift, ranks)
         origin = lax.rem(own + ranks - shift, ranks)
-        block = lax.dynamic_index_in_dim(blocks, target, 0, keepdims=True)
-        moved = lax.ppermute(block, "dp", [(j, (j + shift) % ranks) for j in range(ranks)])
-        received.append((origin, moved))
+        pairs = [(j, (j + shift) % ranks) for j in range(ranks)]
+        received.append((origin, lax.ppermute(block_for(target), "dp", pairs)))
     return received
 
 
-def join_blocks(blocks, received):
-    for origin, block in received:
-        blocks = lax.dynamic_update_slice_in_dim(blocks, block, origin, 0)
-    return blocks
-
-
-def tie(value, received, first, last):
+def settle_kernel(width, origin_ref, *refs):
+    block_refs, (in_ref, out_ref, held_ref, load_sem) = refs[:-4], refs[-4:]
+    del origin_ref
+    at = pl.program_id(0)
+    tiles = width // 128
+
+    def load(n):
+        return pltpu.make_async_copy(block_refs[n].at[0], held_ref.at[n], load_sem.at[n])
+
+    @pl.when(at == 0)
+    def _():
+        for n in range(len(block_refs)):
+            load(n).start()
+
+    for n in range(len(block_refs)):
+        pl.when(at == n)(load(n).wait)
+    portion, depth, _ = held_ref.shape[1:]
+    for e in range(portion):
+        for j in range(2):
+            for tile in range(tiles):
+                rows = pl.ds(tile * 2 + j, depth, stride=2 * tiles)
+                start = j * width + tile * 128
+                in_ref[e, rows, :] = held_ref[at, e, :, start : start + 128].astype(F32)
+        out_ref[e] = held_ref[at, e, :, 2 * width :].astype(F32)
+
+
+def settle(sent, owned, width):
+    portions = len(sent)
+    ranks = len(sent[0])
+    blocks = [block for received in sent for _, block in received]
+    origins = jnp.stack([origin for origin, _ in sent[0]]).astype(jnp.int32)
+    portion, depth, _ = blocks[0].shape[1:]
+    in_rows = depth * 2 * width // 128
+
+    def place(step, origins):
+        return origins[lax.rem(step, ranks)] * portions + step // ranks, 0, 0
+
+    return pl.pallas_call(
+        functools.partial(settle_kernel, width),
+        grid_spec=pltpu.PrefetchScalarGridSpec(
+            num_scalar_prefetch=1,
+            grid=(len(blocks),),
+            in_specs=[pl.BlockSpec(memory_space=pl.ANY)] * len(blocks),
+            out_specs=(
+                pl.BlockSpec((portion, in_rows, 128), place),
+                pl.BlockSpec((portion, depth, width), place),
+            ),
+            scratch_shapes=[
+                pltpu.VMEM((len(blocks),) + blocks[0].shape[1:], BF16),
+                pltpu.SemaphoreType.DMA((len(blocks),)),
+            ],
+        ),
+        out_shape=(
+            jax.ShapeDtypeStruct((owned * ranks, in_rows, 128), F32),
+            jax.ShapeDtypeStruct((owned * ranks, depth, width), F32),
+        ),
+        compiler_params=pltpu.CompilerParams(vmem_limit_bytes=40 * 1024 * 1024),
+    )(origins, *blocks)
+
+
+def tie(value, received, part, parts):
+    number = len(received) - 1
+    first, last = 1 + number * part // parts, 1 + number * (part + 1) // parts
     blocks = [block for _, block in received[first:last]]
-    if not blocks:
-        return value, received
     value, blocks = lax.optimization_barrier((value, blocks))
     renewed = [(origin, block) for (origin, _), block in zip(received[first:last], blocks)]
     return value, received[:first] + renewed + received[last:]
 
 
-def expert_kernel(
-    owned,
-    width,
-    rows_ref,
-    pull_ref,
-    position_ref,
-    gate_ref,
-    column_ref,
-    weight_ref,
-    mixture_ref,
-    returned_ref,
-    chosen_ref,
-    pulled_ref,
-    d_gate_up_ref,
-    hidden_ref,
-    place_ref,
-    mixed_ref,
-    back_ref,
-):
+def expert_kernel(ranks, owned, width, added, origin_ref, rows_ref, pull_ref, *refs):
+    position_ref, gate_ref, column_ref, *refs = refs
+    block_refs, refs = refs[:ranks], refs[ranks:]
+    before, refs = refs[: 2 * added], refs[2 * added :]
+    mixture_ref, returned_ref, chosen_ref, pulled_ref, d_gate_up_ref, hidden_ref, *refs = refs
+    place_ref, mixed_ref, back_ref, weight_ref, load_sem = refs
+
+    @pl.when(pl.program_id(0) == 0)
+    def _():
+        loads = [
+            pltpu.make_async_copy(
+                block_refs[n].at[0], weight_ref.at[origin_ref[n]], load_sem.at[n]
+            )
+            for n in range(ranks)
+        ]
+        for load in loads:
+            load.start()
+        for load in loads:
+            load.wait()
+
     group_tokens, features = rows_ref.shape
     chunk = min(features, 512)
     slot = lax.broadcasted_iota(jnp.int32, (CAP, group_tokens), 0)
@@ -528,36 +634,77 @@
         back_ref[e * CAP : (e + 1) * CAP] = lax.dot_general(
             d_gate_up_ref[e, 0], weight_in, last, preferred_element_type=F32
         ).astype(BF16)
-    returned_ref[:, features:] = spread.astype(BF16)
+    def finish(target_ref, number, columns, total):
+        if added:
+            total = total + before[number][:, columns].astype(F32)
+        target_ref[:, columns] = total.astype(BF16)
+
+    finish(returned_ref, 1, slice(features, features + 128), spread)
     for start in range(0, features, chunk):
         columns = slice(start, start + chunk)
-        mixture_ref[:, columns] = lax.dot_general(
-            place_ref[...], mixed_ref[:, columns], first, preferred_element_type=F32
-        ).astype(BF16)
-        returned_ref[:, columns] = lax.dot_general(
-            place_ref[...], back_ref[:, columns], first, preferred_element_type=F32
-        ).astype(BF16)
-
-
-def expert_math(rows, pull, position, gate, column, weights):
+        for number, (target_ref, source_ref) in enumerate(
+            ((mixture_ref, mixed_ref), (returned_ref, back_ref))
+        ):
+            total = lax.dot_general(
+                place_ref[...], source_ref[:, columns], first, preferred_element_type=F32
+            )
+            finish(target_ref, number, columns, total)
+
+
+def expert_math(rows, pull, position, gate, column, received, before, last):
     groups, owned, group_tokens = position.shape
     tokens, features = rows.shape
-    ranks, _, depth, _ = weights.shape
-    width = weights.shape[3] // 3
+    ranks = len(received)
+    depth = features // ranks
+    width = received[0][1].shape[3] // 3
     slots = owned * CAP
-    by_rows = pl.BlockSpec((group_tokens, features), lambda g: (g, 0))
-    by_group = pl.BlockSpec((1, owned, group_tokens), lambda g: (g, 0, 0))
+    origins = jnp.stack([origin for origin, _ in received]).astype(jnp.int32)
+    by_rows = pl.BlockSpec((group_tokens, features), lambda g, _: (g, 0))
+    by_group = pl.BlockSpec((1, owned, group_tokens), lambda g, _: (g, 0, 0))
+    by_returned = pl.BlockSpec((group_tokens, features + 128), lambda g, _: (g, 0))
 
     def by_slots(columns):
-        return pl.BlockSpec((owned, 1, CAP, columns), lambda g: (0, g, 0, 0))
+        return pl.BlockSpec((owned, 1, CAP, columns), lambda g, _: (0, g, 0, 0))
 
     def slot_array(columns):
         return jax.ShapeDtypeStruct((owned, groups, CAP, columns), BF16)
 
+    aliases = {}
+    if before:
+        aliases = {6 + ranks: 0, 7 + ranks: 1}
+    elif last:
+        aliases = {2: 0}
     flops = 2 * groups * slots * features * (4 * group_tokens + 6 * width)
     return pl.pallas_call(
-        functools.partial(expert_kernel, owned, width),
-        grid=(groups,),
+        functools.partial(expert_kernel, ranks, owned, width, 1 if before else 0),
+        grid_spec=pltpu.PrefetchScalarGridSpec(
+            num_scalar_prefetch=1,
+            grid=(groups,),
+            in_specs=[
+                by_rows,
+                by_rows,
+                by_group,
+                by_group,
+                pl.BlockSpec((owned, 128), lambda g, _: (0, 0)),
+            ]
+            + [pl.BlockSpec(memory_space=pl.ANY)] * ranks
+            + ([by_rows, by_returned] if before else []),
+            out_specs=(
+                by_rows,
+                by_returned,
+                by_slots(features),
+                by_slots(features),
+                by_slots(2 * width),
+                by_slots(width),
+            ),
+            scratch_shapes=[
+                pltpu.VMEM((slots, group_tokens), BF16),
+                pltpu.VMEM((slots, features), BF16),
+                pltpu.VMEM((slots, features), BF16),
+                pltpu.VMEM((ranks, owned, depth, 3 * width), BF16),
+                pltpu.SemaphoreType.DMA((ranks,)),
+            ],
+        ),
         out_shape=(
             jax.ShapeDtypeStruct((tokens, features), BF16),
             jax.ShapeDtypeStruct((tokens, features + 128), BF16),
@@ -566,37 +713,23 @@
             slot_array(2 * width),
             slot_array(width),
         ),
-        in_specs=[
-            by_rows,
-            by_rows,
-            by_group,
-            by_group,
-            pl.BlockSpec((owned, 128), lambda g: (0, 0)),
-            pl.BlockSpec(
-                (ranks, owned, depth, 3 * width),
-                lambda g: (0, 0, 0, 0),
-                pipeline_mode=pl.Buffered(1),
-            ),
-        ],
-        out_specs=(
-            by_rows,
-            pl.BlockSpec((group_tokens, features + 128), lambda g: (g, 0)),
-            by_slots(features),
-            by_slots(features),
-            by_slots(2 * width),
-            by_slots(width),
-        ),
-        scratch_shapes=[
-            pltpu.VMEM((slots, group_tokens), BF16),
-            pltpu.VMEM((slots, features), BF16),
-            pltpu.VMEM((slots, features), BF16),
-        ],
-        input_output_aliases={1: 0},
+        input_output_aliases=aliases,
         compiler_params=pltpu.CompilerParams(vmem_limit_bytes=60 * 1024 * 1024),
         cost_estimate=pl.CostEstimate(
-            flops=flops, bytes_accessed=4 * tokens * features * 2 + slots * groups * features * 4, transcendentals=0
+            flops=flops,
+            bytes_accessed=4 * tokens * features * 2 + slots * groups * features * 4,
+            transcendentals=0,
         ),
-    )(rows, pull, position, gate, column, weights)
+    )(
+        origins,
+        rows,
+        pull,
+        position,
+        gate,
+        column,
+        *[block for _, block in received],
+        *before,
+    )
 
 
 def body(
@@ -648,11 +781,14 @@
     small_width = -(-small.size // (depth * 128)) * 128
     small = jnp.pad(small, (0, depth * small_width - small.size)).reshape(depth, small_width)
     own_tokens = by_micro(tokens)
-    sources = [w_qkv[:, 0], w_qkv[:, 1], w_qkv[:, 2], small, w_out, own_tokens]
+    pull_own = by_micro(cotangent)
+    sources = [w_qkv[:, 0], w_qkv[:, 1], w_qkv[:, 2], small, w_out, own_tokens, pull_own]
     pieces = tuple((n, 0, sources[n].shape[1], True, ("inner",)) for n in range(5))
     pieces += ((5, 0, features, False, ("side", "core")),)
-    full_q, full_k, full_v, small_all, full_out, raw_rows = gather_blocks(
-        sources, [ranks] * 5 + [quarters], pieces, ranks, 1
+    half = features // 2
+    pieces += tuple((6, n * half, half, True, ("inner", "side", "core")) for n in range(2))
+    full_q, full_k, full_v, small_all, full_out, raw_rows, pull_all = gather_blocks(
+        sources, [ranks] * 5 + [quarters, ranks * quarters], pieces, ranks, 1
     )
     small_all = small_all.reshape(ranks, depth * small_width)
     ends = [sum(sizes[: n + 1]) for n in range(len(sizes))]
@@ -663,15 +799,20 @@
     all_ids = small_all[:, ends[3] : ends[4]].astype(jnp.int32)
     qk_rows = jnp.transpose(full_qk, (1, 2, 0)).reshape(2, local_width)
 
-    blocks = jnp.concatenate(
-        [
-            expert_in.reshape(ranks, owned, depth, 2 * width),
-            expert_out.reshape(ranks, owned, depth, width),
-        ],
-        axis=3,
-    )
-    blocks, raw_rows = lax.optimization_barrier((blocks, raw_rows))
-    held = send_blocks(blocks, ranks)
+    portions = 2 if owned % 2 == 0 else 1
+    portion = owned // portions
+    raw_rows, expert_in, expert_out = lax.optimization_barrier((raw_rows, expert_in, expert_out))
+
+    def weight_block(number, target):
+        start = target * owned + number * portion
+        part_in = lax.dynamic_slice_in_dim(expert_in, start, portion, 0)
+        part_out = lax.dynamic_slice_in_dim(expert_out, start, portion, 0)
+        joined = jnp.concatenate([part_in.reshape(portion, depth, 2 * width), part_out], axis=2)
+        return joined[None]
+
+    held = [
+        send_blocks(functools.partial(weight_block, number), ranks) for number in range(portions)
+    ]
 
     raw_rows = raw_rows.astype(F32)
     rows_one = (raw_rows * norm_factor(raw_rows) * gain_one).astype(BF16)
@@ -700,19 +841,18 @@
 
     def scatter_quarters(array):
         across = ((0, 0, features, False, ("side", "core")),)
-        return scatter_blocks(array, across, quarters, ranks, 2).astype(F32).reshape(own_shape)
+        (result,) = scatter_blocks([array], across, [quarters], ranks, 2)
+        return result.astype(F32).reshape(own_shape)
 
     attended = scatter_quarters(dot("tf,df->td", head_out, full_out).astype(BF16))
-    attended, held = tie(attended, held, 0, ranks // 4)
+    attended, held[0] = tie(attended, held[0], 0, 2)
     inputs = own_tokens.astype(F32).reshape(own_shape)
     residual = inputs + attended
     factor_two = norm_factor(residual)
     normed_two = (residual * factor_two * gain_two).astype(BF16).reshape(local_tokens, features)
 
     rows_all = gather_everywhere(normed_two, ranks, 3)
-    pull_own = by_micro(cotangent)
-    pull_own, rows_all = lax.optimization_barrier((pull_own, rows_all))
-    pull_all = gather_everywhere(pull_own, ranks, 3)
+    rows_all, held[0] = tie(rows_all, held[0], 1, 2)
     router_probs = softmax_rows(dot("td,de->te", rows_all, full_router))
 
     first = rank * owned
@@ -728,16 +868,35 @@
     gate_own = jnp.swapaxes(gate_own.reshape(ranks, group_tokens, owned), 1, 2)
     lanes = jnp.arange(128, dtype=jnp.int32)
     column = (names[:, None] == lanes).astype(F32)
-    mixture_all, returned_all, chosen, pulled, d_gate_up, hidden = expert_math(
-        rows_all, pull_all, position, gate_own, column, join_blocks(blocks, held)
-    )
-
-    grad_in = dot("egsrk,egsf->rekf", chosen.reshape(owned, ranks, CAP, ranks, depth), d_gate_up)
-    grad_out = dot("egsrk,egsf->rekf", pulled.reshape(owned, ranks, CAP, ranks, depth), hidden)
-    grad_blocks = jnp.concatenate([grad_in.astype(BF16), grad_out.astype(BF16)], axis=3)
-    returned_all, grad_blocks = lax.optimization_barrier((returned_all, grad_blocks))
-    sent = send_blocks(grad_blocks, ranks)
+    before = ()
+    sent = []
+    for number in range(portions):
+        part = slice(number * portion, (number + 1) * portion)
+        mixture_all, returned_all, chosen, pulled, d_gate_up, hidden = expert_math(
+            rows_all,
+            pull_all,
+            position[:, part],
+            gate_own[:, part],
+            column[part],
+            held[number],
+            before,
+            number == portions - 1,
+        )
+        by_depth = (portion, ranks, CAP, ranks, depth)
+        grad_in = dot("egsrk,egsf->rekf", chosen.reshape(by_depth), d_gate_up)
+        grad_out = dot("egsrk,egsf->rekf", pulled.reshape(by_depth), hidden)
+        grad_blocks = jnp.concatenate([grad_in.astype(BF16), grad_out.astype(BF16)], axis=3)
+        returned_all, grad_blocks = lax.optimization_barrier((returned_all, grad_blocks))
+        before = (mixture_all, returned_all)
+
+        def grad_block(grad_blocks, target):
+            return lax.dynamic_index_in_dim(grad_blocks, target, 0, keepdims=True)
+
+        sent.append(send_blocks(functools.partial(grad_block, grad_blocks), ranks))
+    if portions > 1:
+        returned_all, sent[0] = tie(returned_all, sent[0], 0, 2)
     returned_own = scatter_everywhere(returned_all, ranks, 4)
+    returned_own, sent[0] = tie(returned_own, sent[0], portions - 1, portions)
 
     returned_f = returned_own[:, :features].astype(F32)
     d_probs = returned_own[:, features : features + experts].astype(F32)
@@ -756,7 +915,7 @@
     (rows_back,) = gather_blocks(
         [d_attended], [quarters], ((0, 0, features, False, ("side", "core")),), ranks, 8
     )
-    rows_back, sent = tie(rows_back, sent, 0, ranks // 4)
+    rows_back, sent[-1] = tie(rows_back, sent[-1], 0, 4)
     d_heads = to_sequences(dot("td,df->tf", rows_back, full_out).astype(BF16)).reshape(heads_shape)
     grad_w_out = dot("td,tf->df", rows_back, head_out)
     d_weights = dot("mqhc,mkhc->mhqk", d_heads, value_heads)
@@ -790,6 +949,7 @@
     d_q = from_sequences(d_query_raw.astype(BF16))
     d_k = from_sequences(d_key_raw.astype(BF16))
     d_v = from_sequences(d_values)
+    d_q, sent[-1] = tie(d_q, sent[-1], 1, 4)
     d_normed_one = scatter_quarters(
         (
             dot("tf,df->td", d_q, full_q)
@@ -811,24 +971,19 @@
     grads = [dot("td,tf->df", rows_one, part).astype(BF16) for part in (d_q, d_k, d_v)]
     grads += [grad_w_out.astype(BF16), small_grads.reshape(features, slim).astype(BF16)]
     grads = jnp.concatenate(grads, axis=1)
-    cut = 2 * local_width
-    pieces = (
-        (0, 0, cut, True, ("inner",)),
-        (0, cut, grads.shape[1] - cut, True, ("inner",)),
-    )
-    grads_own = scatter_blocks(grads, pieces, ranks, ranks, 9).astype(F32)
+    grads, sent[-1] = tie(grads, sent[-1], 2, 4)
+    mixture_own, grads_own = scatter_everywhere(mixture_all, ranks, 10, grads)
+    grads_own = grads_own.astype(F32)
     grad_qkv_own = grads_own[:, : 3 * local_width].reshape(depth, 3, local_width)
     grad_out_own = grads_own[:, 3 * local_width : 4 * local_width]
     small_own = grads_own[:, 4 * local_width :].reshape(-1)
     shared_own = lax.psum(small_own[:shared], "tensor")
     grad_qk_own = small_own[shared : shared + qk_gain.size].reshape(qk_gain.shape)
 
-    mixture_all, _ = lax.optimization_barrier((mixture_all, rows_back))
-    mixture_own = scatter_everywhere(mixture_all, ranks, 10)
     layer_out = (residual + mixture_own.astype(F32).reshape(own_shape)).astype(BF16)
-    expert_grads = join_blocks(grad_blocks, sent).astype(F32).reshape(experts, depth, 3 * width)
-    grad_expert_in = expert_grads[:, :, : 2 * width].reshape(experts, depth, 2, width)
-    grad_expert_out = expert_grads[:, :, 2 * width :]
+    grad_expert_in, grad_expert_out = settle(sent, owned, width)
+    grad_expert_in = grad_expert_in.reshape(experts, depth, width // 128, 2, 128)
+    grad_expert_in = jnp.swapaxes(grad_expert_in, 2, 3).reshape(experts, depth, 2, width)
     return (
         jnp.swapaxes(layer_out, 0, 1),
         jnp.swapaxes(grad_tokens, 0, 1),

time: 1540 us -> 1170 us (0.76)
  Pallas kernels: 1130 us -> 759 us
  local copies, waits for them, and re-layouts: 187 us -> 131 us
  waiting for transfers between devices: 2.97 us -> 37.7 us
  starting transfers between devices: 30 us -> 50 us
    pallas_call x4 -> x3, Pallas kernels: 503 us -> 292 us  [gather_blocks(): pl.pallas_call(functools.partial(gather_kernel, ranks, arrays, pieces), o...]
    pallas_call x6 -> x7, Pallas kernels: 631 us -> 466 us  [the longest x4 313 us: scatter_blocks(): pl.pallas_call(functools.partial(scatter_kernel, ranks, arrays, pieces),...]
    ppermute x14 -> x28, waiting for transfers between devices: 2.97 us -> 37.7 us  [send_blocks(): received.append((origin, lax.ppermute(block_for(target), 'dp', pairs)))]
    dynamic_update_slice x12 -> x0, local copies, waits for them, and re-layouts: 31.8 us -> none  [join_blocks(): blocks = lax.dynamic_update_slice_in_dim(blocks, block, origin, 0)]
    reshape x3 -> x16, local copies, waits for them, and re-layouts: 51.7 us -> 21.1 us  [weight_block(): part_in.reshape(portion, depth, 2 * width)]
    ppermute x14 -> x28, starting transfers between devices: 30 us -> 50 us  [send_blocks(): received.append((origin, lax.ppermute(block_for(target), 'dp', pairs)))]
    broadcast_in_dim x0 -> x15, other arithmetic: none -> 18.9 us  [weight_block(): return joined[None]]
    slice x2 -> x3, local copies, waits for them, and re-layouts: 19.3 us -> 1.92 us  [the longest x1 0.67 us: body(): gate_own[:, part]]
  transfers between devices with their start and end apart: 14 -> 28, of which waited for: 1 -> 2; matrix products, arithmetic and copies ran while one was open for 8% -> 22% of each run, Pallas kernels for 52% -> 49%
where the time goes in v3:
time: 1170 us; the launch traced here: 1160 us
  Pallas kernels  759 us (65%)
  local copies, waits for them, and re-layouts  131 us (11%)
  matrix products  107 us (9%)
  other arithmetic  52.6 us (4%)
  starting transfers between devices  50 us (4%)
  waiting for transfers between devices  37.7 us (3%)
  blocking collectives  22.9 us (2%)
    pallas_call x4, Pallas kernels, scatter_blocks(): pl.pallas_call(functools.partial(scatter_kernel, ranks, arrays, pieces),...  313 us
    pallas_call x3, Pallas kernels, gather_blocks(): pl.pallas_call(functools.partial(gather_kernel, ranks, arrays, pieces), o...  292 us
    pallas_call x2, Pallas kernels, expert_math(): pl.pallas_call(functools.partial(expert_kernel, ranks, owned, width, 1 if...  142 us
    dot_general x26, matrix products, dot(): return jnp.einsum(spec, left, right, preferred_element_type=F32)  107 us
    ppermute x28, starting transfers between devices, send_blocks(): received.append((origin, lax.ppermute(block_for(target), 'dp', pairs)))  50 us
    ppermute x28, waiting for transfers between devices, send_blocks(): received.append((origin, lax.ppermute(block_for(target), 'dp', pairs)))  37.7 us
  transfers between devices with their start and end apart: 28, of which 2 were waited for; matrix products, arithmetic and copies ran while one was open for 22% of the time, Pallas kernels for 49%

profile of v3, /device:TPU:0, one launch (start us, length us, event | category | flops | bytes accessed | tf_op | source)
XLA Modules:
  0.0 1162.9 jit_solution(9383430981148032087)
XLA Ops:
  10.4 171.7 %shard_map.195 = (bf16[2048,512]{1,0:T(8,128)(2,1)}, bf16[2048,512]{1,0:T(8,128)(2,1)}, bf16[2048,512]{1,0:T(8,128)(2,1)}, bf16[2048,128]{1,0:T(8,128)(2,1)}, bf...) custom-call(bf16[256,512]{1,0:T(8,128)(2,1)} %get-tuple-element.233.refs_0_, ...), custom_call_target="tpu_custom_call" | custom-call | bytes 27787264 | tf_op jit(solution)/shard_map/pallas_call | solution.py:221
  182.1 4.4 constant_dynamic-slice_fusion.16
  188.2 7.8 constant_dynamic-slice_fusion.17
  203.0 2.3 collective-permute-start.2
  221.0 3.1 convolution_convert_fusion.7
  225.1 3.5 fusion.100
  230.9 3.5 fusion.102
  237.7 2.5 reshape.408
  244.7 4.5 reshape.469
  249.2 3.8 copy.299
  254.8 6.3 all-reduce.3
  265.6 2.5 fusion.53
  269.4 4.2 convolution_convert_fusion.4.refs_0_
  273.6 16.9 %shard_map.196 = bf16[128,2048]{1,0:T(8,128)(2,1)} custom-call(bf16[512,2048]{1,0:T(8,128)(2,1)} %convolution_convert_fusion.4.refs_0_), custom_call_target="tpu_custom_call" | custom-call | flops 1048576 | bytes 2097152 | tf_op jit(solution)/shard_map/pallas_call | solution.py:438
  294.0 2.2 reshape.431
  296.2 2.2 reshape.430
  305.6 2.2 reshape.421
  310.0 2.2 maximum_bitcast_fusion.14
  331.2 103.3 %shard_map.197.rows_ref = bf16[4096,2048]{1,0:T(8,128)(2,1)} custom-call(bf16[128,2048]{1,0:T(8,128)(2,1)} %bitcast.267), custom_call_target="tpu_custom_call" | custom-call | bytes 16777216 | tf_op jit(solution)/shard_map/pallas_call | solution.py:221
  434.8 2.9 collective-permute-start.9
  437.7 2.5 collective-permute-start.10
  441.5 10.8 fusion.111
  454.2 2.3 fusion.41
  459.1 69.7 %shard_map.198 = (bf16[4096,2048]{1,0:T(8,128)(2,1)}, bf16[4096,2176]{1,0:T(8,128)(2,1)}, bf16[2,8,176,2048]{3,2,1,0:T(8,128)(2,1)}, bf16[2,8,176,2048]{3,2,1,0:...) custom-call(s32[8]{0:T(128)} %stack.62.origin_ref, ...), custom_call_target="tpu_custom_call" | custom-call | flops 41339060224 | bytes 90177536 | tf_op jit(solution)/shard_map/pallas_call | solution.py:678
  528.8 12.0 %fusion.18 = bf16[8,2,256,512]{3,2,1,0:T(8,128)(2,1)} fusion(bf16[2,8,22,8,8,256]{5,4,3,2,1,0:T(8,128)(2,1)} %bitcast.312, bf16[2,8,176,512]{3,2,1,0:T(8,128)(2,1)} %get-tuple-element.87), kind=kOutput, calls=%fused_computation.24 | convolution fusion | flops 5907677184 | bytes 18612224 | tf_op jit(solution)/shard_map/egsrk,egsf->rekf/dot_general | solution.py:38
  544.0 9.1 fusion.43
  553.0 2.7 pad_maximum_fusion
  555.7 2.4 constant_dynamic-slice_fusion.3
  558.5 2.7 collective-permute-start.19
  563.3 14.3 %collective-permute-done.13.refs_10_ = bf16[1,2,256,768]{3,2,1,0:T(8,128)(2,1)} collective-permute-done((bf16[1,2,256,768]{3,2,1,0:T(8,128)(2,1)}, bf16[1,2,256,768]{3,2,1,0:T(8,128)(2,1)}, u32[]{:S(2)}, u32[]{:S(2)}) %collective-permute-start.13) | collective-permute-done | bytes 786464 | tf_op jit(solution)/shard_map/ppermute | solution.py:499
  577.6 2.4 collective-permute-start.14
  580.0 71.9 %shard_map.199 = (bf16[4096,2048]{1,0:T(8,128)(2,1)}, bf16[4096,2176]{1,0:T(8,128)(2,1)}, bf16[2,8,176,2048]{3,2,1,0:T(8,128)(2,1)}, bf16[2,8,176,2048]{3,2,1,0:...) custom-call(s32[8]{0:T(128)} %stack.62.origin_ref, ...), custom_call_target="tpu_custom_call", output_to_operand_aliasing={{0}: (14, {}), {1}: (15, {})} | custom-call | flops 41339060224 | bytes 90177536 | tf_op jit(solution)/shard_map/pallas_call | solution.py:678
  651.9 12.3 %fusion.19 = bf16[8,2,256,512]{3,2,1,0:T(8,128)(2,1)} fusion(bf16[2,8,22,8,8,256]{5,4,3,2,1,0:T(8,128)(2,1)} %bitcast.311, bf16[2,8,176,512]{3,2,1,0:T(8,128)(2,1)} %get-tuple-element.94), kind=kOutput, calls=%fused_computation.25 | convolution fusion | flops 5907677184 | bytes 18612224 | tf_op jit(solution)/shard_map/egsrk,egsf->rekf/dot_general | solution.py:38
  664.3 10.4 fusion.46
  674.7 2.3 collective-permute-start.17
  677.0 3.3 pad_maximum_fusion.1
  680.4 2.5 constant_dynamic-slice_fusion
  682.9 2.5 collective-permute-start.21
  686.0 117.1 %shard_map.200 = bf16[128,2176]{1,0:T(8,128)(2,1)} custom-call(bf16[4096,2176]{1,0:T(8,128)(2,1)} %get-tuple-element.100.refs_0_), custom_call_target="tpu_custom_call" | custom-call | flops 8912896 | bytes 17825792 | tf_op jit(solution)/shard_map/pallas_call | solution.py:438
  803.1 10.2 collective-permute-start.27
  813.4 2.9 collective-permute-start.23
  820.7 17.3 %shard_map.201 = bf16[512,2048]{1,0:T(8,128)(2,1)} custom-call(bf16[128,2048]{1,0:T(8,128)(2,1)} %bitcast.284), custom_call_target="tpu_custom_call" | custom-call | bytes 2097152 | tf_op jit(solution)/shard_map/pallas_call | solution.py:221
  838.1 2.2 collective-permute-start.22
  840.2 3.5 convolution_convert_fusion.6
  848.6 3.4 fusion.54
  852.0 2.5 multiply_reduce_fusion
  869.4 2.5 copy.324
  872.0 2.6 reshape.443
  874.6 5.7 all-reduce.2
  883.0 2.5 copy.318
  885.5 2.6 reshape.441
  890.2 23.3 %collective-permute-done.23.refs_11_ = bf16[1,2,256,768]{3,2,1,0:T(8,128)(2,1)} collective-permute-done((bf16[1,2,256,768]{3,2,1,0:T(8,128)(2,1)}, bf16[1,2,256,768]{3,2,1,0:T(8,128)(2,1)}, u32[]{:S(2)}, u32[]{:S(2)}) %collective-permute-start.23) | collective-permute-done | bytes 786464 | tf_op jit(solution)/shard_map/ppermute | solution.py:499
  916.9 3.0 fusion.27
  919.9 2.6 add_convert_fusion.refs_0_
  922.5 16.9 %shard_map.202 = bf16[128,2048]{1,0:T(8,128)(2,1)} custom-call(bf16[512,2048]{1,0:T(8,128)(2,1)} %add_convert_fusion.refs_0_), custom_call_target="tpu_custom_call" | custom-call | flops 1048576 | bytes 2097152 | tf_op jit(solution)/shard_map/pallas_call | solution.py:438
  940.8 4.6 fusion.26
  946.3 2.8 fusion.25
  951.2 4.5 fusion.24
  956.6 161.6 %shard_map.203 = (bf16[128,2048]{1,0:T(8,128)(2,1)}, bf16[256,2176]{1,0:T(8,128)(2,1)}) custom-call(bf16[4096,2048]{1,0:T(8,128)(2,1)} %get-tuple-element.92.refs_0_, bf16[2048,2176]{1,0:T(8,128)(2,1)} %constant_dynamic-update-slice_fusion.1.refs_1_), custom_call_target="tpu_custom_call" | custom-call | flops 12845056 | bytes 25690112 | tf_op jit(solution)/shard_map/pallas_call | solution.py:438
  1120.1 2.5 slice.135
  1128.5 3.0 copy.336
  1131.5 3.0 copy.340
  1135.3 10.9 psum.39
  1150.2 12.4 %shard_map.204 = (f32[32,1024,128]{2,1,0:T(8,128)}, f32[32,256,256]{2,1,0:T(8,128)}) custom-call(s32[8]{0:T(128)S(1)} %copy-done.2, bf16[1,2,256,768]{3,2,1,0:T(8,128)(2,1)S(1)} %get-tuple-element.208.refs_0_, bf16[1,2,256,768]{3,2,1,0:T(8,128)(2,1)} %collective-permute-done.14.refs_1_, bf16[1,2,256,768]{3,2,1,0:T(8,128)(2,1)} %collective-permute-done.15.refs_2_, ...), custom_call_target="tpu_custom_call" | custom-call | tf_op jit(solution)/shard_map/pallas_call | solution.py:540
  (384 shorter events, 146.4 us)
Async XLA Ops:
  0.6 7.9 copy-start.18
  0.7 8.8 copy-start.58
  182.1 6.1 copy-start.16
  198.2 126.5 %collective-permute-start = (bf16[1,2,256,768]{3,2,1,0:T(8,128)(2,1)}, bf16[1,2,256,768]{3,2,1,0:T(8,128)(2,1)}, u32[]{:S(2)}, u32[]{:S(2)}) collective-permute-start(bf16[1,2,256,768]{3,2,1,0:T(8,128)(2,1)} %maximum_bitcast_fusion), channel_id=1, source_target_pairs={{0,4},{4,8},{8,12},{12,16},{16,20},{20,24},{24,28},{28,0},{1,5},{5... | collective-permute-start | bytes 2359304 | tf_op jit(solution)/shard_map/ppermute | solution.py:499
  201.6 125.1 %collective-permute-start.1 = (bf16[1,2,256,768]{3,2,1,0:T(8,128)(2,1)}, bf16[1,2,256,768]{3,2,1,0:T(8,128)(2,1)}, u32[]{:S(2)}, u32[]{:S(2)}) collective-permute-start(bf16[1,2,256,768]{3,2,1,0:T(8,128)(2,1)} %maximum_bitcast_fusion.1), channel_id=1, source_target_pairs={{0,8},{4,12},{8,16},{12,20},{16,24},{20,28},{24,0},{28,4},{1,9},{5... | collective-permute-start | bytes 2359304 | tf_op jit(solution)/shard_map/ppermute | solution.py:499
  203.0 124.3 %collective-permute-start.2 = (bf16[1,2,256,768]{3,2,1,0:T(8,128)(2,1)}, bf16[1,2,256,768]{3,2,1,0:T(8,128)(2,1)}, u32[]{:S(2)}, u32[]{:S(2)}) collective-permute-start(bf16[1,2,256,768]{3,2,1,0:T(8,128)(2,1)} %maximum_bitcast_fusion.2), channel_id=1, source_target_pairs={{0,12},{4,16},{8,20},{12,24},{16,28},{20,0},{24,4},{28,8},{1,13},{... | collective-permute-start | bytes 2359304 | tf_op jit(solution)/shard_map/ppermute | solution.py:499
  206.6 227.9 %collective-permute-start.3 = (bf16[1,2,256,768]{3,2,1,0:T(8,128)(2,1)}, bf16[1,2,256,768]{3,2,1,0:T(8,128)(2,1)}, u32[]{:S(2)}, u32[]{:S(2)}) collective-permute-start(bf16[1,2,256,768]{3,2,1,0:T(8,128)(2,1)} %maximum_bitcast_fusion.3), channel_id=1, source_target_pairs={{0,16},{4,20},{8,24},{12,28},{16,0},{20,4},{24,8},{28,12},{1,17},{... | collective-permute-start | bytes 2359304 | tf_op jit(solution)/shard_map/ppermute | solution.py:499
  208.1 8.8 copy-start.33
  211.5 223.3 %collective-permute-start.4 = (bf16[1,2,256,768]{3,2,1,0:T(8,128)(2,1)}, bf16[1,2,256,768]{3,2,1,0:T(8,128)(2,1)}, u32[]{:S(2)}, u32[]{:S(2)}) collective-permute-start(bf16[1,2,256,768]{3,2,1,0:T(8,128)(2,1)} %maximum_bitcast_fusion.4), channel_id=1, source_target_pairs={{0,20},{4,24},{8,28},{12,0},{16,4},{20,8},{24,12},{28,16},{1,21},{... | collective-permute-start | bytes 2359304 | tf_op jit(solution)/shard_map/ppermute | solution.py:499
  218.0 112.3 %copy-start.68 = (f32[1,2,8,128]{3,1,2,0:T(2,128)}, f32[1,2,8,128]{3,1,2,0:T(2,128)S(1)}, u32[]{:S(2)}) copy-start(f32[1,2,8,128]{3,1,2,0:T(2,128)S(1)} %copy.378) | copy-start | bytes 24580
  219.1 43.8 %copy-start.76 = (f32[4,128]{1,0:T(4,128)}, f32[4,128]{1,0:T(4,128)S(1)}, u32[]{:S(2)}) copy-start(f32[4,128]{1,0:T(4,128)S(1)} %copy.289) | copy-start | bytes 6148
  219.7 43.1 %copy-start.78 = (f32[4,128]{1,0:T(4,128)}, f32[4,128]{1,0:T(4,128)S(1)}, u32[]{:S(2)}) copy-start(f32[4,128]{1,0:T(4,128)S(1)} %copy.292) | copy-start | bytes 6148
  221.0 220.5 %copy-start.21 = (bf16[2048,32]{1,0:T(8,128)(2,1)}, bf16[2048,32]{1,0:T(8,128)(2,1)S(1)}, u32[]{:S(2)}) copy-start(bf16[2048,32]{1,0:T(8,128)(2,1)S(1)} %reshape.423) | copy-start | bytes 393220
  241.8 21.0 %copy-start.6 = (f32[2,256,4,128]{1,3,2,0:T(8,128)}, f32[2,256,4,128]{1,3,2,0:T(8,128)S(1)}, u32[]{:S(2)}) copy-start(f32[2,256,4,128]{1,3,2,0:T(8,128)S(1)} %copy.288) | copy-start | bytes 3145732
  244.7 18.2 %copy-start.8 = (f32[2,256,4,128]{1,3,2,0:T(8,128)}, f32[2,256,4,128]{1,3,2,0:T(8,128)S(1)}, u32[]{:S(2)}) copy-start(f32[2,256,4,128]{1,3,2,0:T(8,128)S(1)} %copy.291) | copy-start | bytes 3145732
  249.2 5.6 copy-start.82
  249.2 5.6 copy-start.83
  273.6 18.1 %copy-start.45 = (bf16[2,256,2,256]{3,2,1,0:T(2,128)(2,1)S(1)}, bf16[2,256,2,256]{3,2,1,0:T(2,128)(2,1)}, u32[]{:S(2)}) copy-start(bf16[2,256,2,256]{3,2,1,0:T(2,128)(2,1)} %get-tuple-element.184) | copy-start | bytes 1572868
  273.6 19.2 %copy-start.44 = (bf16[2,256,2,256]{3,2,1,0:T(2,128)(2,1)S(1)}, bf16[2,256,2,256]{3,2,1,0:T(2,128)(2,1)}, u32[]{:S(2)}) copy-start(bf16[2,256,2,256]{3,2,1,0:T(2,128)(2,1)} %get-tuple-element.185) | copy-start | bytes 1572868
  292.8 7.8 copy-start.43
  294.0 7.7 copy-start.42
  324.7 113.0 %collective-permute-start.5 = (bf16[1,2,256,768]{3,2,1,0:T(8,128)(2,1)}, bf16[1,2,256,768]{3,2,1,0:T(8,128)(2,1)}, u32[]{:S(2)}, u32[]{:S(2)}) collective-permute-start(bf16[1,2,256,768]{3,2,1,0:T(8,128)(2,1)} %maximum_bitcast_fusion.5), channel_id=1, source_target_pairs={{0,24},{4,28},{8,0},{12,4},{16,8},{20,12},{24,16},{28,20},{1,25},{... | collective-permute-start | bytes 2359304 | tf_op jit(solution)/shard_map/ppermute | solution.py:499
  326.7 113.4 %collective-permute-start.6 = (bf16[1,2,256,768]{3,2,1,0:T(8,128)(2,1)}, bf16[1,2,256,768]{3,2,1,0:T(8,128)(2,1)}, u32[]{:S(2)}, u32[]{:S(2)}) collective-permute-start(bf16[1,2,256,768]{3,2,1,0:T(8,128)(2,1)} %maximum_bitcast_fusion.6), channel_id=1, source_target_pairs={{0,28},{4,0},{8,4},{12,8},{16,12},{20,16},{24,20},{28,24},{1,29},{... | collective-permute-start | bytes 2359304 | tf_op jit(solution)/shard_map/ppermute | solution.py:499
  327.3 213.6 %collective-permute-start.7 = (bf16[1,2,256,768]{3,2,1,0:T(8,128)(2,1)}, bf16[1,2,256,768]{3,2,1,0:T(8,128)(2,1)}, u32[]{:S(2)}, u32[]{:S(2)}) collective-permute-start(bf16[1,2,256,768]{3,2,1,0:T(8,128)(2,1)} %maximum_bitcast_fusion.8), channel_id=1, source_target_pairs={{0,4},{4,8},{8,12},{12,16},{16,20},{20,24},{24,28},{28,0},{1,5},{5... | collective-permute-start | bytes 2359304 | tf_op jit(solution)/shard_map/ppermute | solution.py:499
  329.7 104.8 %copy-start.3 = (f32[2,64,2048]{2,1,0:T(8,128)}, f32[2,64,2048]{2,1,0:T(8,128)S(1)}, u32[]{:S(2)}) copy-start(f32[2,64,2048]{2,1,0:T(8,128)S(1)} %get-tuple-element.183) | copy-start | bytes 3145732
  330.3 104.2 %copy-start.80 = (f32[2,64]{1,0:T(2,128)}, f32[2,64]{1,0:T(2,128)S(1)}, u32[]{:S(2)}) copy-start(f32[2,64]{1,0:T(2,128)S(1)} %get-tuple-element.255) | copy-start | bytes 1540
  434.5 107.9 %collective-permute-start.8 = (bf16[1,2,256,768]{3,2,1,0:T(8,128)(2,1)}, bf16[1,2,256,768]{3,2,1,0:T(8,128)(2,1)}, u32[]{:S(2)}, u32[]{:S(2)}) collective-permute-start(bf16[1,2,256,768]{3,2,1,0:T(8,128)(2,1)} %maximum_bitcast_fusion.9), channel_id=1, source_target_pairs={{0,8},{4,12},{8,16},{12,20},{16,24},{20,28},{24,0},{28,4},{1,9},{5... | collective-permute-start | bytes 2359304 | tf_op jit(solution)/shard_map/ppermute | solution.py:499
  434.8 123.3 %collective-permute-start.9 = (bf16[1,2,256,768]{3,2,1,0:T(8,128)(2,1)}, bf16[1,2,256,768]{3,2,1,0:T(8,128)(2,1)}, u32[]{:S(2)}, u32[]{:S(2)}) collective-permute-start(bf16[1,2,256,768]{3,2,1,0:T(8,128)(2,1)} %maximum_bitcast_fusion.10), channel_id=1, source_target_pairs={{0,12},{4,16},{8,20},{12,24},{16,28},{20,0},{24,4},{28,8},{1,13},{... | collective-permute-start | bytes 2359304 | tf_op jit(solution)/shard_map/ppermute | solution.py:499
  437.7 120.8 %collective-permute-start.10 = (bf16[1,2,256,768]{3,2,1,0:T(8,128)(2,1)}, bf16[1,2,256,768]{3,2,1,0:T(8,128)(2,1)}, u32[]{:S(2)}, u32[]{:S(2)}) collective-permute-start(bf16[1,2,256,768]{3,2,1,0:T(8,128)(2,1)} %maximum_bitcast_fusion.11), channel_id=1, source_target_pairs={{0,16},{4,20},{8,24},{12,28},{16,0},{20,4},{24,8},{28,12},{1,17},{... | collective-permute-start | bytes 2359304 | tf_op jit(solution)/shard_map/ppermute | solution.py:499
  440.2 121.0 %collective-permute-start.11 = (bf16[1,2,256,768]{3,2,1,0:T(8,128)(2,1)}, bf16[1,2,256,768]{3,2,1,0:T(8,128)(2,1)}, u32[]{:S(2)}, u32[]{:S(2)}) collective-permute-start(bf16[1,2,256,768]{3,2,1,0:T(8,128)(2,1)} %maximum_bitcast_fusion.12), channel_id=1, source_target_pairs={{0,20},{4,24},{8,28},{12,0},{16,4},{20,8},{24,12},{28,16},{1,21},{... | collective-permute-start | bytes 2359304 | tf_op jit(solution)/shard_map/ppermute | solution.py:499
  528.8 15.1 %copy-start.95 = (bf16[2,8,176,256]{3,2,1,0:T(8,128)(2,1)S(1)}, bf16[2,8,176,256]{3,2,1,0:T(8,128)(2,1)}, u32[]{:S(2)}) copy-start(bf16[2,8,176,256]{3,2,1,0:T(8,128)(2,1)} %get-tuple-element.89) | copy-start | bytes 4325380
  540.9 20.8 %collective-permute-start.12 = (bf16[1,2,256,768]{3,2,1,0:T(8,128)(2,1)}, bf16[1,2,256,768]{3,2,1,0:T(8,128)(2,1)}, u32[]{:S(2)}, u32[]{:S(2)}) collective-permute-start(bf16[1,2,256,768]{3,2,1,0:T(8,128)(2,1)} %maximum_bitcast_fusion.13), channel_id=1, source_target_pairs={{0,24},{4,28},{8,0},{12,4},{16,8},{20,12},{24,16},{28,20},{1,25},{... | collective-permute-start | bytes 2359304 | tf_op jit(solution)/shard_map/ppermute | solution.py:499
  542.4 35.2 %collective-permute-start.13 = (bf16[1,2,256,768]{3,2,1,0:T(8,128)(2,1)}, bf16[1,2,256,768]{3,2,1,0:T(8,128)(2,1)}, u32[]{:S(2)}, u32[]{:S(2)}) collective-permute-start(bf16[1,2,256,768]{3,2,1,0:T(8,128)(2,1)} %maximum_bitcast_fusion.14), channel_id=1, source_target_pairs={{0,28},{4,0},{8,4},{12,8},{16,12},{20,16},{24,20},{28,24},{1,29},{... | collective-permute-start | bytes 2359304 | tf_op jit(solution)/shard_map/ppermute | solution.py:499
  558.2 244.9 %collective-permute-start.20 = (bf16[1,2,256,768]{3,2,1,0:T(8,128)(2,1)}, bf16[1,2,256,768]{3,2,1,0:T(8,128)(2,1)S(1)}, u32[]{:S(2)}, u32[]{:S(2)}) collective-permute-start(bf16[1,2,256,768]{3,2,1,0:T(8,128)(2,1)} %get-tuple-element.209), channel_id=1, source_target_pairs={{0,28},{4,0},{8,4},{12,8},{16,12},{20,16},{24,20},{28,24},{1,29},{... | collective-permute-start | bytes 2359304 | tf_op jit(solution)/shard_map/ppermute | solution.py:499
  558.5 254.9 %collective-permute-start.19 = (bf16[1,2,256,768]{3,2,1,0:T(8,128)(2,1)}, bf16[1,2,256,768]{3,2,1,0:T(8,128)(2,1)S(1)}, u32[]{:S(2)}, u32[]{:S(2)}) collective-permute-start(bf16[1,2,256,768]{3,2,1,0:T(8,128)(2,1)} %get-tuple-element.210), channel_id=1, source_target_pairs={{0,24},{4,28},{8,0},{12,4},{16,8},{20,12},{24,16},{28,20},{1,25},{... | collective-permute-start | bytes 2359304 | tf_op jit(solution)/shard_map/ppermute | solution.py:499
  561.1 113.5 %collective-permute-start.16 = (bf16[1,2,256,768]{3,2,1,0:T(8,128)(2,1)}, bf16[1,2,256,768]{3,2,1,0:T(8,128)(2,1)S(1)}, u32[]{:S(2)}, u32[]{:S(2)}) collective-permute-start(bf16[1,2,256,768]{3,2,1,0:T(8,128)(2,1)} %get-tuple-element.213), channel_id=1, source_target_pairs={{0,12},{4,16},{8,20},{12,24},{16,28},{20,0},{24,4},{28,8},{1,13},{... | collective-permute-start | bytes 2359304 | tf_op jit(solution)/shard_map/ppermute | solution.py:499
  561.7 113.0 %collective-permute-start.15 = (bf16[1,2,256,768]{3,2,1,0:T(8,128)(2,1)}, bf16[1,2,256,768]{3,2,1,0:T(8,128)(2,1)}, u32[]{:S(2)}, u32[]{:S(2)}) collective-permute-start(bf16[1,2,256,768]{3,2,1,0:T(8,128)(2,1)} %get-tuple-element.214), channel_id=1, source_target_pairs={{0,8},{4,12},{8,16},{12,20},{16,24},{20,28},{24,0},{28,4},{1,9},{5... | collective-permute-start | bytes 2359304 | tf_op jit(solution)/shard_map/ppermute | solution.py:499
  577.6 105.3 %collective-permute-start.14 = (bf16[1,2,256,768]{3,2,1,0:T(8,128)(2,1)}, bf16[1,2,256,768]{3,2,1,0:T(8,128)(2,1)}, u32[]{:S(2)}, u32[]{:S(2)}) collective-permute-start(bf16[1,2,256,768]{3,2,1,0:T(8,128)(2,1)} %get-tuple-element.215), channel_id=1, source_target_pairs={{0,4},{4,8},{8,12},{12,16},{16,20},{20,24},{24,28},{28,0},{1,5},{5... | collective-permute-start | bytes 2359304 | tf_op jit(solution)/shard_map/ppermute | solution.py:499
  651.9 12.3 %copy-start.96 = (bf16[2,8,176,256]{3,2,1,0:T(8,128)(2,1)S(1)}, bf16[2,8,176,256]{3,2,1,0:T(8,128)(2,1)}, u32[]{:S(2)}) copy-start(bf16[2,8,176,256]{3,2,1,0:T(8,128)(2,1)} %get-tuple-element.96) | copy-start | bytes 4325380
  674.7 5.7 copy-start
  674.7 138.7 %collective-permute-start.18 = (bf16[1,2,256,768]{3,2,1,0:T(8,128)(2,1)}, bf16[1,2,256,768]{3,2,1,0:T(8,128)(2,1)}, u32[]{:S(2)}, u32[]{:S(2)}) collective-permute-start(bf16[1,2,256,768]{3,2,1,0:T(8,128)(2,1)} %get-tuple-element.211), channel_id=1, source_target_pairs={{0,20},{4,24},{8,28},{12,0},{16,4},{20,8},{24,12},{28,16},{1,21},{... | collective-permute-start | bytes 2359304 | tf_op jit(solution)/shard_map/ppermute | solution.py:499
  674.7 138.8 %collective-permute-start.17 = (bf16[1,2,256,768]{3,2,1,0:T(8,128)(2,1)}, bf16[1,2,256,768]{3,2,1,0:T(8,128)(2,1)}, u32[]{:S(2)}, u32[]{:S(2)}) collective-permute-start(bf16[1,2,256,768]{3,2,1,0:T(8,128)(2,1)} %get-tuple-element.212), channel_id=1, source_target_pairs={{0,16},{4,20},{8,24},{12,28},{16,0},{20,4},{24,8},{28,12},{1,17},{... | collective-permute-start | bytes 2359304 | tf_op jit(solution)/shard_map/ppermute | solution.py:499
  680.4 5.4 copy-start.88
  680.4 5.5 copy-start.87
  680.4 5.5 copy-start.89
  682.9 155.1 %collective-permute-start.21 = (bf16[1,2,256,768]{3,2,1,0:T(8,128)(2,1)}, bf16[1,2,256,768]{3,2,1,0:T(8,128)(2,1)}, u32[]{:S(2)}, u32[]{:S(2)}) collective-permute-start(bf16[1,2,256,768]{3,2,1,0:T(8,128)(2,1)} %get-tuple-element.207), channel_id=1, source_target_pairs={{0,4},{4,8},{8,12},{12,16},{16,20},{20,24},{24,28},{28,0},{1,5},{5... | collective-permute-start | bytes 2359304 | tf_op jit(solution)/shard_map/ppermute | solution.py:499
  686.0 131.3 %copy-start.4 = (f32[2,64,2048]{2,1,0:T(8,128)S(1)}, f32[2,64,2048]{2,1,0:T(8,128)}, u32[]{:S(2)}) copy-start(f32[2,64,2048]{2,1,0:T(8,128)} %copy-done.3) | copy-start | bytes 3145732
  686.0 131.3 %copy-start.22 = (bf16[2048,32]{1,0:T(8,128)(2,1)S(1)}, bf16[2048,32]{1,0:T(8,128)(2,1)}, u32[]{:S(2)}) copy-start(bf16[2048,32]{1,0:T(8,128)(2,1)} %copy-done.21) | copy-start | bytes 393220
  686.0 131.3 %copy-start.81 = (f32[2,64]{1,0:T(2,128)S(1)}, f32[2,64]{1,0:T(2,128)}, u32[]{:S(2)}) copy-start(f32[2,64]{1,0:T(2,128)} %copy-done.80) | copy-start | bytes 1540
  803.1 15.8 %copy-start.41 = (bf16[64,2,2048]{2,1,0:T(2,128)(2,1)S(1)}, bf16[64,2,2048]{2,1,0:T(2,128)(2,1)}, u32[]{:S(2)}) copy-start(bf16[64,2,2048]{2,1,0:T(2,128)(2,1)} %param.13) | copy-start | bytes 1572868
  803.1 15.8 %copy-start.69 = (f32[1,2,8,128]{3,1,2,0:T(2,128)S(1)}, f32[1,2,8,128]{3,1,2,0:T(2,128)}, u32[]{:S(2)}) copy-start(f32[1,2,8,128]{3,1,2,0:T(2,128)} %copy-done.68) | copy-start | bytes 24580
  803.1 15.8 %copy-start.90 = (f32[2,64]{1,0:T(2,128)S(1)}, f32[2,64]{1,0:T(2,128)}, u32[]{:S(2)}) copy-start(f32[2,64]{1,0:T(2,128)} %get-tuple-element.254) | copy-start | bytes 1540
  803.1 346.0 %collective-permute-start.27 = (bf16[1,2,256,768]{3,2,1,0:T(8,128)(2,1)}, bf16[1,2,256,768]{3,2,1,0:T(8,128)(2,1)}, u32[]{:S(2)}, u32[]{:S(2)}) collective-permute-start(bf16[1,2,256,768]{3,2,1,0:T(8,128)(2,1)} %get-tuple-element.200), channel_id=1, source_target_pairs={{0,28},{4,0},{8,4},{12,8},{16,12},{20,16},{24,20},{28,24},{1,29},{... | collective-permute-start | bytes 2359304 | tf_op jit(solution)/shard_map/ppermute | solution.py:499
  813.3 335.8 %collective-permute-start.26 = (bf16[1,2,256,768]{3,2,1,0:T(8,128)(2,1)}, bf16[1,2,256,768]{3,2,1,0:T(8,128)(2,1)}, u32[]{:S(2)}, u32[]{:S(2)}) collective-permute-start(bf16[1,2,256,768]{3,2,1,0:T(8,128)(2,1)} %get-tuple-element.201), channel_id=1, source_target_pairs={{0,24},{4,28},{8,0},{12,4},{16,8},{20,12},{24,16},{28,20},{1,25},{... | collective-permute-start | bytes 2359304 | tf_op jit(solution)/shard_map/ppermute | solution.py:499
  813.4 143.3 %collective-permute-start.25 = (bf16[1,2,256,768]{3,2,1,0:T(8,128)(2,1)}, bf16[1,2,256,768]{3,2,1,0:T(8,128)(2,1)}, u32[]{:S(2)}, u32[]{:S(2)}) collective-permute-start(bf16[1,2,256,768]{3,2,1,0:T(8,128)(2,1)} %get-tuple-element.203), channel_id=1, source_target_pairs={{0,20},{4,24},{8,28},{12,0},{16,4},{20,8},{24,12},{28,16},{1,21},{... | collective-permute-start | bytes 2359304 | tf_op jit(solution)/shard_map/ppermute | solution.py:499
  813.4 100.1 %collective-permute-start.23 = (bf16[1,2,256,768]{3,2,1,0:T(8,128)(2,1)}, bf16[1,2,256,768]{3,2,1,0:T(8,128)(2,1)}, u32[]{:S(2)}, u32[]{:S(2)}) collective-permute-start(bf16[1,2,256,768]{3,2,1,0:T(8,128)(2,1)} %get-tuple-element.205), channel_id=1, source_target_pairs={{0,12},{4,16},{8,20},{12,24},{16,28},{20,0},{24,4},{28,8},{1,13},{... | collective-permute-start | bytes 2359304 | tf_op jit(solution)/shard_map/ppermute | solution.py:499
  838.1 75.5 %collective-permute-start.22 = (bf16[1,2,256,768]{3,2,1,0:T(8,128)(2,1)}, bf16[1,2,256,768]{3,2,1,0:T(8,128)(2,1)}, u32[]{:S(2)}, u32[]{:S(2)}) collective-permute-start(bf16[1,2,256,768]{3,2,1,0:T(8,128)(2,1)} %get-tuple-element.206), channel_id=1, source_target_pairs={{0,8},{4,12},{8,16},{12,20},{16,24},{20,28},{24,0},{28,4},{1,9},{5... | collective-permute-start | bytes 2359304 | tf_op jit(solution)/shard_map/ppermute | solution.py:499
  888.1 25.4 %copy-start.25 = (bf16[4,2,64,512]{3,2,1,0:T(8,128)(2,1)S(1)}, bf16[4,2,64,512]{3,2,1,0:T(8,128)(2,1)}, u32[]{:S(2)}) copy-start(bf16[4,2,64,512]{3,2,1,0:T(8,128)(2,1)} %copy.326) | copy-start | bytes 1572868
  888.1 25.4 %copy-start.40 = (bf16[2048,512]{1,0:T(8,128)(2,1)S(1)}, bf16[2048,512]{1,0:T(8,128)(2,1)}, u32[]{:S(2)}) copy-start(bf16[2048,512]{1,0:T(8,128)(2,1)} %get-tuple-element.71) | copy-start | bytes 6291460
  913.5 43.1 %collective-permute-start.24 = (bf16[1,2,256,768]{3,2,1,0:T(8,128)(2,1)}, bf16[1,2,256,768]{3,2,1,0:T(8,128)(2,1)}, u32[]{:S(2)}, u32[]{:S(2)}) collective-permute-start(bf16[1,2,256,768]{3,2,1,0:T(8,128)(2,1)} %get-tuple-element.204), channel_id=1, source_target_pairs={{0,16},{4,20},{8,24},{12,28},{16,0},{20,4},{24,8},{28,12},{1,17},{... | collective-permute-start | bytes 2359304 | tf_op jit(solution)/shard_map/ppermute | solution.py:499
  922.5 16.9 %copy-start.19 = (bf16[64,2,2048]{2,1,0:T(2,128)(2,1)S(1)}, bf16[64,2,2048]{2,1,0:T(2,128)(2,1)}, u32[]{:S(2)}) copy-start(bf16[64,2,2048]{2,1,0:T(2,128)(2,1)} %param.12) | copy-start | bytes 1572868
  940.8 5.5 copy-start.24
  940.8 5.5 copy-start.35
  1131.5 17.6 %copy-start.2 = (s32[8]{0:T(128)S(1)}, s32[8]{0:T(128)}, u32[]{:S(2)}) copy-start(s32[8]{0:T(128)} %stack.62.origin_ref) | copy-start | bytes 100
  (61 other events, 167.1 us)

commit v4 on v3

--- a/solution.py
+++ b/solution.py
@@ -241,10 +241,11 @@
 
 
 def gather_everywhere(block, ranks, collective_id):
-    half = block.shape[1] // 2
+    columns = block.shape[1]
+    cut = columns // 256 * 128
     pieces = (
-        (0, 0, half, True, ("inner", "side", "core")),
-        (0, half, half, True, ("side", "inner", "core")),
+        (0, 0, cut, True, ("inner", "side", "core")),
+        (0, cut, columns - cut, True, ("side", "inner", "core")),
     )
     return gather_blocks([block], [4 * ranks], pieces, ranks, collective_id)[0]
 
@@ -489,15 +490,80 @@
     return (result, other) if beside is not None else result
 
 
-def send_blocks(block_for, ranks):
+def send_blocks(blocks, ranks):
     own = lax.axis_index("dp")
-    received = [(own, block_for(own))]
+    received = [(own, blocks[0])]
     for shift in range(1, ranks):
-        target = lax.rem(own + shift, ranks)
         origin = lax.rem(own + ranks - shift, ranks)
         pairs = [(j, (j + shift) % ranks) for j in range(ranks)]
-        received.append((origin, lax.ppermute(block_for(target), "dp", pairs)))
+        received.append((origin, lax.ppermute(blocks[shift], "dp", pairs)))
     return received
+
+
+def pack_kernel(width, target_ref, in_ref, out_ref, *refs):
+    block_refs, (wide_ref, held_ref, sem) = refs[:-3], refs[-3:]
+    del target_ref
+    at = pl.program_id(0)
+    tiles = width // 128
+    steps = len(block_refs)
+    portion, depth, _ = held_ref.shape[1:]
+
+    def store(n):
+        return pltpu.make_async_copy(held_ref.at[n % 2], block_refs[n].at[0], sem.at[n % 2])
+
+    for n in range(2, steps):
+        pl.when(at == n)(store(n - 2).wait)
+    slot = lax.rem(at, 2)
+    for e in range(portion):
+        wide_ref[...] = in_ref[e].astype(F32)
+        for j in range(2):
+            for tile in range(tiles):
+                rows = pl.ds(tile * 2 + j, depth, stride=2 * tiles)
+                start = j * width + tile * 128
+                held_ref[slot, e, :, start : start + 128] = wide_ref[rows, :].astype(BF16)
+        held_ref[slot, e, :, 2 * width :] = out_ref[e]
+    for n in range(steps):
+        pl.when(at == n)(store(n).start)
+
+    @pl.when(at == steps - 1)
+    def _():
+        for n in range(max(0, steps - 2), steps):
+            store(n).wait()
+
+
+def pack(expert_in, expert_out, ranks, portions):
+    experts, depth, _, width = expert_in.shape
+    portion = experts // ranks // portions
+    tiles = width // 128
+    rank = lax.axis_index("dp")
+    targets = lax.rem(rank + jnp.arange(ranks, dtype=jnp.int32), ranks)
+    in_rows = jnp.swapaxes(expert_in.reshape(experts, depth, 2, tiles, 128), 2, 3)
+    in_rows = in_rows.reshape(experts, depth * tiles * 2, 128)
+    block = jax.ShapeDtypeStruct((1, portion, depth, 3 * width), BF16)
+
+    def place(step, targets):
+        return targets[lax.rem(step, ranks)] * portions + step // ranks, 0, 0
+
+    blocks = pl.pallas_call(
+        functools.partial(pack_kernel, width),
+        grid_spec=pltpu.PrefetchScalarGridSpec(
+            num_scalar_prefetch=1,
+            grid=(portions * ranks,),
+            in_specs=[
+                pl.BlockSpec((portion, depth * tiles * 2, 128), place),
+                pl.BlockSpec((portion, depth, width), place),
+            ],
+            out_specs=(pl.BlockSpec(memory_space=pl.ANY),) * (portions * ranks),
+            scratch_shapes=[
+                pltpu.VMEM((depth * tiles * 2, 128), F32),
+                pltpu.VMEM((2, portion, depth, 3 * width), BF16),
+                pltpu.SemaphoreType.DMA((2,)),
+            ],
+        ),
+        out_shape=(block,) * (portions * ranks),
+        compiler_params=pltpu.CompilerParams(vmem_limit_bytes=32 * 1024 * 1024),
+    )(targets, in_rows, expert_out)
+    return [list(blocks[n * ranks : (n + 1) * ranks]) for n in range(portions)]
 
 
 def settle_kernel(width, origin_ref, *refs):
@@ -564,17 +630,19 @@
     number = len(received) - 1
     first, last = 1 + number * part // parts, 1 + number * (part + 1) // parts
     blocks = [block for _, block in received[first:last]]
+    if not blocks:
+        return value, received
     value, blocks = lax.optimization_barrier((value, blocks))
     renewed = [(origin, block) for (origin, _), block in zip(received[first:last], blocks)]
     return value, received[:first] + renewed + received[last:]
 
 
 def expert_kernel(ranks, owned, width, added, origin_ref, rows_ref, pull_ref, *refs):
-    position_ref, gate_ref, column_ref, *refs = refs
+    position_ref, across_ref, column_ref, *refs = refs
     block_refs, refs = refs[:ranks], refs[ranks:]
     before, refs = refs[: 2 * added], refs[2 * added :]
     mixture_ref, returned_ref, chosen_ref, pulled_ref, d_gate_up_ref, hidden_ref, *refs = refs
-    place_ref, mixed_ref, back_ref, weight_ref, load_sem = refs
+    place_ref, turned_ref, mixed_ref, back_ref, weight_ref, turned_weight_ref, dots_ref, load_sem = refs
 
     @pl.when(pl.program_id(0) == 0)
     def _():
@@ -588,26 +656,37 @@
             load.start()
         for load in loads:
             load.wait()
-
-    group_tokens, features = rows_ref.shape
+        depth = weight_ref.shape[2]
+        for e in range(owned):
+            for n in range(ranks):
+                turned_weight_ref[e, :, n * depth : (n + 1) * depth] = weight_ref[n, e].T
+
+    group_tokens, features = pull_ref.shape
     chunk = min(features, 512)
     slot = lax.broadcasted_iota(jnp.int32, (CAP, group_tokens), 0)
-    last = (((1,), (1,)), ((), ()))
-    first = (((0,), (0,)), ((), ()))
+    lane = lax.broadcasted_iota(jnp.int32, (group_tokens, owned * CAP), 1)
+    turned = jnp.zeros((group_tokens, owned * CAP), BF16)
     for e in range(owned):
         place_ref[e * CAP : (e + 1) * CAP] = (position_ref[0, e : e + 1] == slot).astype(BF16)
+        found = across_ref[0, :, e : e + 1]
+        hit = (found >= 0) & (found + e * CAP == lane)
+        turned = jnp.where(hit, jnp.ones_like(turned), turned)
+    turned_ref[...] = turned
     for start in range(0, features, chunk):
         columns = slice(start, start + chunk)
         chosen = jnp.dot(place_ref[...], rows_ref[:, columns], preferred_element_type=F32)
         chosen_ref[:, 0, :, columns] = chosen.astype(BF16).reshape(owned, CAP, chunk)
         pulled = jnp.dot(place_ref[...], pull_ref[:, columns], preferred_element_type=F32)
         pulled_ref[:, 0, :, columns] = pulled.astype(BF16).reshape(owned, CAP, chunk)
-    spread = jnp.zeros((group_tokens, 128), F32)
     for e in range(owned):
         weight_in = weight_ref[:, e, :, : 2 * width].reshape(features, 2 * width)
         weight_out = weight_ref[:, e, :, 2 * width :].reshape(features, width)
-        here = position_ref[0, e : e + 1] == slot
-        gate = jnp.sum(jnp.where(here, gate_ref[0, e : e + 1], 0.0), axis=1, keepdims=True)
+        gate = jnp.dot(
+            place_ref[e * CAP : (e + 1) * CAP],
+            rows_ref[:, features:],
+            preferred_element_type=F32,
+        )
+        gate = jnp.sum(gate * column_ref[owned + e : owned + e + 1], axis=1, keepdims=True)
         gate_up = jnp.dot(chosen_ref[e, 0], weight_in, preferred_element_type=F32)
         d_plain = jnp.dot(pulled_ref[e, 0], weight_out, preferred_element_type=F32)
         gate_part = gate_up[:, :width]
@@ -616,44 +695,40 @@
         activated = gate_part * sigmoid_gate
         hidden = activated * up_part
         slot_dots = jnp.sum(hidden * d_plain, axis=1, keepdims=True)
-        spread = spread + lax.dot_general(
-            place_ref[e * CAP : (e + 1) * CAP],
-            (slot_dots * column_ref[e : e + 1]).astype(BF16),
-            first,
-            preferred_element_type=F32,
-        )
+        dots_ref[e * CAP : (e + 1) * CAP] = (slot_dots * column_ref[e : e + 1]).astype(BF16)
         d_hidden = d_plain * gate
         d_gate_part = d_hidden * up_part * sigmoid_gate * (1.0 + gate_part * (1.0 - sigmoid_gate))
         d_up_part = d_hidden * activated
         hidden_ref[e, 0] = (hidden * gate).astype(BF16)
         d_gate_up_ref[e, 0, :, :width] = d_gate_part.astype(BF16)
         d_gate_up_ref[e, 0, :, width:] = d_up_part.astype(BF16)
-        mixed_ref[e * CAP : (e + 1) * CAP] = lax.dot_general(
-            hidden_ref[e, 0], weight_out, last, preferred_element_type=F32
+        mixed_ref[e * CAP : (e + 1) * CAP] = jnp.dot(
+            hidden_ref[e, 0], turned_weight_ref[e, 2 * width :], preferred_element_type=F32
         ).astype(BF16)
-        back_ref[e * CAP : (e + 1) * CAP] = lax.dot_general(
-            d_gate_up_ref[e, 0], weight_in, last, preferred_element_type=F32
+        back_ref[e * CAP : (e + 1) * CAP] = jnp.dot(
+            d_gate_up_ref[e, 0], turned_weight_ref[e, : 2 * width], preferred_element_type=F32
         ).astype(BF16)
     def finish(target_ref, number, columns, total):
         if added:
             total = total + before[number][:, columns].astype(F32)
         target_ref[:, columns] = total.astype(BF16)
 
+    spread = jnp.dot(turned_ref[...], dots_ref[...], preferred_element_type=F32)
     finish(returned_ref, 1, slice(features, features + 128), spread)
     for start in range(0, features, chunk):
         columns = slice(start, start + chunk)
         for number, (target_ref, source_ref) in enumerate(
             ((mixture_ref, mixed_ref), (returned_ref, back_ref))
         ):
-            total = lax.dot_general(
-                place_ref[...], source_ref[:, columns], first, preferred_element_type=F32
+            total = jnp.dot(
+                turned_ref[...], source_ref[:, columns], preferred_element_type=F32
             )
             finish(target_ref, number, columns, total)
 
 
-def expert_math(rows, pull, position, gate, column, received, before, last):
+def expert_math(rows, pull, position, column, received, before, last):
     groups, owned, group_tokens = position.shape
-    tokens, features = rows.shape
+    tokens, features = pull.shape
     ranks = len(received)
     depth = features // ranks
     width = received[0][1].shape[3] // 3
@@ -681,11 +756,11 @@
             num_scalar_prefetch=1,
             grid=(groups,),
             in_specs=[
-                by_rows,
+                by_returned,
                 by_rows,
                 by_group,
-                by_group,
-                pl.BlockSpec((owned, 128), lambda g, _: (0, 0)),
+                pl.BlockSpec((1, group_tokens, owned), lambda g, _: (g, 0, 0)),
+                pl.BlockSpec((2 * owned, 128), lambda g, _: (0, 0)),
             ]
             + [pl.BlockSpec(memory_space=pl.ANY)] * ranks
             + ([by_rows, by_returned] if before else []),
@@ -699,9 +774,12 @@
             ),
             scratch_shapes=[
                 pltpu.VMEM((slots, group_tokens), BF16),
+                pltpu.VMEM((group_tokens, slots), BF16),
                 pltpu.VMEM((slots, features), BF16),
                 pltpu.VMEM((slots, features), BF16),
                 pltpu.VMEM((ranks, owned, depth, 3 * width), BF16),
+                pltpu.VMEM((owned, 3 * width, features), BF16),
+                pltpu.VMEM((slots, 128), BF16),
                 pltpu.SemaphoreType.DMA((ranks,)),
             ],
         ),
@@ -725,7 +803,7 @@
         rows,
         pull,
         position,
-        gate,
+        jnp.swapaxes(position, 1, 2),
         column,
         *[block for _, block in received],
         *before,
@@ -749,14 +827,12 @@
     expert_out,
 ):
     rank = lax.axis_index("dp")
-    quarter = lax.axis_index("tensor")
     local_rows, micro_count, features = tokens.shape
     experts, depth, _, width = expert_in.shape
     top_count = expert_ids.shape[2]
     owned = experts // ranks
     local_tokens = local_rows * micro_count
     group_tokens = quarters * local_tokens
-    all_tokens = ranks * group_tokens
     head_dim = qk_gain.shape[0] * ranks
     local_heads = qk_gain.shape[2]
     local_width = local_heads * head_dim
@@ -801,18 +877,9 @@
 
     portions = 2 if owned % 2 == 0 else 1
     portion = owned // portions
-    raw_rows, expert_in, expert_out = lax.optimization_barrier((raw_rows, expert_in, expert_out))
-
-    def weight_block(number, target):
-        start = target * owned + number * portion
-        part_in = lax.dynamic_slice_in_dim(expert_in, start, portion, 0)
-        part_out = lax.dynamic_slice_in_dim(expert_out, start, portion, 0)
-        joined = jnp.concatenate([part_in.reshape(portion, depth, 2 * width), part_out], axis=2)
-        return joined[None]
-
-    held = [
-        send_blocks(functools.partial(weight_block, number), ranks) for number in range(portions)
-    ]
+    packed = pack(expert_in, expert_out, ranks, portions)
+    packed, raw_rows = lax.optimization_barrier((packed, raw_rows))
+    held = [send_blocks(blocks, ranks) for blocks in packed]
 
     raw_rows = raw_rows.astype(F32)
     rows_one = (raw_rows * norm_factor(raw_rows) * gain_one).astype(BF16)
@@ -839,21 +906,24 @@
     head_out = dot("mhqk,mkhc->mqhc", weights_low, value_heads).astype(BF16)
     head_out = from_sequences(head_out.reshape(micro_count, seq_len, local_width))
 
-    def scatter_quarters(array):
-        across = ((0, 0, features, False, ("side", "core")),)
-        (result,) = scatter_blocks([array], across, [quarters], ranks, 2)
-        return result.astype(F32).reshape(own_shape)
-
-    attended = scatter_quarters(dot("tf,df->td", head_out, full_out).astype(BF16))
+    across = ((0, 0, features, False, ("side", "core")),)
+
+    attended = dot("tf,df->td", head_out, full_out).astype(BF16)
+    (attended,) = scatter_blocks([attended], across, [quarters], ranks, 2)
     attended, held[0] = tie(attended, held[0], 0, 2)
     inputs = own_tokens.astype(F32).reshape(own_shape)
-    residual = inputs + attended
+    residual = inputs + attended.astype(F32).reshape(own_shape)
     factor_two = norm_factor(residual)
     normed_two = (residual * factor_two * gain_two).astype(BF16).reshape(local_tokens, features)
 
-    rows_all = gather_everywhere(normed_two, ranks, 3)
+    probs_own = softmax_rows(dot("td,de->te", normed_two, full_router))
+    probs_high = probs_own.astype(BF16)
+    probs_low = (probs_own - probs_high.astype(F32)).astype(BF16)
+    beside = [probs_high, probs_low, jnp.zeros((local_tokens, 128 - 2 * experts), BF16)]
+    rows_all = gather_everywhere(jnp.concatenate([normed_two] + beside, axis=1), ranks, 3)
     rows_all, held[0] = tie(rows_all, held[0], 1, 2)
-    router_probs = softmax_rows(dot("td,de->te", rows_all, full_router))
+    if portions > 1:
+        rows_all, held[1] = tie(rows_all, held[1], 0, 3)
 
     first = rank * owned
     routes = all_ids.reshape(ranks, quarters, local_rows, micro_count, top_count)
@@ -864,10 +934,9 @@
     earlier = (order[:, None] < order[None, :]).astype(BF16)
     position = dot("ges,st->get", member.astype(BF16), earlier)
     position = jnp.where(member, position, -1.0).astype(jnp.int32)
-    gate_own = lax.dynamic_slice_in_dim(router_probs, first, owned, 1)
-    gate_own = jnp.swapaxes(gate_own.reshape(ranks, group_tokens, owned), 1, 2)
     lanes = jnp.arange(128, dtype=jnp.int32)
-    column = (names[:, None] == lanes).astype(F32)
+    column = [names[:, None] == lanes, names[:, None] == lax.rem(lanes, experts)]
+    column[1] = column[1] & (lanes < 2 * experts)
     before = ()
     sent = []
     for number in range(portions):
@@ -876,8 +945,7 @@
             rows_all,
             pull_all,
             position[:, part],
-            gate_own[:, part],
-            column[part],
+            jnp.concatenate([masks[part] for masks in column]).astype(F32),
             held[number],
             before,
             number == portions - 1,
@@ -888,20 +956,23 @@
         grad_blocks = jnp.concatenate([grad_in.astype(BF16), grad_out.astype(BF16)], axis=3)
         returned_all, grad_blocks = lax.optimization_barrier((returned_all, grad_blocks))
         before = (mixture_all, returned_all)
-
-        def grad_block(grad_blocks, target):
-            return lax.dynamic_index_in_dim(grad_blocks, target, 0, keepdims=True)
-
-        sent.append(send_blocks(functools.partial(grad_block, grad_blocks), ranks))
+        if number + 1 < portions:
+            grad_blocks, held[number + 1] = tie(grad_blocks, held[number + 1], 0, 1)
+        targets = [lax.rem(rank + shift, ranks) for shift in range(ranks)]
+        blocks = [lax.dynamic_index_in_dim(grad_blocks, to, 0, keepdims=True) for to in targets]
+        sent.append(send_blocks(blocks, ranks))
     if portions > 1:
-        returned_all, sent[0] = tie(returned_all, sent[0], 0, 2)
+        for part in range(4):
+            returned_all, sent[0] = tie(returned_all, sent[0], part, 7)
     returned_own = scatter_everywhere(returned_all, ranks, 4)
-    returned_own, sent[0] = tie(returned_own, sent[0], portions - 1, portions)
+    if portions > 1:
+        for part in range(4, 7):
+            returned_own, sent[0] = tie(returned_own, sent[0], part, 7)
+    for part in range(2):
+        returned_own, sent[-1] = tie(returned_own, sent[-1], part, 7)
 
     returned_f = returned_own[:, :features].astype(F32)
     d_probs = returned_own[:, features : features + experts].astype(F32)
-    first_token = (rank * quarters + quarter) * local_tokens
-    probs_own = lax.dynamic_slice_in_dim(router_probs, first_token, local_tokens, 0)
     d_logits = (
         probs_own * (d_probs - jnp.sum(d_probs * probs_own, axis=-1, keepdims=True))
     ).astype(BF16)
@@ -915,7 +986,6 @@
     (rows_back,) = gather_blocks(
         [d_attended], [quarters], ((0, 0, features, False, ("side", "core")),), ranks, 8
     )
-    rows_back, sent[-1] = tie(rows_back, sent[-1], 0, 4)
     d_heads = to_sequences(dot("td,df->tf", rows_back, full_out).astype(BF16)).reshape(heads_shape)
     grad_w_out = dot("td,tf->df", rows_back, head_out)
     d_weights = dot("mqhc,mkhc->mhqk", d_heads, value_heads)
@@ -949,14 +1019,13 @@
     d_q = from_sequences(d_query_raw.astype(BF16))
     d_k = from_sequences(d_key_raw.astype(BF16))
     d_v = from_sequences(d_values)
-    d_q, sent[-1] = tie(d_q, sent[-1], 1, 4)
-    d_normed_one = scatter_quarters(
-        (
-            dot("tf,df->td", d_q, full_q)
-            + dot("tf,df->td", d_k, full_k)
-            + dot("tf,df->td", d_v, full_v)
-        ).astype(BF16)
-    )
+    d_normed_one = (
+        dot("tf,df->td", d_q, full_q)
+        + dot("tf,df->td", d_k, full_k)
+        + dot("tf,df->td", d_v, full_v)
+    ).astype(BF16)
+    (d_normed_one,) = scatter_blocks([d_normed_one], across, [quarters], ranks, 2)
+    d_normed_one = d_normed_one.astype(F32).reshape(own_shape)
     factor_one = norm_factor(inputs)
     grad_tokens = (d_residual + norm_back(inputs, factor_one, gain_one, d_normed_one)).astype(BF16)
     grad_gain_one = jnp.sum(inputs * factor_one * d_normed_one, axis=(0, 1))
@@ -971,7 +1040,8 @@
     grads = [dot("td,tf->df", rows_one, part).astype(BF16) for part in (d_q, d_k, d_v)]
     grads += [grad_w_out.astype(BF16), small_grads.reshape(features, slim).astype(BF16)]
     grads = jnp.concatenate(grads, axis=1)
-    grads, sent[-1] = tie(grads, sent[-1], 2, 4)
+    for part in range(2, 6):
+        grads, sent[-1] = tie(grads, sent[-1], part, 7)
     mixture_own, grads_own = scatter_everywhere(mixture_all, ranks, 10, grads)
     grads_own = grads_own.astype(F32)
     grad_qkv_own = grads_own[:, : 3 * local_width].reshape(depth, 3, local_width)

time: 1170 us -> 1160 us (level)
  waiting for transfers between devices: 37.7 us -> 0.07 us
  Pallas kernels: 759 us -> 793 us
  starting transfers between devices: 50 us -> 68 us
  other arithmetic: 52.6 us -> 34.9 us
    ppermute x28, waiting for transfers between devices: 37.7 us -> 0.07 us  [send_blocks(): received.append((origin, lax.ppermute(blocks[shift], 'dp', pairs)))]
    reshape x17 -> x0, local copies, waits for them, and re-layouts: 21.7 us -> none  [the longest x16 21.1 us: weight_block(): part_in.reshape(portion, depth, 2 * width)]
    broadcast_in_dim x15 -> x0, other arithmetic: 18.9 us -> none  [weight_block(): return joined[None]]
    ppermute x28, starting transfers between devices: 50 us -> 68 us  [send_blocks(): received.append((origin, lax.ppermute(blocks[shift], 'dp', pairs)))]
    pallas_call x4, Pallas kernels: 313 us -> 329 us  [scatter_blocks(): pl.pallas_call(functools.partial(scatter_kernel, ranks, arrays, pieces),...]
    dynamic_slice x5 -> x2, local copies, waits for them, and re-layouts: 17.7 us -> 4.68 us  [body(): lax.dynamic_index_in_dim(grad_blocks, to, 0, keepdims=True)]
    pallas_call x3, Pallas kernels: 292 us -> 305 us  [gather_blocks(): pl.pallas_call(functools.partial(gather_kernel, ranks, arrays, pieces), o...]
    pallas_call x0 -> x1, Pallas kernels: none -> 12.3 us  [pack(): pl.pallas_call(functools.partial(pack_kernel, width), grid_spec=pltpu.Pre...]
  transfers between devices with their start and end apart: 28 -> 28, of which waited for: 2 -> 0; matrix products, arithmetic and copies ran while one was open for 22% -> 21% of each run, Pallas kernels for 49% -> 52%
where the time goes in v4:
time: 1160 us; the launch traced here: 1150 us
  Pallas kernels  793 us (68%)
  local copies, waits for them, and re-layouts  124 us (11%)
  matrix products  104 us (9%)
  starting transfers between devices  68 us (6%)
  other arithmetic  34.9 us (3%)
  blocking collectives  22.9 us (2%)
    pallas_call x4, Pallas kernels, scatter_blocks(): pl.pallas_call(functools.partial(scatter_kernel, ranks, arrays, pieces),...  329 us
    pallas_call x3, Pallas kernels, gather_blocks(): pl.pallas_call(functools.partial(gather_kernel, ranks, arrays, pieces), o...  305 us
    pallas_call x2, Pallas kernels, expert_math(): pl.pallas_call(functools.partial(expert_kernel, ranks, owned, width, 1 if...  135 us
    dot_general x26, matrix products, dot(): return jnp.einsum(spec, left, right, preferred_element_type=F32)  104 us
    ppermute x28, starting transfers between devices, send_blocks(): received.append((origin, lax.ppermute(blocks[shift], 'dp', pairs)))  68 us
    unnamed x169, local copies, waits for them, and re-layouts  29.8 us
  transfers between devices with their start and end apart: 28, of which 0 were waited for; matrix products, arithmetic and copies ran while one was open for 21% of the time, Pallas kernels for 52%

profile of v4, /device:TPU:0, one launch (start us, length us, event | category | flops | bytes accessed | tf_op | source)
XLA Modules:
  0.0 1149.2 jit_solution(17266027070044550558)
XLA Ops:
  13.5 12.3 %shard_map.195 = (bf16[1,2,256,768]{3,2,1,0:T(8,128)(2,1)S(1)}, bf16[1,2,256,768]{3,2,1,0:T(8,128)(2,1)S(1)}, bf16[1,2,256,768]{3,2,1,0:T(8,128)(2,1)S(1)}, bf16...) custom-call(s32[8]{0:T(128)S(1)} %compare_select_fusion.target_ref, ...), custom_call_target="tpu_custom_call" | custom-call | tf_op jit(solution)/shard_map/pallas_call | solution.py:547
  33.0 171.7 %shard_map.196 = (bf16[2048,512]{1,0:T(8,128)(2,1)}, bf16[2048,512]{1,0:T(8,128)(2,1)}, bf16[2048,512]{1,0:T(8,128)(2,1)}, bf16[2048,128]{1,0:T(8,128)(2,1)}, bf...) custom-call(bf16[256,512]{1,0:T(8,128)(2,1)} %get-tuple-element.308.refs_0_, ...), custom_call_target="tpu_custom_call" | custom-call | bytes 27787264 | tf_op jit(solution)/shard_map/pallas_call | solution.py:221
  204.6 2.2 collective-permute-start
  206.8 2.3 collective-permute-start.2
  210.7 2.4 collective-permute-start.4
  222.9 3.6 convolution_convert_fusion.7
  229.3 3.5 fusion.102
  235.0 3.5 fusion.104
  240.6 2.5 reshape.373
  243.1 2.6 copy.295
  245.7 2.5 reshape.375
  248.3 2.5 copy.298
  250.8 4.5 reshape.417
  255.3 2.7 copy.308
  260.6 3.3 select_convert_fusion
  263.9 6.2 all-reduce.3
  271.0 2.2 fusion.88
  275.3 3.5 fusion.55
  283.9 6.8 slice_bitcast_fusion.4
  290.7 2.6 convolution_convert_fusion.4.refs_0_
  294.5 2.8 copy.311.refs_0_
  297.3 2.8 copy.316.refs_0_
  300.8 16.9 %shard_map.197 = bf16[128,2048]{1,0:T(8,128)(2,1)} custom-call(bf16[512,2048]{1,0:T(8,128)(2,1)} %convolution_convert_fusion.4.refs_0_), custom_call_target="tpu_custom_call" | custom-call | flops 1048576 | bytes 2097152 | tf_op jit(solution)/shard_map/pallas_call | solution.py:439
  329.7 114.8 %shard_map.198.rows_ref = bf16[4096,2176]{1,0:T(8,128)(2,1)} custom-call(bf16[128,2176]{1,0:T(8,128)(2,1)} %concatenate.28.refs_0_), custom_call_target="tpu_custom_call" | custom-call | bytes 17825792 | tf_op jit(solution)/shard_map/pallas_call | solution.py:221
  444.5 3.0 collective-permute-start.10
  448.4 2.3 collective-permute-start.12
  450.7 3.2 collective-permute-start.13
  453.9 66.1 %shard_map.199 = (bf16[4096,2048]{1,0:T(8,128)(2,1)}, bf16[4096,2176]{1,0:T(8,128)(2,1)}, bf16[2,8,176,2048]{3,2,1,0:T(8,128)(2,1)}, bf16[2,8,176,2048]{3,2,1,0:...) custom-call(s32[8]{0:T(128)} %stack.62.origin_ref, ...), custom_call_target="tpu_custom_call" | custom-call | flops 41339060224 | bytes 90177536 | tf_op jit(solution)/shard_map/pallas_call | solution.py:753
  520.1 12.0 %fusion.18 = bf16[8,2,256,512]{3,2,1,0:T(8,128)(2,1)} fusion(bf16[2,8,22,8,8,256]{5,4,3,2,1,0:T(8,128)(2,1)} %bitcast.300, bf16[2,8,176,512]{3,2,1,0:T(8,128)(2,1)} %get-tuple-element.162), kind=kOutput, calls=%fused_computation.24 | convolution fusion | flops 5907677184 | bytes 18612224 | tf_op jit(solution)/shard_map/egsrk,egsf->rekf/dot_general | solution.py:38
  532.1 10.4 fusion.45
  542.5 3.3 pad_maximum_fusion
  548.0 20.3 %collective-permute-start.17 = (bf16[1,2,256,768]{3,2,1,0:T(8,128)(2,1)}, bf16[1,2,256,768]{3,2,1,0:T(8,128)(2,1)S(1)}, u32[]{:S(2)}, u32[]{:S(2)}) collective-permute-start(bf16[1,2,256,768]{3,2,1,0:T(8,128)(2,1)} %get-tuple-element.299), channel_id=1, source_target_pairs={{0,16},{4,20},{8,24},{12,28},{16,0},{20,4},{24,8},{28,12},{1,17},{... | collective-permute-start | bytes 2359304 | tf_op jit(solution)/shard_map/ppermute | solution.py:499
  571.0 68.4 %shard_map.200 = (bf16[4096,2048]{1,0:T(8,128)(2,1)}, bf16[4096,2176]{1,0:T(8,128)(2,1)}, bf16[2,8,176,2048]{3,2,1,0:T(8,128)(2,1)}, bf16[2,8,176,2048]{3,2,1,0:...) custom-call(s32[8]{0:T(128)} %stack.62.origin_ref, ...), custom_call_target="tpu_custom_call", output_to_operand_aliasing={{0}: (14, {}), {1}: (15, {})} | custom-call | flops 41339060224 | bytes 90177536 | tf_op jit(solution)/shard_map/pallas_call | solution.py:753
  639.4 12.2 %fusion.19 = bf16[8,2,256,512]{3,2,1,0:T(8,128)(2,1)} fusion(bf16[2,8,22,8,8,256]{5,4,3,2,1,0:T(8,128)(2,1)} %bitcast.298, bf16[2,8,176,512]{3,2,1,0:T(8,128)(2,1)} %get-tuple-element.185), kind=kOutput, calls=%fused_computation.25 | convolution fusion | flops 5907677184 | bytes 18612224 | tf_op jit(solution)/shard_map/egsrk,egsf->rekf/dot_general | solution.py:38
  651.7 10.4 fusion.48
  662.0 3.3 pad_maximum_fusion.1
  665.3 4.2 collective-permute-start.20
  671.6 2.5 constant_dynamic-slice_fusion
  678.1 133.2 %shard_map.201 = bf16[128,2176]{1,0:T(8,128)(2,1)} custom-call(bf16[4096,2176]{1,0:T(8,128)(2,1)} %get-tuple-element.194.refs_0_), custom_call_target="tpu_custom_call" | custom-call | flops 8912896 | bytes 17825792 | tf_op jit(solution)/shard_map/pallas_call | solution.py:439
  811.4 10.0 collective-permute-start.27
  821.5 2.9 collective-permute-start.24
  827.9 2.3 fusion.114
  830.2 18.6 %shard_map.202 = bf16[512,2048]{1,0:T(8,128)(2,1)} custom-call(bf16[128,2048]{1,0:T(8,128)(2,1)} %bitcast.275), custom_call_target="tpu_custom_call" | custom-call | bytes 2097152 | tf_op jit(solution)/shard_map/pallas_call | solution.py:221
  848.7 3.5 convolution_convert_fusion.6
  857.1 3.4 fusion.56
  860.4 2.5 multiply_reduce_fusion
  867.8 2.5 copy.326
  870.4 2.6 reshape.389
  873.0 6.2 all-reduce.2
  881.4 3.3 fusion.117
  884.7 2.9 fusion.27
  896.4 2.5 copy.332
  899.0 2.7 reshape.391
  906.8 2.6 add_convert_fusion.refs_0_
  909.4 16.9 %shard_map.203 = bf16[128,2048]{1,0:T(8,128)(2,1)} custom-call(bf16[512,2048]{1,0:T(8,128)(2,1)} %add_convert_fusion.refs_0_), custom_call_target="tpu_custom_call" | custom-call | flops 1048576 | bytes 2097152 | tf_op jit(solution)/shard_map/pallas_call | solution.py:439
  928.0 4.7 fusion.26
  933.5 2.9 fusion.25
  938.4 4.4 fusion.24
  943.8 161.8 %shard_map.204 = (bf16[128,2048]{1,0:T(8,128)(2,1)}, bf16[256,2176]{1,0:T(8,128)(2,1)}) custom-call(bf16[4096,2048]{1,0:T(8,128)(2,1)} %get-tuple-element.183.refs_0_, bf16[2048,2176]{1,0:T(8,128)(2,1)} %constant_dynamic-update-slice_fusion.1.refs_1_), custom_call_target="tpu_custom_call" | custom-call | flops 12845056 | bytes 25690112 | tf_op jit(solution)/shard_map/pallas_call | solution.py:439
  1107.5 2.5 slice.133
  1116.1 3.0 copy.344
  1119.1 3.0 copy.348
  1122.9 10.5 psum.39
  1136.3 12.6 %shard_map.205 = (f32[32,1024,128]{2,1,0:T(8,128)}, f32[32,256,256]{2,1,0:T(8,128)}) custom-call(s32[8]{0:T(128)S(1)} %copy-done.1, bf16[1,2,256,768]{3,2,1,0:T(8,128)(2,1)S(1)} %get-tuple-element.295.refs_0_, bf16[1,2,256,768]{3,2,1,0:T(8,128)(2,1)} %collective-permute-done.14.refs_1_, bf16[1,2,256,768]{3,2,1,0:T(8,128)(2,1)} %collective-permute-done.15.refs_2_, ...), custom_call_target="tpu_custom_call" | custom-call | tf_op jit(solution)/shard_map/pallas_call | solution.py:606
  (319 shorter events, 121.0 us)
Async XLA Ops:
  0.6 9.8 copy-start.41
  204.6 114.4 %collective-permute-start = (bf16[1,2,256,768]{3,2,1,0:T(8,128)(2,1)}, bf16[1,2,256,768]{3,2,1,0:T(8,128)(2,1)}, u32[]{:S(2)}, u32[]{:S(2)}) collective-permute-start(bf16[1,2,256,768]{3,2,1,0:T(8,128)(2,1)} %copy-done.9), channel_id=1, source_target_pairs={{0,4},{4,8},{8,12},{12,16},{16,20},{20,24},{24,28},{28,0},{1,5},{5... | collective-permute-start | bytes 2359304 | tf_op jit(solution)/shard_map/ppermute | solution.py:499
  206.8 114.2 %collective-permute-start.1 = (bf16[1,2,256,768]{3,2,1,0:T(8,128)(2,1)}, bf16[1,2,256,768]{3,2,1,0:T(8,128)(2,1)}, u32[]{:S(2)}, u32[]{:S(2)}) collective-permute-start(bf16[1,2,256,768]{3,2,1,0:T(8,128)(2,1)} %copy-done.8), channel_id=1, source_target_pairs={{0,8},{4,12},{8,16},{12,20},{16,24},{20,28},{24,0},{28,4},{1,9},{5... | collective-permute-start | bytes 2359304 | tf_op jit(solution)/shard_map/ppermute | solution.py:499
  206.8 114.8 %collective-permute-start.2 = (bf16[1,2,256,768]{3,2,1,0:T(8,128)(2,1)}, bf16[1,2,256,768]{3,2,1,0:T(8,128)(2,1)}, u32[]{:S(2)}, u32[]{:S(2)}) collective-permute-start(bf16[1,2,256,768]{3,2,1,0:T(8,128)(2,1)} %copy-done.7), channel_id=1, source_target_pairs={{0,12},{4,16},{8,20},{12,24},{16,28},{20,0},{24,4},{28,8},{1,13},{... | collective-permute-start | bytes 2359304 | tf_op jit(solution)/shard_map/ppermute | solution.py:499
  209.2 115.4 %collective-permute-start.3 = (bf16[1,2,256,768]{3,2,1,0:T(8,128)(2,1)}, bf16[1,2,256,768]{3,2,1,0:T(8,128)(2,1)}, u32[]{:S(2)}, u32[]{:S(2)}) collective-permute-start(bf16[1,2,256,768]{3,2,1,0:T(8,128)(2,1)} %copy-done.6), channel_id=1, source_target_pairs={{0,16},{4,20},{8,24},{12,28},{16,0},{20,4},{24,8},{28,12},{1,17},{... | collective-permute-start | bytes 2359304 | tf_op jit(solution)/shard_map/ppermute | solution.py:499
  210.7 233.7 %collective-permute-start.4 = (bf16[1,2,256,768]{3,2,1,0:T(8,128)(2,1)}, bf16[1,2,256,768]{3,2,1,0:T(8,128)(2,1)}, u32[]{:S(2)}, u32[]{:S(2)}) collective-permute-start(bf16[1,2,256,768]{3,2,1,0:T(8,128)(2,1)} %copy-done.5), channel_id=1, source_target_pairs={{0,20},{4,24},{8,28},{12,0},{16,4},{20,8},{24,12},{28,16},{1,21},{... | collective-permute-start | bytes 2359304 | tf_op jit(solution)/shard_map/ppermute | solution.py:499
  222.7 3.7 copy-start.42
  222.8 48.2 %copy-start.58 = (f32[4,128]{1,0:T(4,128)}, f32[4,128]{1,0:T(4,128)S(1)}, u32[]{:S(2)}) copy-start(f32[4,128]{1,0:T(4,128)S(1)} %copy.296) | copy-start | bytes 6148
  222.9 48.1 %copy-start.60 = (f32[4,128]{1,0:T(4,128)}, f32[4,128]{1,0:T(4,128)S(1)}, u32[]{:S(2)}) copy-start(f32[4,128]{1,0:T(4,128)S(1)} %copy.299) | copy-start | bytes 6148
  260.6 10.1 copy-start.50
  260.6 10.1 copy-start.51
  260.6 10.1 copy-start.62
  271.0 4.3 copy-start.46
  283.9 6.8 copy-start.48
  283.9 6.8 copy-start.73
  297.3 20.4 %copy-start.69 = (s32[4]{0:T(128)S(1)}, s32[4]{0:T(128)}, u32[]{:S(2)}) copy-start(s32[4]{0:T(128)} %iota_add_fusion) | copy-start | bytes 52
  297.3 20.4 %copy-start.72 = (s32[128]{0:T(128)S(1)}, s32[128]{0:T(128)}, u32[]{:S(2)}) copy-start(s32[128]{0:T(128)} %iota_and_fusion) | copy-start | bytes 1540
  300.8 22.3 %copy-start.13 = (bf16[64,2,2048]{2,1,0:T(2,128)(2,1)S(1)}, bf16[64,2,2048]{2,1,0:T(2,128)(2,1)}, u32[]{:S(2)}) copy-start(bf16[64,2,2048]{2,1,0:T(2,128)(2,1)} %param.12) | copy-start | bytes 1572868
  300.8 26.2 %copy-start.27 = (bf16[2048,32]{1,0:T(8,128)(2,1)S(1)}, bf16[2048,32]{1,0:T(8,128)(2,1)}, u32[]{:S(2)}) copy-start(bf16[2048,32]{1,0:T(8,128)(2,1)} %reshape.380) | copy-start | bytes 393220
  319.0 125.5 %collective-permute-start.5 = (bf16[1,2,256,768]{3,2,1,0:T(8,128)(2,1)}, bf16[1,2,256,768]{3,2,1,0:T(8,128)(2,1)}, u32[]{:S(2)}, u32[]{:S(2)}) collective-permute-start(bf16[1,2,256,768]{3,2,1,0:T(8,128)(2,1)} %get-tuple-element.145), channel_id=1, source_target_pairs={{0,24},{4,28},{8,0},{12,4},{16,8},{20,12},{24,16},{28,20},{1,25},{... | collective-permute-start | bytes 2359304 | tf_op jit(solution)/shard_map/ppermute | solution.py:499
  321.1 126.5 %collective-permute-start.6 = (bf16[1,2,256,768]{3,2,1,0:T(8,128)(2,1)}, bf16[1,2,256,768]{3,2,1,0:T(8,128)(2,1)}, u32[]{:S(2)}, u32[]{:S(2)}) collective-permute-start(bf16[1,2,256,768]{3,2,1,0:T(8,128)(2,1)} %get-tuple-element.146), channel_id=1, source_target_pairs={{0,28},{4,0},{8,4},{12,8},{16,12},{20,16},{24,20},{28,24},{1,29},{... | collective-permute-start | bytes 2359304 | tf_op jit(solution)/shard_map/ppermute | solution.py:499
  321.6 126.8 %collective-permute-start.7 = (bf16[1,2,256,768]{3,2,1,0:T(8,128)(2,1)}, bf16[1,2,256,768]{3,2,1,0:T(8,128)(2,1)}, u32[]{:S(2)}, u32[]{:S(2)}) collective-permute-start(bf16[1,2,256,768]{3,2,1,0:T(8,128)(2,1)} %get-tuple-element.148), channel_id=1, source_target_pairs={{0,4},{4,8},{8,12},{12,16},{16,20},{20,24},{24,28},{28,0},{1,5},{5... | collective-permute-start | bytes 2359304 | tf_op jit(solution)/shard_map/ppermute | solution.py:499
  324.6 126.1 %collective-permute-start.8 = (bf16[1,2,256,768]{3,2,1,0:T(8,128)(2,1)}, bf16[1,2,256,768]{3,2,1,0:T(8,128)(2,1)}, u32[]{:S(2)}, u32[]{:S(2)}) collective-permute-start(bf16[1,2,256,768]{3,2,1,0:T(8,128)(2,1)} %get-tuple-element.149), channel_id=1, source_target_pairs={{0,8},{4,12},{8,16},{12,20},{16,24},{20,28},{24,0},{28,4},{1,9},{5... | collective-permute-start | bytes 2359304 | tf_op jit(solution)/shard_map/ppermute | solution.py:499
  444.5 101.3 %collective-permute-start.9 = (bf16[1,2,256,768]{3,2,1,0:T(8,128)(2,1)}, bf16[1,2,256,768]{3,2,1,0:T(8,128)(2,1)}, u32[]{:S(2)}, u32[]{:S(2)}) collective-permute-start(bf16[1,2,256,768]{3,2,1,0:T(8,128)(2,1)} %copy-done.3), channel_id=1, source_target_pairs={{0,12},{4,16},{8,20},{12,24},{16,28},{20,0},{24,4},{28,8},{1,13},{... | collective-permute-start | bytes 2359304 | tf_op jit(solution)/shard_map/ppermute | solution.py:499
  444.5 101.3 %collective-permute-start.10 = (bf16[1,2,256,768]{3,2,1,0:T(8,128)(2,1)S(1)}, bf16[1,2,256,768]{3,2,1,0:T(8,128)(2,1)}, u32[]{:S(2)}, u32[]{:S(2)}) collective-permute-start(bf16[1,2,256,768]{3,2,1,0:T(8,128)(2,1)S(1)} %get-tuple-element.170), channel_id=1, source_target_pairs={{0,16},{4,20},{8,24},{12,28},{16,0},{20,4},{24,8},{28,12},{1,17},{... | collective-permute-start | bytes 2359304 | tf_op jit(solution)/shard_map/ppermute | solution.py:499
  447.6 98.3 %collective-permute-start.11 = (bf16[1,2,256,768]{3,2,1,0:T(8,128)(2,1)S(1)}, bf16[1,2,256,768]{3,2,1,0:T(8,128)(2,1)}, u32[]{:S(2)}, u32[]{:S(2)}) collective-permute-start(bf16[1,2,256,768]{3,2,1,0:T(8,128)(2,1)S(1)} %get-tuple-element.171), channel_id=1, source_target_pairs={{0,20},{4,24},{8,28},{12,0},{16,4},{20,8},{24,12},{28,16},{1,21},{... | collective-permute-start | bytes 2359304 | tf_op jit(solution)/shard_map/ppermute | solution.py:499
  448.4 97.4 %collective-permute-start.12 = (bf16[1,2,256,768]{3,2,1,0:T(8,128)(2,1)S(1)}, bf16[1,2,256,768]{3,2,1,0:T(8,128)(2,1)}, u32[]{:S(2)}, u32[]{:S(2)}) collective-permute-start(bf16[1,2,256,768]{3,2,1,0:T(8,128)(2,1)S(1)} %get-tuple-element.172), channel_id=1, source_target_pairs={{0,24},{4,28},{8,0},{12,4},{16,8},{20,12},{24,16},{28,20},{1,25},{... | collective-permute-start | bytes 2359304 | tf_op jit(solution)/shard_map/ppermute | solution.py:499
  450.7 95.2 %collective-permute-start.13 = (bf16[1,2,256,768]{3,2,1,0:T(8,128)(2,1)S(1)}, bf16[1,2,256,768]{3,2,1,0:T(8,128)(2,1)}, u32[]{:S(2)}, u32[]{:S(2)}) collective-permute-start(bf16[1,2,256,768]{3,2,1,0:T(8,128)(2,1)S(1)} %get-tuple-element.173), channel_id=1, source_target_pairs={{0,28},{4,0},{8,4},{12,8},{16,12},{20,16},{24,20},{28,24},{1,29},{... | collective-permute-start | bytes 2359304 | tf_op jit(solution)/shard_map/ppermute | solution.py:499
  520.1 12.0 %copy-start.76 = (bf16[2,8,176,256]{3,2,1,0:T(8,128)(2,1)S(1)}, bf16[2,8,176,256]{3,2,1,0:T(8,128)(2,1)}, u32[]{:S(2)}) copy-start(bf16[2,8,176,256]{3,2,1,0:T(8,128)(2,1)} %get-tuple-element.164) | copy-start | bytes 4325380
  548.0 121.5 %collective-permute-start.17 = (bf16[1,2,256,768]{3,2,1,0:T(8,128)(2,1)}, bf16[1,2,256,768]{3,2,1,0:T(8,128)(2,1)S(1)}, u32[]{:S(2)}, u32[]{:S(2)}) collective-permute-start(bf16[1,2,256,768]{3,2,1,0:T(8,128)(2,1)} %get-tuple-element.299), channel_id=1, source_target_pairs={{0,16},{4,20},{8,24},{12,28},{16,0},{20,4},{24,8},{28,12},{1,17},{... | collective-permute-start | bytes 2359304 | tf_op jit(solution)/shard_map/ppermute | solution.py:499
  568.4 103.2 %collective-permute-start.16 = (bf16[1,2,256,768]{3,2,1,0:T(8,128)(2,1)S(1)}, bf16[1,2,256,768]{3,2,1,0:T(8,128)(2,1)S(1)}, u32[]{:S(2)}, u32[]{:S(2)}) collective-permute-start(bf16[1,2,256,768]{3,2,1,0:T(8,128)(2,1)S(1)} %get-tuple-element.300), channel_id=1, source_target_pairs={{0,12},{4,16},{8,20},{12,24},{16,28},{20,0},{24,4},{28,8},{1,13},{... | collective-permute-start | bytes 2359304 | tf_op jit(solution)/shard_map/ppermute | solution.py:499
  570.4 103.8 %collective-permute-start.15 = (bf16[1,2,256,768]{3,2,1,0:T(8,128)(2,1)}, bf16[1,2,256,768]{3,2,1,0:T(8,128)(2,1)}, u32[]{:S(2)}, u32[]{:S(2)}) collective-permute-start(bf16[1,2,256,768]{3,2,1,0:T(8,128)(2,1)} %get-tuple-element.301), channel_id=1, source_target_pairs={{0,8},{4,12},{8,16},{12,20},{16,24},{20,28},{24,0},{28,4},{1,9},{5... | collective-permute-start | bytes 2359304 | tf_op jit(solution)/shard_map/ppermute | solution.py:499
  570.4 105.8 %collective-permute-start.14 = (bf16[1,2,256,768]{3,2,1,0:T(8,128)(2,1)}, bf16[1,2,256,768]{3,2,1,0:T(8,128)(2,1)}, u32[]{:S(2)}, u32[]{:S(2)}) collective-permute-start(bf16[1,2,256,768]{3,2,1,0:T(8,128)(2,1)} %get-tuple-element.302), channel_id=1, source_target_pairs={{0,4},{4,8},{8,12},{12,16},{16,20},{20,24},{24,28},{28,0},{1,5},{5... | collective-permute-start | bytes 2359304 | tf_op jit(solution)/shard_map/ppermute | solution.py:499
  639.4 12.3 %copy-start.75 = (bf16[2,8,176,256]{3,2,1,0:T(8,128)(2,1)S(1)}, bf16[2,8,176,256]{3,2,1,0:T(8,128)(2,1)}, u32[]{:S(2)}) copy-start(bf16[2,8,176,256]{3,2,1,0:T(8,128)(2,1)} %get-tuple-element.187) | copy-start | bytes 4325380
  665.3 156.0 %collective-permute-start.20 = (bf16[1,2,256,768]{3,2,1,0:T(8,128)(2,1)}, bf16[1,2,256,768]{3,2,1,0:T(8,128)(2,1)}, u32[]{:S(2)}, u32[]{:S(2)}) collective-permute-start(bf16[1,2,256,768]{3,2,1,0:T(8,128)(2,1)} %get-tuple-element.296), channel_id=1, source_target_pairs={{0,28},{4,0},{8,4},{12,8},{16,12},{20,16},{24,20},{28,24},{1,29},{... | collective-permute-start | bytes 2359304 | tf_op jit(solution)/shard_map/ppermute | solution.py:499
  669.5 151.9 %collective-permute-start.19 = (bf16[1,2,256,768]{3,2,1,0:T(8,128)(2,1)}, bf16[1,2,256,768]{3,2,1,0:T(8,128)(2,1)}, u32[]{:S(2)}, u32[]{:S(2)}) collective-permute-start(bf16[1,2,256,768]{3,2,1,0:T(8,128)(2,1)} %get-tuple-element.297), channel_id=1, source_target_pairs={{0,24},{4,28},{8,0},{12,4},{16,8},{20,12},{24,16},{28,20},{1,25},{... | collective-permute-start | bytes 2359304 | tf_op jit(solution)/shard_map/ppermute | solution.py:499
  671.5 6.1 copy-start.45
  671.5 6.1 copy-start.43
  671.5 6.2 copy-start.53
  671.5 6.3 copy-start.55
  671.6 6.4 copy-start.68
  671.6 6.5 copy-start.67
  671.6 139.8 %collective-permute-start.18 = (bf16[1,2,256,768]{3,2,1,0:T(8,128)(2,1)}, bf16[1,2,256,768]{3,2,1,0:T(8,128)(2,1)}, u32[]{:S(2)}, u32[]{:S(2)}) collective-permute-start(bf16[1,2,256,768]{3,2,1,0:T(8,128)(2,1)} %get-tuple-element.298), channel_id=1, source_target_pairs={{0,20},{4,24},{8,28},{12,0},{16,4},{20,8},{24,12},{28,16},{1,21},{... | collective-permute-start | bytes 2359304 | tf_op jit(solution)/shard_map/ppermute | solution.py:499
  674.2 147.3 %collective-permute-start.21 = (bf16[1,2,256,768]{3,2,1,0:T(8,128)(2,1)}, bf16[1,2,256,768]{3,2,1,0:T(8,128)(2,1)}, u32[]{:S(2)}, u32[]{:S(2)}) collective-permute-start(bf16[1,2,256,768]{3,2,1,0:T(8,128)(2,1)} %get-tuple-element.294), channel_id=1, source_target_pairs={{0,4},{4,8},{8,12},{12,16},{16,20},{20,24},{24,28},{28,0},{1,5},{5... | collective-permute-start | bytes 2359304 | tf_op jit(solution)/shard_map/ppermute | solution.py:499
  676.2 148.2 %collective-permute-start.22 = (bf16[1,2,256,768]{3,2,1,0:T(8,128)(2,1)}, bf16[1,2,256,768]{3,2,1,0:T(8,128)(2,1)}, u32[]{:S(2)}, u32[]{:S(2)}) collective-permute-start(bf16[1,2,256,768]{3,2,1,0:T(8,128)(2,1)} %get-tuple-element.293), channel_id=1, source_target_pairs={{0,8},{4,12},{8,16},{12,20},{16,24},{20,28},{24,0},{28,4},{1,9},{5... | collective-permute-start | bytes 2359304 | tf_op jit(solution)/shard_map/ppermute | solution.py:499
  678.1 147.2 %copy-start.26 = (bf16[2,64,2048]{2,1,0:T(8,128)(2,1)S(1)}, bf16[2,64,2048]{2,1,0:T(8,128)(2,1)}, u32[]{:S(2)}) copy-start(bf16[2,64,2048]{2,1,0:T(8,128)(2,1)} %copy-done.25) | copy-start | bytes 1572868
  678.1 148.3 %copy-start.28 = (bf16[2048,32]{1,0:T(8,128)(2,1)S(1)}, bf16[2048,32]{1,0:T(8,128)(2,1)}, u32[]{:S(2)}) copy-start(bf16[2048,32]{1,0:T(8,128)(2,1)} %reshape.380) | copy-start | bytes 393220
  811.3 16.5 %copy-start.14 = (bf16[64,2,2048]{2,1,0:T(2,128)(2,1)S(1)}, bf16[64,2,2048]{2,1,0:T(2,128)(2,1)}, u32[]{:S(2)}) copy-start(bf16[64,2,2048]{2,1,0:T(2,128)(2,1)} %param.12) | copy-start | bytes 1572868
  811.3 16.5 %copy-start.17 = (bf16[128,2048]{1,0:T(8,128)(2,1)S(1)}, bf16[128,2048]{1,0:T(8,128)(2,1)}, u32[]{:S(2)}) copy-start(bf16[128,2048]{1,0:T(8,128)(2,1)} %shard_map.197) | copy-start | bytes 1572868
  811.3 16.5 %copy-start.47 = (bf16[64,2,2048]{2,1,0:T(2,128)(2,1)S(1)}, bf16[64,2,2048]{2,1,0:T(2,128)(2,1)}, u32[]{:S(2)}) copy-start(bf16[64,2,2048]{2,1,0:T(2,128)(2,1)} %param.13) | copy-start | bytes 1572868
  811.4 325.0 %collective-permute-start.27 = (bf16[1,2,256,768]{3,2,1,0:T(8,128)(2,1)}, bf16[1,2,256,768]{3,2,1,0:T(8,128)(2,1)}, u32[]{:S(2)}, u32[]{:S(2)}) collective-permute-start(bf16[1,2,256,768]{3,2,1,0:T(8,128)(2,1)} %get-tuple-element.287), channel_id=1, source_target_pairs={{0,28},{4,0},{8,4},{12,8},{16,12},{20,16},{24,20},{28,24},{1,29},{... | collective-permute-start | bytes 2359304 | tf_op jit(solution)/shard_map/ppermute | solution.py:499
  821.4 122.4 %collective-permute-start.26 = (bf16[1,2,256,768]{3,2,1,0:T(8,128)(2,1)}, bf16[1,2,256,768]{3,2,1,0:T(8,128)(2,1)}, u32[]{:S(2)}, u32[]{:S(2)}) collective-permute-start(bf16[1,2,256,768]{3,2,1,0:T(8,128)(2,1)} %get-tuple-element.289), channel_id=1, source_target_pairs={{0,24},{4,28},{8,0},{12,4},{16,8},{20,12},{24,16},{28,20},{1,25},{... | collective-permute-start | bytes 2359304 | tf_op jit(solution)/shard_map/ppermute | solution.py:499
  821.4 122.4 %collective-permute-start.25 = (bf16[1,2,256,768]{3,2,1,0:T(8,128)(2,1)}, bf16[1,2,256,768]{3,2,1,0:T(8,128)(2,1)}, u32[]{:S(2)}, u32[]{:S(2)}) collective-permute-start(bf16[1,2,256,768]{3,2,1,0:T(8,128)(2,1)} %get-tuple-element.290), channel_id=1, source_target_pairs={{0,20},{4,24},{8,28},{12,0},{16,4},{20,8},{24,12},{28,16},{1,21},{... | collective-permute-start | bytes 2359304 | tf_op jit(solution)/shard_map/ppermute | solution.py:499
  821.5 122.3 %collective-permute-start.24 = (bf16[1,2,256,768]{3,2,1,0:T(8,128)(2,1)}, bf16[1,2,256,768]{3,2,1,0:T(8,128)(2,1)}, u32[]{:S(2)}, u32[]{:S(2)}) collective-permute-start(bf16[1,2,256,768]{3,2,1,0:T(8,128)(2,1)} %get-tuple-element.291), channel_id=1, source_target_pairs={{0,16},{4,20},{8,24},{12,28},{16,0},{20,4},{24,8},{28,12},{1,17},{... | collective-permute-start | bytes 2359304 | tf_op jit(solution)/shard_map/ppermute | solution.py:499
  824.4 119.3 %collective-permute-start.23 = (bf16[1,2,256,768]{3,2,1,0:T(8,128)(2,1)}, bf16[1,2,256,768]{3,2,1,0:T(8,128)(2,1)}, u32[]{:S(2)}, u32[]{:S(2)}) collective-permute-start(bf16[1,2,256,768]{3,2,1,0:T(8,128)(2,1)} %get-tuple-element.292), channel_id=1, source_target_pairs={{0,12},{4,16},{8,20},{12,24},{16,28},{20,0},{24,4},{28,8},{1,13},{... | collective-permute-start | bytes 2359304 | tf_op jit(solution)/shard_map/ppermute | solution.py:499
  852.2 4.9 copy-start.57
  909.4 16.9 %copy-start.15 = (bf16[64,2,2048]{2,1,0:T(2,128)(2,1)S(1)}, bf16[64,2,2048]{2,1,0:T(2,128)(2,1)}, u32[]{:S(2)}) copy-start(bf16[64,2,2048]{2,1,0:T(2,128)(2,1)} %param.12) | copy-start | bytes 1572868
  909.4 16.9 %copy-start.18 = (bf16[128,2048]{1,0:T(8,128)(2,1)S(1)}, bf16[128,2048]{1,0:T(8,128)(2,1)}, u32[]{:S(2)}) copy-start(bf16[128,2048]{1,0:T(8,128)(2,1)} %shard_map.197) | copy-start | bytes 1572868
  909.4 16.9 %copy-start.30 = (f32[128,2048]{1,0:T(8,128)S(1)}, f32[128,2048]{1,0:T(8,128)}, u32[]{:S(2)}) copy-start(f32[128,2048]{1,0:T(8,128)} %copy-done.29) | copy-start | bytes 3145732
  928.0 5.5 copy-start.34
  928.0 5.5 copy-start.36
  938.4 4.4 copy-start.38
  1105.6 4.4 copy-start.22
  1119.1 17.2 %copy-start.1 = (s32[8]{0:T(128)S(1)}, s32[8]{0:T(128)}, u32[]{:S(2)}) copy-start(s32[8]{0:T(128)} %stack.62.origin_ref) | copy-start | bytes 100
  (42 other events, 86.0 us)

commit v5 on v4

--- a/solution.py
+++ b/solution.py
@@ -203,11 +203,12 @@
         for n, steps in enumerate(chain_steps(ranks, outer)):
             for bits in all_bits(dims):
                 level = level_of(bits)
-                turn = len(dims) + 1 if level == len(dims) else max(level - 1, 0)
-                events.append((turn, abs(steps), n, level, p, steps, bits))
-    for event in sorted(event for event in events if event[1] == 0 and event[3] == 0):
+                turn = 4 if level == len(dims) else max(level - 1, 0)
+                key = abs(steps) + level if turn < 4 else 0
+                events.append((turn, key, n, level, p, steps, bits))
+    for event in sorted(event for event in events if event[5] == 0 and event[3] == 0):
         forward(*event[4:])
-    for event in sorted(event for event in events if event[1] or event[3]):
+    for event in sorted(event for event in events if event[5] or event[3]):
         receive(*event[4:])
     for conditions, description in started:
         run_if(conditions, lambda: copy(*description).wait_send())

time: 1160 us -> 1150 us (level)
  no operation moved by 1% of the time
where the time goes in v5:
time: 1150 us
  Pallas kernels  789 us (69%)
  local copies, waits for them, and re-layouts  124 us (11%)
  matrix products  104 us (9%)
  starting transfers between devices  70.4 us (6%)
  other arithmetic  34.9 us (3%)
  blocking collectives  23 us (2%)
    pallas_call x4, Pallas kernels, scatter_blocks(): pl.pallas_call(functools.partial(scatter_kernel, ranks, arrays, pieces),...  329 us
    pallas_call x3, Pallas kernels, gather_blocks(): pl.pallas_call(functools.partial(gather_kernel, ranks, arrays, pieces), o...  301 us
    pallas_call x2, Pallas kernels, expert_math(): pl.pallas_call(functools.partial(expert_kernel, ranks, owned, width, 1 if...  135 us
    dot_general x26, matrix products, dot(): return jnp.einsum(spec, left, right, preferred_element_type=F32)  104 us
    ppermute x28, starting transfers between devices, send_blocks(): received.append((origin, lax.ppermute(blocks[shift], 'dp', pairs)))  70.4 us
    unnamed x169, local copies, waits for them, and re-layouts  29.8 us
  transfers between devices with their start and end apart: 28, of which 0 were waited for; matrix products, arithmetic and copies ran while one was open for 21% of the time, Pallas kernels for 52%

profile of v5, /device:TPU:0, one launch (start us, length us, event | category | flops | bytes accessed | tf_op | source)
XLA Modules:
  0.0 1147.7 jit_solution(4491657490845378652)
XLA Ops:
  11.3 2.2 copy-done
  13.5 12.3 %shard_map.195 = (bf16[1,2,256,768]{3,2,1,0:T(8,128)(2,1)S(1)}, bf16[1,2,256,768]{3,2,1,0:T(8,128)(2,1)S(1)}, bf16[1,2,256,768]{3,2,1,0:T(8,128)(2,1)S(1)}, bf16...) custom-call(s32[8]{0:T(128)S(1)} %compare_select_fusion.target_ref, ...), custom_call_target="tpu_custom_call" | custom-call | tf_op jit(solution)/shard_map/pallas_call | solution.py:548
  33.0 172.3 %shard_map.196 = (bf16[2048,512]{1,0:T(8,128)(2,1)}, bf16[2048,512]{1,0:T(8,128)(2,1)}, bf16[2048,512]{1,0:T(8,128)(2,1)}, bf16[2048,128]{1,0:T(8,128)(2,1)}, bf...) custom-call(bf16[256,512]{1,0:T(8,128)(2,1)} %get-tuple-element.308.refs_0_, ...), custom_call_target="tpu_custom_call" | custom-call | bytes 27787264 | tf_op jit(solution)/shard_map/pallas_call | solution.py:222
  206.8 3.0 collective-permute-start.2
  210.7 3.5 collective-permute-start.4
  224.0 3.6 convolution_convert_fusion.7
  230.4 3.5 fusion.102
  236.1 3.5 fusion.104
  241.7 2.5 reshape.373
  244.2 2.6 copy.295
  246.8 2.5 reshape.375
  249.3 2.5 copy.298
  251.9 4.5 reshape.417
  256.4 2.7 copy.308
  261.7 3.3 select_convert_fusion
  265.0 6.2 all-reduce.3
  272.1 2.2 fusion.88
  276.3 3.5 fusion.55
  285.0 6.8 slice_bitcast_fusion.4
  291.8 2.6 convolution_convert_fusion.4.refs_0_
  295.6 2.8 copy.311.refs_0_
  298.4 2.8 copy.316.refs_0_
  301.9 16.9 %shard_map.197 = bf16[128,2048]{1,0:T(8,128)(2,1)} custom-call(bf16[512,2048]{1,0:T(8,128)(2,1)} %convolution_convert_fusion.4.refs_0_), custom_call_target="tpu_custom_call" | custom-call | flops 1048576 | bytes 2097152 | tf_op jit(solution)/shard_map/pallas_call | solution.py:440
  330.4 110.0 %shard_map.198.rows_ref = bf16[4096,2176]{1,0:T(8,128)(2,1)} custom-call(bf16[128,2176]{1,0:T(8,128)(2,1)} %concatenate.28.refs_0_), custom_call_target="tpu_custom_call" | custom-call | bytes 17825792 | tf_op jit(solution)/shard_map/pallas_call | solution.py:222
  441.5 4.3 collective-permute-start.10
  450.1 66.1 %shard_map.199 = (bf16[4096,2048]{1,0:T(8,128)(2,1)}, bf16[4096,2176]{1,0:T(8,128)(2,1)}, bf16[2,8,176,2048]{3,2,1,0:T(8,128)(2,1)}, bf16[2,8,176,2048]{3,2,1,0:...) custom-call(s32[8]{0:T(128)} %stack.62.origin_ref, ...), custom_call_target="tpu_custom_call" | custom-call | flops 41339060224 | bytes 90177536 | tf_op jit(solution)/shard_map/pallas_call | solution.py:754
  516.3 12.0 %fusion.18 = bf16[8,2,256,512]{3,2,1,0:T(8,128)(2,1)} fusion(bf16[2,8,22,8,8,256]{5,4,3,2,1,0:T(8,128)(2,1)} %bitcast.300, bf16[2,8,176,512]{3,2,1,0:T(8,128)(2,1)} %get-tuple-element.162), kind=kOutput, calls=%fused_computation.24 | convolution fusion | flops 5907677184 | bytes 18612224 | tf_op jit(solution)/shard_map/egsrk,egsf->rekf/dot_general | solution.py:38
  528.3 10.4 fusion.45
  538.7 3.3 pad_maximum_fusion
  542.0 2.2 constant_dynamic-slice_fusion.2
  544.2 22.1 %collective-permute-start.17 = (bf16[1,2,256,768]{3,2,1,0:T(8,128)(2,1)}, bf16[1,2,256,768]{3,2,1,0:T(8,128)(2,1)S(1)}, u32[]{:S(2)}, u32[]{:S(2)}) collective-permute-start(bf16[1,2,256,768]{3,2,1,0:T(8,128)(2,1)} %get-tuple-element.299), channel_id=1, source_target_pairs={{0,16},{4,20},{8,24},{12,28},{16,0},{20,4},{24,8},{28,12},{1,17},{... | collective-permute-start | bytes 2359304 | tf_op jit(solution)/shard_map/ppermute | solution.py:500
  566.3 2.6 collective-permute-start.16
  569.5 68.4 %shard_map.200 = (bf16[4096,2048]{1,0:T(8,128)(2,1)}, bf16[4096,2176]{1,0:T(8,128)(2,1)}, bf16[2,8,176,2048]{3,2,1,0:T(8,128)(2,1)}, bf16[2,8,176,2048]{3,2,1,0:...) custom-call(s32[8]{0:T(128)} %stack.62.origin_ref, ...), custom_call_target="tpu_custom_call", output_to_operand_aliasing={{0}: (14, {}), {1}: (15, {})} | custom-call | flops 41339060224 | bytes 90177536 | tf_op jit(solution)/shard_map/pallas_call | solution.py:754
  637.9 12.2 %fusion.19 = bf16[8,2,256,512]{3,2,1,0:T(8,128)(2,1)} fusion(bf16[2,8,22,8,8,256]{5,4,3,2,1,0:T(8,128)(2,1)} %bitcast.298, bf16[2,8,176,512]{3,2,1,0:T(8,128)(2,1)} %get-tuple-element.185), kind=kOutput, calls=%fused_computation.25 | convolution fusion | flops 5907677184 | bytes 18612224 | tf_op jit(solution)/shard_map/egsrk,egsf->rekf/dot_general | solution.py:38
  650.2 10.4 fusion.48
  660.6 3.3 pad_maximum_fusion.1
  663.9 4.2 collective-permute-start.20
  670.2 2.5 constant_dynamic-slice_fusion
  676.7 133.3 %shard_map.201 = bf16[128,2176]{1,0:T(8,128)(2,1)} custom-call(bf16[4096,2176]{1,0:T(8,128)(2,1)} %get-tuple-element.194.refs_0_), custom_call_target="tpu_custom_call" | custom-call | flops 8912896 | bytes 17825792 | tf_op jit(solution)/shard_map/pallas_call | solution.py:440
  810.0 9.6 collective-permute-start.27
  819.8 2.9 collective-permute-start.24
  826.2 2.3 fusion.114
  828.5 18.3 %shard_map.202 = bf16[512,2048]{1,0:T(8,128)(2,1)} custom-call(bf16[128,2048]{1,0:T(8,128)(2,1)} %bitcast.275), custom_call_target="tpu_custom_call" | custom-call | bytes 2097152 | tf_op jit(solution)/shard_map/pallas_call | solution.py:222
  846.8 3.5 convolution_convert_fusion.6
  855.1 3.4 fusion.56
  858.5 2.5 multiply_reduce_fusion
  865.9 2.5 copy.326
  868.4 2.6 reshape.389
  871.0 6.0 all-reduce.2
  879.3 3.3 fusion.117
  882.6 2.9 fusion.27
  894.3 2.5 copy.332
  896.9 2.7 reshape.391
  904.7 2.6 add_convert_fusion.refs_0_
  907.3 16.9 %shard_map.203 = bf16[128,2048]{1,0:T(8,128)(2,1)} custom-call(bf16[512,2048]{1,0:T(8,128)(2,1)} %add_convert_fusion.refs_0_), custom_call_target="tpu_custom_call" | custom-call | flops 1048576 | bytes 2097152 | tf_op jit(solution)/shard_map/pallas_call | solution.py:440
  925.9 4.7 fusion.26
  931.4 2.9 fusion.25
  936.3 4.4 fusion.24
  941.7 162.1 %shard_map.204 = (bf16[128,2048]{1,0:T(8,128)(2,1)}, bf16[256,2176]{1,0:T(8,128)(2,1)}) custom-call(bf16[4096,2048]{1,0:T(8,128)(2,1)} %get-tuple-element.183.refs_0_, bf16[2048,2176]{1,0:T(8,128)(2,1)} %constant_dynamic-update-slice_fusion.1.refs_1_), custom_call_target="tpu_custom_call" | custom-call | flops 12845056 | bytes 25690112 | tf_op jit(solution)/shard_map/pallas_call | solution.py:440
  1105.7 2.5 slice.133
  1114.3 3.0 copy.344
  1117.3 3.0 copy.348
  1121.1 10.8 psum.39
  1134.8 12.6 %shard_map.205 = (f32[32,1024,128]{2,1,0:T(8,128)}, f32[32,256,256]{2,1,0:T(8,128)}) custom-call(s32[8]{0:T(128)S(1)} %copy-done.1, bf16[1,2,256,768]{3,2,1,0:T(8,128)(2,1)S(1)} %get-tuple-element.295.refs_0_, bf16[1,2,256,768]{3,2,1,0:T(8,128)(2,1)} %collective-permute-done.14.refs_1_, bf16[1,2,256,768]{3,2,1,0:T(8,128)(2,1)} %collective-permute-done.15.refs_2_, ...), custom_call_target="tpu_custom_call" | custom-call | tf_op jit(solution)/shard_map/pallas_call | solution.py:607
  (319 shorter events, 119.6 us)
Async XLA Ops:
  0.6 9.8 copy-start.41
  205.2 114.9 %collective-permute-start = (bf16[1,2,256,768]{3,2,1,0:T(8,128)(2,1)}, bf16[1,2,256,768]{3,2,1,0:T(8,128)(2,1)}, u32[]{:S(2)}, u32[]{:S(2)}) collective-permute-start(bf16[1,2,256,768]{3,2,1,0:T(8,128)(2,1)} %copy-done.9), channel_id=1, source_target_pairs={{0,4},{4,8},{8,12},{12,16},{16,20},{20,24},{24,28},{28,0},{1,5},{5... | collective-permute-start | bytes 2359304 | tf_op jit(solution)/shard_map/ppermute | solution.py:500
  206.8 114.2 %collective-permute-start.1 = (bf16[1,2,256,768]{3,2,1,0:T(8,128)(2,1)}, bf16[1,2,256,768]{3,2,1,0:T(8,128)(2,1)}, u32[]{:S(2)}, u32[]{:S(2)}) collective-permute-start(bf16[1,2,256,768]{3,2,1,0:T(8,128)(2,1)} %copy-done.8), channel_id=1, source_target_pairs={{0,8},{4,12},{8,16},{12,20},{16,24},{20,28},{24,0},{28,4},{1,9},{5... | collective-permute-start | bytes 2359304 | tf_op jit(solution)/shard_map/ppermute | solution.py:500
  206.8 115.0 %collective-permute-start.2 = (bf16[1,2,256,768]{3,2,1,0:T(8,128)(2,1)}, bf16[1,2,256,768]{3,2,1,0:T(8,128)(2,1)}, u32[]{:S(2)}, u32[]{:S(2)}) collective-permute-start(bf16[1,2,256,768]{3,2,1,0:T(8,128)(2,1)} %copy-done.7), channel_id=1, source_target_pairs={{0,12},{4,16},{8,20},{12,24},{16,28},{20,0},{24,4},{28,8},{1,13},{... | collective-permute-start | bytes 2359304 | tf_op jit(solution)/shard_map/ppermute | solution.py:500
  209.8 114.7 %collective-permute-start.3 = (bf16[1,2,256,768]{3,2,1,0:T(8,128)(2,1)}, bf16[1,2,256,768]{3,2,1,0:T(8,128)(2,1)}, u32[]{:S(2)}, u32[]{:S(2)}) collective-permute-start(bf16[1,2,256,768]{3,2,1,0:T(8,128)(2,1)} %copy-done.6), channel_id=1, source_target_pairs={{0,16},{4,20},{8,24},{12,28},{16,0},{20,4},{24,8},{28,12},{1,17},{... | collective-permute-start | bytes 2359304 | tf_op jit(solution)/shard_map/ppermute | solution.py:500
  210.7 229.8 %collective-permute-start.4 = (bf16[1,2,256,768]{3,2,1,0:T(8,128)(2,1)}, bf16[1,2,256,768]{3,2,1,0:T(8,128)(2,1)}, u32[]{:S(2)}, u32[]{:S(2)}) collective-permute-start(bf16[1,2,256,768]{3,2,1,0:T(8,128)(2,1)} %copy-done.5), channel_id=1, source_target_pairs={{0,20},{4,24},{8,28},{12,0},{16,4},{20,8},{24,12},{28,16},{1,21},{... | collective-permute-start | bytes 2359304 | tf_op jit(solution)/shard_map/ppermute | solution.py:500
  223.8 3.7 copy-start.42
  223.9 48.1 %copy-start.58 = (f32[4,128]{1,0:T(4,128)}, f32[4,128]{1,0:T(4,128)S(1)}, u32[]{:S(2)}) copy-start(f32[4,128]{1,0:T(4,128)S(1)} %copy.296) | copy-start | bytes 6148
  224.0 48.1 %copy-start.60 = (f32[4,128]{1,0:T(4,128)}, f32[4,128]{1,0:T(4,128)S(1)}, u32[]{:S(2)}) copy-start(f32[4,128]{1,0:T(4,128)S(1)} %copy.299) | copy-start | bytes 6148
  261.7 10.1 copy-start.50
  261.7 10.1 copy-start.51
  261.7 10.1 copy-start.62
  272.0 4.3 copy-start.46
  285.0 6.8 copy-start.48
  285.0 6.8 copy-start.73
  298.4 20.4 %copy-start.69 = (s32[4]{0:T(128)S(1)}, s32[4]{0:T(128)}, u32[]{:S(2)}) copy-start(s32[4]{0:T(128)} %iota_add_fusion) | copy-start | bytes 52
  298.4 20.4 %copy-start.72 = (s32[128]{0:T(128)S(1)}, s32[128]{0:T(128)}, u32[]{:S(2)}) copy-start(s32[128]{0:T(128)} %iota_and_fusion) | copy-start | bytes 1540
  301.9 21.2 %copy-start.13 = (bf16[64,2,2048]{2,1,0:T(2,128)(2,1)S(1)}, bf16[64,2,2048]{2,1,0:T(2,128)(2,1)}, u32[]{:S(2)}) copy-start(bf16[64,2,2048]{2,1,0:T(2,128)(2,1)} %param.12) | copy-start | bytes 1572868
  301.9 25.9 %copy-start.27 = (bf16[2048,32]{1,0:T(8,128)(2,1)S(1)}, bf16[2048,32]{1,0:T(8,128)(2,1)}, u32[]{:S(2)}) copy-start(bf16[2048,32]{1,0:T(8,128)(2,1)} %reshape.380) | copy-start | bytes 393220
  320.1 121.4 %collective-permute-start.5 = (bf16[1,2,256,768]{3,2,1,0:T(8,128)(2,1)}, bf16[1,2,256,768]{3,2,1,0:T(8,128)(2,1)}, u32[]{:S(2)}, u32[]{:S(2)}) collective-permute-start(bf16[1,2,256,768]{3,2,1,0:T(8,128)(2,1)} %get-tuple-element.145), channel_id=1, source_target_pairs={{0,24},{4,28},{8,0},{12,4},{16,8},{20,12},{24,16},{28,20},{1,25},{... | collective-permute-start | bytes 2359304 | tf_op jit(solution)/shard_map/ppermute | solution.py:500
  321.0 124.8 %collective-permute-start.6 = (bf16[1,2,256,768]{3,2,1,0:T(8,128)(2,1)}, bf16[1,2,256,768]{3,2,1,0:T(8,128)(2,1)}, u32[]{:S(2)}, u32[]{:S(2)}) collective-permute-start(bf16[1,2,256,768]{3,2,1,0:T(8,128)(2,1)} %get-tuple-element.146), channel_id=1, source_target_pairs={{0,28},{4,0},{8,4},{12,8},{16,12},{20,16},{24,20},{28,24},{1,29},{... | collective-permute-start | bytes 2359304 | tf_op jit(solution)/shard_map/ppermute | solution.py:500
  321.8 124.9 %collective-permute-start.7 = (bf16[1,2,256,768]{3,2,1,0:T(8,128)(2,1)}, bf16[1,2,256,768]{3,2,1,0:T(8,128)(2,1)}, u32[]{:S(2)}, u32[]{:S(2)}) collective-permute-start(bf16[1,2,256,768]{3,2,1,0:T(8,128)(2,1)} %get-tuple-element.148), channel_id=1, source_target_pairs={{0,4},{4,8},{8,12},{12,16},{16,20},{20,24},{24,28},{28,0},{1,5},{5... | collective-permute-start | bytes 2359304 | tf_op jit(solution)/shard_map/ppermute | solution.py:500
  324.5 124.3 %collective-permute-start.8 = (bf16[1,2,256,768]{3,2,1,0:T(8,128)(2,1)}, bf16[1,2,256,768]{3,2,1,0:T(8,128)(2,1)}, u32[]{:S(2)}, u32[]{:S(2)}) collective-permute-start(bf16[1,2,256,768]{3,2,1,0:T(8,128)(2,1)} %get-tuple-element.149), channel_id=1, source_target_pairs={{0,8},{4,12},{8,16},{12,20},{16,24},{20,28},{24,0},{28,4},{1,9},{5... | collective-permute-start | bytes 2359304 | tf_op jit(solution)/shard_map/ppermute | solution.py:500
  440.5 101.5 %collective-permute-start.9 = (bf16[1,2,256,768]{3,2,1,0:T(8,128)(2,1)}, bf16[1,2,256,768]{3,2,1,0:T(8,128)(2,1)}, u32[]{:S(2)}, u32[]{:S(2)}) collective-permute-start(bf16[1,2,256,768]{3,2,1,0:T(8,128)(2,1)} %copy-done.3), channel_id=1, source_target_pairs={{0,12},{4,16},{8,20},{12,24},{16,28},{20,0},{24,4},{28,8},{1,13},{... | collective-permute-start | bytes 2359304 | tf_op jit(solution)/shard_map/ppermute | solution.py:500
  441.5 100.4 %collective-permute-start.10 = (bf16[1,2,256,768]{3,2,1,0:T(8,128)(2,1)S(1)}, bf16[1,2,256,768]{3,2,1,0:T(8,128)(2,1)}, u32[]{:S(2)}, u32[]{:S(2)}) collective-permute-start(bf16[1,2,256,768]{3,2,1,0:T(8,128)(2,1)S(1)} %get-tuple-element.170), channel_id=1, source_target_pairs={{0,16},{4,20},{8,24},{12,28},{16,0},{20,4},{24,8},{28,12},{1,17},{... | collective-permute-start | bytes 2359304 | tf_op jit(solution)/shard_map/ppermute | solution.py:500
  445.9 96.1 %collective-permute-start.11 = (bf16[1,2,256,768]{3,2,1,0:T(8,128)(2,1)S(1)}, bf16[1,2,256,768]{3,2,1,0:T(8,128)(2,1)}, u32[]{:S(2)}, u32[]{:S(2)}) collective-permute-start(bf16[1,2,256,768]{3,2,1,0:T(8,128)(2,1)S(1)} %get-tuple-element.171), channel_id=1, source_target_pairs={{0,20},{4,24},{8,28},{12,0},{16,4},{20,8},{24,12},{28,16},{1,21},{... | collective-permute-start | bytes 2359304 | tf_op jit(solution)/shard_map/ppermute | solution.py:500
  446.7 95.3 %collective-permute-start.12 = (bf16[1,2,256,768]{3,2,1,0:T(8,128)(2,1)S(1)}, bf16[1,2,256,768]{3,2,1,0:T(8,128)(2,1)}, u32[]{:S(2)}, u32[]{:S(2)}) collective-permute-start(bf16[1,2,256,768]{3,2,1,0:T(8,128)(2,1)S(1)} %get-tuple-element.172), channel_id=1, source_target_pairs={{0,24},{4,28},{8,0},{12,4},{16,8},{20,12},{24,16},{28,20},{1,25},{... | collective-permute-start | bytes 2359304 | tf_op jit(solution)/shard_map/ppermute | solution.py:500
  448.8 93.2 %collective-permute-start.13 = (bf16[1,2,256,768]{3,2,1,0:T(8,128)(2,1)S(1)}, bf16[1,2,256,768]{3,2,1,0:T(8,128)(2,1)}, u32[]{:S(2)}, u32[]{:S(2)}) collective-permute-start(bf16[1,2,256,768]{3,2,1,0:T(8,128)(2,1)S(1)} %get-tuple-element.173), channel_id=1, source_target_pairs={{0,28},{4,0},{8,4},{12,8},{16,12},{20,16},{24,20},{28,24},{1,29},{... | collective-permute-start | bytes 2359304 | tf_op jit(solution)/shard_map/ppermute | solution.py:500
  516.2 12.0 %copy-start.76 = (bf16[2,8,176,256]{3,2,1,0:T(8,128)(2,1)S(1)}, bf16[2,8,176,256]{3,2,1,0:T(8,128)(2,1)}, u32[]{:S(2)}) copy-start(bf16[2,8,176,256]{3,2,1,0:T(8,128)(2,1)} %get-tuple-element.164) | copy-start | bytes 4325380
  544.2 123.9 %collective-permute-start.17 = (bf16[1,2,256,768]{3,2,1,0:T(8,128)(2,1)}, bf16[1,2,256,768]{3,2,1,0:T(8,128)(2,1)S(1)}, u32[]{:S(2)}, u32[]{:S(2)}) collective-permute-start(bf16[1,2,256,768]{3,2,1,0:T(8,128)(2,1)} %get-tuple-element.299), channel_id=1, source_target_pairs={{0,16},{4,20},{8,24},{12,28},{16,0},{20,4},{24,8},{28,12},{1,17},{... | collective-permute-start | bytes 2359304 | tf_op jit(solution)/shard_map/ppermute | solution.py:500
  566.3 103.8 %collective-permute-start.16 = (bf16[1,2,256,768]{3,2,1,0:T(8,128)(2,1)S(1)}, bf16[1,2,256,768]{3,2,1,0:T(8,128)(2,1)S(1)}, u32[]{:S(2)}, u32[]{:S(2)}) collective-permute-start(bf16[1,2,256,768]{3,2,1,0:T(8,128)(2,1)S(1)} %get-tuple-element.300), channel_id=1, source_target_pairs={{0,12},{4,16},{8,20},{12,24},{16,28},{20,0},{24,4},{28,8},{1,13},{... | collective-permute-start | bytes 2359304 | tf_op jit(solution)/shard_map/ppermute | solution.py:500
  568.9 103.8 %collective-permute-start.15 = (bf16[1,2,256,768]{3,2,1,0:T(8,128)(2,1)}, bf16[1,2,256,768]{3,2,1,0:T(8,128)(2,1)}, u32[]{:S(2)}, u32[]{:S(2)}) collective-permute-start(bf16[1,2,256,768]{3,2,1,0:T(8,128)(2,1)} %get-tuple-element.301), channel_id=1, source_target_pairs={{0,8},{4,12},{8,16},{12,20},{16,24},{20,28},{24,0},{28,4},{1,9},{5... | collective-permute-start | bytes 2359304 | tf_op jit(solution)/shard_map/ppermute | solution.py:500
  568.9 105.2 %collective-permute-start.14 = (bf16[1,2,256,768]{3,2,1,0:T(8,128)(2,1)}, bf16[1,2,256,768]{3,2,1,0:T(8,128)(2,1)}, u32[]{:S(2)}, u32[]{:S(2)}) collective-permute-start(bf16[1,2,256,768]{3,2,1,0:T(8,128)(2,1)} %get-tuple-element.302), channel_id=1, source_target_pairs={{0,4},{4,8},{8,12},{12,16},{16,20},{20,24},{24,28},{28,0},{1,5},{5... | collective-permute-start | bytes 2359304 | tf_op jit(solution)/shard_map/ppermute | solution.py:500
  637.9 12.3 %copy-start.75 = (bf16[2,8,176,256]{3,2,1,0:T(8,128)(2,1)S(1)}, bf16[2,8,176,256]{3,2,1,0:T(8,128)(2,1)}, u32[]{:S(2)}) copy-start(bf16[2,8,176,256]{3,2,1,0:T(8,128)(2,1)} %get-tuple-element.187) | copy-start | bytes 4325380
  663.9 155.8 %collective-permute-start.20 = (bf16[1,2,256,768]{3,2,1,0:T(8,128)(2,1)}, bf16[1,2,256,768]{3,2,1,0:T(8,128)(2,1)}, u32[]{:S(2)}, u32[]{:S(2)}) collective-permute-start(bf16[1,2,256,768]{3,2,1,0:T(8,128)(2,1)} %get-tuple-element.296), channel_id=1, source_target_pairs={{0,28},{4,0},{8,4},{12,8},{16,12},{20,16},{24,20},{28,24},{1,29},{... | collective-permute-start | bytes 2359304 | tf_op jit(solution)/shard_map/ppermute | solution.py:500
  668.1 151.6 %collective-permute-start.19 = (bf16[1,2,256,768]{3,2,1,0:T(8,128)(2,1)}, bf16[1,2,256,768]{3,2,1,0:T(8,128)(2,1)}, u32[]{:S(2)}, u32[]{:S(2)}) collective-permute-start(bf16[1,2,256,768]{3,2,1,0:T(8,128)(2,1)} %get-tuple-element.297), channel_id=1, source_target_pairs={{0,24},{4,28},{8,0},{12,4},{16,8},{20,12},{24,16},{28,20},{1,25},{... | collective-permute-start | bytes 2359304 | tf_op jit(solution)/shard_map/ppermute | solution.py:500
  670.1 6.1 copy-start.45
  670.1 6.1 copy-start.43
  670.1 6.2 copy-start.53
  670.1 6.3 copy-start.55
  670.1 6.4 copy-start.68
  670.1 6.5 copy-start.67
  670.1 139.9 %collective-permute-start.18 = (bf16[1,2,256,768]{3,2,1,0:T(8,128)(2,1)}, bf16[1,2,256,768]{3,2,1,0:T(8,128)(2,1)}, u32[]{:S(2)}, u32[]{:S(2)}) collective-permute-start(bf16[1,2,256,768]{3,2,1,0:T(8,128)(2,1)} %get-tuple-element.298), channel_id=1, source_target_pairs={{0,20},{4,24},{8,28},{12,0},{16,4},{20,8},{24,12},{28,16},{1,21},{... | collective-permute-start | bytes 2359304 | tf_op jit(solution)/shard_map/ppermute | solution.py:500
  672.7 147.1 %collective-permute-start.21 = (bf16[1,2,256,768]{3,2,1,0:T(8,128)(2,1)}, bf16[1,2,256,768]{3,2,1,0:T(8,128)(2,1)}, u32[]{:S(2)}, u32[]{:S(2)}) collective-permute-start(bf16[1,2,256,768]{3,2,1,0:T(8,128)(2,1)} %get-tuple-element.294), channel_id=1, source_target_pairs={{0,4},{4,8},{8,12},{12,16},{16,20},{20,24},{24,28},{28,0},{1,5},{5... | collective-permute-start | bytes 2359304 | tf_op jit(solution)/shard_map/ppermute | solution.py:500
  674.2 148.5 %collective-permute-start.22 = (bf16[1,2,256,768]{3,2,1,0:T(8,128)(2,1)}, bf16[1,2,256,768]{3,2,1,0:T(8,128)(2,1)}, u32[]{:S(2)}, u32[]{:S(2)}) collective-permute-start(bf16[1,2,256,768]{3,2,1,0:T(8,128)(2,1)} %get-tuple-element.293), channel_id=1, source_target_pairs={{0,8},{4,12},{8,16},{12,20},{16,24},{20,28},{24,0},{28,4},{1,9},{5... | collective-permute-start | bytes 2359304 | tf_op jit(solution)/shard_map/ppermute | solution.py:500
  676.7 147.0 %copy-start.26 = (bf16[2,64,2048]{2,1,0:T(8,128)(2,1)S(1)}, bf16[2,64,2048]{2,1,0:T(8,128)(2,1)}, u32[]{:S(2)}) copy-start(bf16[2,64,2048]{2,1,0:T(8,128)(2,1)} %copy-done.25) | copy-start | bytes 1572868
  676.7 148.0 %copy-start.28 = (bf16[2048,32]{1,0:T(8,128)(2,1)S(1)}, bf16[2048,32]{1,0:T(8,128)(2,1)}, u32[]{:S(2)}) copy-start(bf16[2048,32]{1,0:T(8,128)(2,1)} %reshape.380) | copy-start | bytes 393220
  810.0 16.1 %copy-start.14 = (bf16[64,2,2048]{2,1,0:T(2,128)(2,1)S(1)}, bf16[64,2,2048]{2,1,0:T(2,128)(2,1)}, u32[]{:S(2)}) copy-start(bf16[64,2,2048]{2,1,0:T(2,128)(2,1)} %param.12) | copy-start | bytes 1572868
  810.0 16.1 %copy-start.17 = (bf16[128,2048]{1,0:T(8,128)(2,1)S(1)}, bf16[128,2048]{1,0:T(8,128)(2,1)}, u32[]{:S(2)}) copy-start(bf16[128,2048]{1,0:T(8,128)(2,1)} %shard_map.197) | copy-start | bytes 1572868
  810.0 16.1 %copy-start.47 = (bf16[64,2,2048]{2,1,0:T(2,128)(2,1)S(1)}, bf16[64,2,2048]{2,1,0:T(2,128)(2,1)}, u32[]{:S(2)}) copy-start(bf16[64,2,2048]{2,1,0:T(2,128)(2,1)} %param.13) | copy-start | bytes 1572868
  810.0 324.8 %collective-permute-start.27 = (bf16[1,2,256,768]{3,2,1,0:T(8,128)(2,1)}, bf16[1,2,256,768]{3,2,1,0:T(8,128)(2,1)}, u32[]{:S(2)}, u32[]{:S(2)}) collective-permute-start(bf16[1,2,256,768]{3,2,1,0:T(8,128)(2,1)} %get-tuple-element.287), channel_id=1, source_target_pairs={{0,28},{4,0},{8,4},{12,8},{16,12},{20,16},{24,20},{28,24},{1,29},{... | collective-permute-start | bytes 2359304 | tf_op jit(solution)/shard_map/ppermute | solution.py:500
  819.7 122.0 %collective-permute-start.26 = (bf16[1,2,256,768]{3,2,1,0:T(8,128)(2,1)}, bf16[1,2,256,768]{3,2,1,0:T(8,128)(2,1)}, u32[]{:S(2)}, u32[]{:S(2)}) collective-permute-start(bf16[1,2,256,768]{3,2,1,0:T(8,128)(2,1)} %get-tuple-element.289), channel_id=1, source_target_pairs={{0,24},{4,28},{8,0},{12,4},{16,8},{20,12},{24,16},{28,20},{1,25},{... | collective-permute-start | bytes 2359304 | tf_op jit(solution)/shard_map/ppermute | solution.py:500
  819.7 122.0 %collective-permute-start.25 = (bf16[1,2,256,768]{3,2,1,0:T(8,128)(2,1)}, bf16[1,2,256,768]{3,2,1,0:T(8,128)(2,1)}, u32[]{:S(2)}, u32[]{:S(2)}) collective-permute-start(bf16[1,2,256,768]{3,2,1,0:T(8,128)(2,1)} %get-tuple-element.290), channel_id=1, source_target_pairs={{0,20},{4,24},{8,28},{12,0},{16,4},{20,8},{24,12},{28,16},{1,21},{... | collective-permute-start | bytes 2359304 | tf_op jit(solution)/shard_map/ppermute | solution.py:500
  819.8 121.9 %collective-permute-start.24 = (bf16[1,2,256,768]{3,2,1,0:T(8,128)(2,1)}, bf16[1,2,256,768]{3,2,1,0:T(8,128)(2,1)}, u32[]{:S(2)}, u32[]{:S(2)}) collective-permute-start(bf16[1,2,256,768]{3,2,1,0:T(8,128)(2,1)} %get-tuple-element.291), channel_id=1, source_target_pairs={{0,16},{4,20},{8,24},{12,28},{16,0},{20,4},{24,8},{28,12},{1,17},{... | collective-permute-start | bytes 2359304 | tf_op jit(solution)/shard_map/ppermute | solution.py:500
  822.7 119.0 %collective-permute-start.23 = (bf16[1,2,256,768]{3,2,1,0:T(8,128)(2,1)}, bf16[1,2,256,768]{3,2,1,0:T(8,128)(2,1)}, u32[]{:S(2)}, u32[]{:S(2)}) collective-permute-start(bf16[1,2,256,768]{3,2,1,0:T(8,128)(2,1)} %get-tuple-element.292), channel_id=1, source_target_pairs={{0,12},{4,16},{8,20},{12,24},{16,28},{20,0},{24,4},{28,8},{1,13},{... | collective-permute-start | bytes 2359304 | tf_op jit(solution)/shard_map/ppermute | solution.py:500
  850.2 4.9 copy-start.57
  907.3 16.9 %copy-start.15 = (bf16[64,2,2048]{2,1,0:T(2,128)(2,1)S(1)}, bf16[64,2,2048]{2,1,0:T(2,128)(2,1)}, u32[]{:S(2)}) copy-start(bf16[64,2,2048]{2,1,0:T(2,128)(2,1)} %param.12) | copy-start | bytes 1572868
  907.3 16.9 %copy-start.18 = (bf16[128,2048]{1,0:T(8,128)(2,1)S(1)}, bf16[128,2048]{1,0:T(8,128)(2,1)}, u32[]{:S(2)}) copy-start(bf16[128,2048]{1,0:T(8,128)(2,1)} %shard_map.197) | copy-start | bytes 1572868
  907.3 17.0 %copy-start.30 = (f32[128,2048]{1,0:T(8,128)S(1)}, f32[128,2048]{1,0:T(8,128)}, u32[]{:S(2)}) copy-start(f32[128,2048]{1,0:T(8,128)} %copy-done.29) | copy-start | bytes 3145732
  925.9 5.5 copy-start.34
  925.9 5.5 copy-start.36
  936.3 4.4 copy-start.38
  1103.8 4.4 copy-start.22
  1117.3 17.5 %copy-start.1 = (s32[8]{0:T(128)S(1)}, s32[8]{0:T(128)}, u32[]{:S(2)}) copy-start(s32[8]{0:T(128)} %stack.62.origin_ref) | copy-start | bytes 100
  (42 other events, 86.0 us)
